TPU v7x, 32 devices: a whole 2x2x4 slice. The times are simulated.
32 devices in a mesh: tiles: 2 (over x), rows: 16 (over z, y, core).
Axes of the slice: x: 2, y: 2, z: 4, core: 2. Of those that a mesh axis runs over, the one named last changes fastest.
Arguments:
- reflect: bfloat16 [128, 6, 32, 2048], P('rows', None, None, 'tiles'), parts along dimension 3, may hold values from 0 to 6.5
- clear_conf: int32 [128, 32, 2048], P('rows', None, 'tiles'), parts along dimension 2, may hold values from 0 to 100
- sun_view: int32 [128, 3, 32, 2048], P('rows', None, None, 'tiles'), parts along dimension 3, may hold values from 0 to 18000, as said below
- sensor_id: int32 [128], replicated, may hold values from 0 to 3
- band_gain: float32 [4, 6], replicated, may hold values from 0.5 to 1.5
- sensor_weight: float32 [4], replicated, may hold values from 0.5 to 2
- prior: float32 [32, 18, 2048], P('rows', None, 'tiles'), parts along dimension 2, may hold values from -1.75 to 1.75
Outputs:
- brdf_weights: float32 [32, 18, 2048], P('rows', None, 'tiles'), parts along dimension 2
There are 2 independent parts, one for each index of `tiles`. A program takes and returns all parts, laid end to end along the dimension named above; an argument that names none is the same for every part. Nothing has to cross between parts.
Inputs may be any that keep to these rules, and one draw needn't show every extreme that they name: `sun_view`: component 0 is the solar zenith, 2000 to 7000; component 1 the view zenith, 0 to 1500; component 2 the relative azimuth, 0 to 18000.
All inputs are finite; a program needn't handle non-finite values.
Results may differ from a plain program's by a relative error of at most 0.0003.
Values may be sent and summed in bfloat16 or wider, within the bound.
No kernel may reach another device: no remote copies, remote signals or barrier semaphores. Data moves between devices by JAX's collectives and lax.ppermute only.
A program may use at most 128 MiB of HBM per device.

v0:
```python
import functools
import math

import jax
import jax.numpy as jnp
from jax import lax
from jax.experimental import pallas as pl
from jax.experimental.pallas import tpu as pltpu
from jax.sharding import PartitionSpec as P

TO_RADIAN = math.pi / 18000.0
PRIOR_PULL = 0.1
SMOOTH_PULL = 0.5
SHIFT = 3.0
GAIN = 0.4
ENTRIES = 24
LANES = 128
QUANT = 32000.0
GROUP = LANES // 4
CHUNKS = 2


R_POLY = (0.9428089773, 0.04714460664, 0.007527079489, 0.001965302741, 9.052799897e-05, 0.0004621408027)
S_POLY = (0.6002109608, -0.09003726006, -0.007977343822, -0.001801806492, 3.702625389e-06, -0.0003981650976)
SIN_25 = (0.9999999567, -0.1666626093, 0.008276695349)
COS_25 = (0.9999999997, -0.4999999562, 0.04166553086, -0.001379415437)
SIN_15 = (0.999999998, -0.1666661418, 0.008312938059)
COS_15 = (0.9999999858, -0.4999963087, 0.04152366947)
SIN_90 = (0.9999999947, -0.1666665666, 0.008333024663, -0.00019807389, 2.601844464e-06)


def horner(coefs, x):
    acc = coefs[-1] * x + coefs[-2]
    for coef in coefs[-3::-1]:
        acc = acc * x + coef
    return acc


def of_degrees(coefs, x, x2, factor, odd):
    scaled = [factor * coef * TO_RADIAN ** (2 * k + odd) for k, coef in enumerate(coefs)]
    value = horner(scaled, x2)
    return value * x if odd else value


def ross_li(sun, view, azim):
    x = (sun - 4500).astype(jnp.float32)
    x2 = x * x
    half = math.sqrt(0.5)
    sin_x, cos_x = of_degrees(SIN_25, x, x2, half, 1), of_degrees(COS_25, x, x2, half, 0)
    cos_sun, sin_sun = cos_x - sin_x, cos_x + sin_x
    v = view.astype(jnp.float32)
    v2 = v * v
    sin_view, cos_view = of_degrees(SIN_15, v, v2, 1.0, 1), of_degrees(COS_15, v, v2, 1.0, 0)
    a = (9000 - azim).astype(jnp.float32)
    cos_azim = of_degrees(SIN_90, a, a * a, 1.0, 1)
    prod = cos_sun * cos_view
    cos_phase = prod + sin_sun * sin_view * cos_azim
    total = cos_sun + cos_view
    recip = pl.reciprocal(total * prod, approx=False)
    inv_total = recip * prod
    sec_prod = recip * total
    u = 1.0 - cos_phase
    u_up = 1.0 + cos_phase
    bent = u * (u * lax.rsqrt(u)) * horner(R_POLY, u)
    volume = (bent + (0.5 * math.pi) * cos_phase) * inv_total - 0.25 * math.pi
    sin2 = u * u_up
    sin_phase = sin2 * lax.rsqrt(sin2)
    w = jnp.maximum(1.0 - (2.0 * inv_total) * sin_phase, 1e-30)
    overlap = w * (w * lax.rsqrt(w)) * horner(S_POLY, w)
    geometric = sec_prod * (total * (overlap - 1.0) + 0.5 * u_up)
    return volume, geometric


def lane_group(shape):
    return lax.broadcasted_iota(jnp.int32, shape, len(shape) - 1) // GROUP


def pack(tiles, msg_ref, block):
    rows = tiles[0].shape[0]
    top = jnp.abs(tiles[0])
    for tile in tiles[1:]:
        top = jnp.maximum(top, jnp.abs(tile))
    for shift in (LANES // 2, LANES // 4):
        top = jnp.maximum(top, pltpu.roll(top, shift, axis=1))
    level = jnp.ceil(8.0 * jnp.log2(jnp.maximum(top, 1e-30)))
    factor = QUANT * jnp.exp2(-0.125 * level)
    group = lane_group((16, LANES))
    scales = level[0:16]
    for t in range(1, rows // 16):
        scales = jnp.where(group == t, level[16 * t : 16 * t + 16], scales)
    scales = scales.astype(jnp.int32).astype(jnp.int16)
    msg_ref[block, 0] = scales
    numbers = [jnp.round(tile * factor).astype(jnp.int32) for tile in tiles]
    for c, number in enumerate(numbers):
        coded = number.astype(jnp.int16)
        for t in range(rows // 16):
            msg_ref[block, 1 + t * len(tiles) + c] = coded[16 * t : 16 * t + 16]
    return scales, numbers


def as_float(x):
    return x.astype(jnp.int32).astype(jnp.float32)


def factors_of(scales, row_tiles):
    scales = as_float(scales)
    group = lane_group((16, LANES))
    factors = []
    for t in range(row_tiles):
        level = jnp.where(group == t, scales, 0.0)
        for shift in (LANES // 2, LANES // 4):
            level = level + pltpu.roll(level, shift, axis=1)
        factors.append(jnp.exp2(0.125 * level) * (1.0 / QUANT))
    return factors


def unpack(read, row_tiles, col_tiles):
    factors = factors_of(read(0), row_tiles)
    return [
        jnp.concatenate([as_float(read(1 + t * col_tiles + c)) * factors[t] for t in range(row_tiles)], axis=0) for c in range(col_tiles)
    ]


def sums_kernel(
    me_ref, ids_ref, gain_ref, weight_ref, reflect_ref, conf_ref, sun_ref, prior_ref, keep_ref, msg_ref, sums_ref, kernels_ref, *, scale, rows_here
):
    dates, bands, tile_rows, cols = reflect_ref.shape
    me = me_ref[0]
    block = rows_here * ENTRIES
    obs_count = 3 * bands
    first_tile = pl.program_id(1) * (cols // LANES)

    def lane_tile(index, carry):
        lanes = pl.ds(pl.multiple_of(index * LANES, LANES), LANES)
        sensors = [ids_ref[me * dates + d] for d in range(dates)]

        def store(top, entry, total):
            sums_ref[first_tile + index, pl.ds(top * ENTRIES + entry, 8, stride=ENTRIES), :] = total

        def plus(total, term):
            return term if total is None else total + term

        for top in range(0, tile_rows, 8):
            normal = [None] * 6
            for d in range(dates):
                volume, geometric = ross_li(
                    sun_ref[d, 0, top : top + 8, lanes], sun_ref[d, 1, top : top + 8, lanes], sun_ref[d, 2, top : top + 8, lanes]
                )
                weight = conf_ref[d, top : top + 8, lanes].astype(jnp.float32) * (weight_ref[sensors[d]] * scale)
                weighted_vol = weight * volume
                weighted_geo = weight * geometric
                for i, value in enumerate((weight, weighted_vol, weighted_geo)):
                    kernels_ref[d, i, top : top + 8, :] = value
                terms = (weight, weighted_vol, weighted_geo, weighted_vol * volume, weighted_vol * geometric, weighted_geo * geometric)
                normal = [plus(total, term) for total, term in zip(normal, terms)]
            for k in range(6):
                store(top, obs_count + k, normal[k])
        for b in range(bands):
            observed = [None] * 3
            for d in range(dates):
                signal = reflect_ref[d, b, :, lanes].astype(jnp.float32) * gain_ref[sensors[d], b]
                observed = [plus(total, kernels_ref[d, i] * signal) for i, total in enumerate(observed)]
            for i in range(3):
                for top in range(0, tile_rows, 8):
                    store(top, 3 * b + i, observed[i][top : top + 8])
        return carry

    lax.fori_loop(0, cols // LANES, lane_tile, 0)

    @pl.when(pl.program_id(1) == pl.num_programs(1) - 1)
    def _():
        tiles = range(sums_ref.shape[0])
        first_row = pl.program_id(0) * tile_rows
        for row, source in ((me * rows_here - 1 - first_row, 0), ((me + 1) * rows_here - first_row, rows_here - 1)):

            @pl.when((row >= 0) & (row < tile_rows))
            def _():
                for c in tiles:
                    lanes = slice(c * LANES, (c + 1) * LANES)
                    at = pl.ds(pl.multiple_of(row * ENTRIES, 8), obs_count)
                    part = jnp.concatenate([prior_ref[e, source : source + 1, lanes] for e in range(obs_count)], axis=0)
                    sums_ref[c, at, :] = sums_ref[c, at, :] + SMOOTH_PULL * part

        bit = me % 2
        for j in range(keep_ref.shape[0]):
            own = pl.ds(pl.multiple_of((2 * j + bit) * block, 8), block)
            other = pl.ds(pl.multiple_of((2 * j + 1 - bit) * block, 8), block)
            for c in tiles:
                keep_ref[j, :, c * LANES : (c + 1) * LANES] = sums_ref[c, own, :]
            pack([sums_ref[c, other, :] for c in tiles], msg_ref, j)


def partial_sums(me, reflect, clear_conf, sun_view, sensor_id, band_gain, sensor_weight, prior, scale, chunk):
    dates, bands, rows, cols = reflect.shape
    cols = cols // CHUNKS
    rows_here = prior.shape[1]
    count = rows // rows_here
    tile_rows = 16
    width = min(256, cols)
    first = chunk * (cols // width)
    block = rows_here * ENTRIES
    per_tile = tile_rows // rows_here // 2
    places = 1 + block // 16 * (cols // LANES)
    smem = pl.BlockSpec(memory_space=pltpu.SMEM)
    return pl.pallas_call(
        functools.partial(sums_kernel, scale=scale, rows_here=rows_here),
        grid=(rows // tile_rows, cols // width),
        in_specs=[
            smem,
            smem,
            smem,
            smem,
            pl.BlockSpec((dates, bands, tile_rows, width), lambda i, j: (0, 0, i, first + j)),
            pl.BlockSpec((dates, tile_rows, width), lambda i, j: (0, i, first + j)),
            pl.BlockSpec((dates, 3, tile_rows, width), lambda i, j: (0, 0, i, first + j)),
            pl.BlockSpec((3 * bands, rows_here, cols), lambda i, j: (0, 0, chunk)),
        ],
        out_specs=[
            pl.BlockSpec((per_tile, block, cols), lambda i, j: (i, 0, 0)),
            pl.BlockSpec((per_tile, places, 16, LANES), lambda i, j: (i, 0, 0, 0)),
        ],
        out_shape=[
            jax.ShapeDtypeStruct((count // 2, block, cols), jnp.float32),
            jax.ShapeDtypeStruct((count // 2, places, 16, LANES), jnp.int16),
        ],
        scratch_shapes=[
            pltpu.VMEM((cols // LANES, tile_rows * ENTRIES, LANES), jnp.float32),
            pltpu.VMEM((dates, 3, tile_rows, LANES), jnp.float32),
        ],
        compiler_params=pltpu.CompilerParams(vmem_limit_bytes=(62 if chunk == 0 else 52) * 2**20),
        name="partial_sums",
    )(me, sensor_id, band_gain, sensor_weight, reflect, clear_conf, sun_view, prior)


def add_split_kernel(bit_ref, *refs, place):
    *parts, keep_ref, msg_ref = refs
    count, block, _ = keep_ref.shape
    bit = bit_ref[0]

    def total(j):
        tiles = []
        for kept_ref, got_ref in zip(parts[0::2], parts[1::2]):
            here = kept_ref.shape[2] // LANES
            came = unpack(lambda at: got_ref[j, at], block // 16, here)
            tiles += [kept_ref[j, :, c * LANES : (c + 1) * LANES] + came[c] for c in range(here)]
        return tiles

    for q in range(count):
        low = q % 2**place
        first = (q - low) * 2 + low
        pack(total(first + (1 - bit) * 2**place), msg_ref, q)
        for c, tile in enumerate(total(first + bit * 2**place)):
            keep_ref[q, :, c * LANES : (c + 1) * LANES] = tile


def add_split(bit, place, *parts):
    count, block, _ = parts[0].shape
    cols = sum(kept.shape[2] for kept in parts[0::2])
    vmem = pl.BlockSpec(memory_space=pltpu.VMEM)
    return pl.pallas_call(
        functools.partial(add_split_kernel, place=place),
        in_specs=[pl.BlockSpec(memory_space=pltpu.SMEM)] + [vmem] * len(parts),
        out_specs=[vmem, vmem],
        out_shape=[
            jax.ShapeDtypeStruct((count // 2, block, cols), jnp.float32),
            jax.ShapeDtypeStruct((count // 2, 1 + block // 16 * (cols // LANES), 16, LANES), jnp.int16),
        ],
        compiler_params=pltpu.CompilerParams(vmem_limit_bytes=24 * 2**20),
        name="add_split",
    )(bit, *parts)


def take(ref, start, size, stride):
    at = pl.ds(start, size, stride=stride)
    return jnp.concatenate([ref[c, at, :] for c in range(ref.shape[0])], axis=1)


def put(ref, start, size, stride, value):
    at = pl.ds(start, size, stride=stride)
    for c in range(ref.shape[0]):
        ref[c, at, :] = value[:, c * LANES : (c + 1) * LANES]


def beside_columns(x):
    cols = x.shape[1]
    col = lax.broadcasted_iota(jnp.int32, x.shape, 1)
    left = jnp.where(col == 0, 0.0, pltpu.roll(x, 1, axis=1))
    right = jnp.where(col == cols - 1, 0.0, pltpu.roll(x, cols - 1, axis=1))
    return left + right


def degree_of(row, shape, total_rows):
    col = lax.broadcasted_iota(jnp.int32, shape, 1)
    edge = (
        (row == 0).astype(jnp.float32)
        + (row == total_rows - 1).astype(jnp.float32)
        + (col == 0).astype(jnp.float32)
        + (col == shape[1] - 1).astype(jnp.float32)
    )
    return 4.0 - edge


def couple(n, v):
    return (
        n[0] * v[0] + n[1] * v[1] + n[2] * v[2],
        n[1] * v[0] + n[3] * v[1] + n[4] * v[2],
        n[2] * v[0] + n[4] * v[1] + n[5] * v[2],
    )


def residual_kernel(me_ref, prior_ref, *refs, total_rows):
    obs_count, rows_here, cols = prior_ref.shape
    *parts, out_ref, msg_ref, first_ref, sums_ref = refs
    block = rows_here * ENTRIES
    tiles = cols // LANES
    at = 0
    for kept_ref, got_ref in zip(parts[0::2], parts[1::2]):
        here = kept_ref.shape[2] // LANES
        came = unpack(lambda place: got_ref[0, place], block // 16, here)
        for c in range(here):
            sums_ref[at] = kept_ref[0, :, c * LANES : (c + 1) * LANES] + came[c]
            at += 1
    shape = (rows_here, cols)
    row = me_ref[0] * rows_here + lax.broadcasted_iota(jnp.int32, shape, 0)
    degree = degree_of(row, shape, total_rows)
    normal = [take(sums_ref, obs_count + k, rows_here, ENTRIES) for k in range(6)]
    for b in range(obs_count // 3):
        fields = [prior_ref[3 * b + i] for i in range(3)]
        coupled = couple(normal, fields)
        for i in range(3):
            field = fields[i]
            beside = beside_columns(field)
            if rows_here > 1:
                zero = jnp.zeros((1, cols), jnp.float32)
                beside = beside + jnp.concatenate([zero, field[:-1]], axis=0) + jnp.concatenate([field[1:], zero], axis=0)
            entry = 3 * b + i
            observed = take(sums_ref, entry, rows_here, ENTRIES)
            put(sums_ref, entry, rows_here, ENTRIES, observed - coupled[i] - SMOOTH_PULL * (degree * field - beside))
    for c in range(tiles):
        out_ref[:, c * LANES : (c + 1) * LANES] = sums_ref[c]
    scales, numbers = pack([sums_ref[c] for c in range(tiles)], msg_ref, 0)
    first_ref[0] = scales
    for c in range(tiles):
        first_ref[1 + c] = numbers[c][0:16].astype(jnp.int16)
    left = jnp.concatenate([number[16:obs_count] for number in numbers], axis=0)
    spare = (first_ref.shape[0] - 1 - tiles) * 16 - left.shape[0]
    if spare:
        left = jnp.concatenate([left, jnp.zeros((spare, LANES), jnp.int32)], axis=0)
    for t in range(left.shape[0] // 16):
        first_ref[1 + tiles + t] = left[16 * t : 16 * t + 16].astype(jnp.int16)


def krylov_kernel(me_ref, own_ref, mate_ref, across_ref, zero_ref, one_ref, two_ref, gram_ref, window_ref, *, total_rows, rows_here):
    cols = own_ref.shape[1]
    obs_count = ENTRIES - 6
    tiles = cols // LANES
    row_tiles = own_ref.shape[0] // 16

    def lay(place, part, r):
        at = pl.ds(place, ENTRIES, stride=8)
        for c in range(tiles):
            window_ref[c, at, :] = part[c][r * ENTRIES : (r + 1) * ENTRIES]

    own = [own_ref[:, c * LANES : (c + 1) * LANES] for c in range(tiles)]
    mate = unpack(lambda place: mate_ref[place], row_tiles, tiles)
    across = unpack(lambda place: across_ref[place], row_tiles, tiles)
    odd = me_ref[0] % 2
    for r in range(2):
        lay(2 + r, own, r)
        lay(4 * (1 - odd) + r, mate, r)
        lay(4 * odd + r, across, r)
    for empty in (6, 7):
        put(window_ref, empty, ENTRIES, 8, jnp.zeros((ENTRIES, cols), jnp.float32))
    window = lambda entry: jnp.concatenate([window_ref[c, entry * 8 : entry * 8 + 8, :] for c in range(cols // LANES)], axis=1)
    shape = (8, cols)
    place = lax.broadcasted_iota(jnp.int32, shape, 0)
    row = me_ref[0] * rows_here + place - 2
    inside = ((row >= 0) & (row < total_rows)).astype(jnp.float32) * GAIN
    own_rows = (place == 2) | (place == 3)
    diag = inside * (PRIOR_PULL - SHIFT + SMOOTH_PULL * degree_of(row, shape, total_rows))
    pull = inside * SMOOTH_PULL
    normal = [window(obs_count + k) * inside for k in range(6)]
    acc = [jnp.zeros((8, LANES), jnp.float32) for _ in range(6)]

    def apply(v, last=False):
        coupled = couple(normal, v)
        out = []
        for i in range(3):
            x = v[i]
            above = pltpu.roll(x, 7, axis=0)
            beside = beside_columns(x) + (2.0 * above if last else above + pltpu.roll(x, 1, axis=0))
            out.append(coupled[i] + diag * x - pull * beside)
        return out

    def fold(x):
        total = x[:, 0:LANES]
        for c in range(LANES, cols, LANES):
            total = total + x[:, c : c + LANES]
        return total

    for b in range(obs_count // 3):
        zero = [window(3 * b + i) for i in range(3)]
        one = apply(zero)
        two = apply(one)
        three = apply(two, last=True)
        for i in range(3):
            zero_ref[3 * b + i] = zero[i][2:4]
            one_ref[3 * b + i] = one[i][2:4]
            two_ref[3 * b + i] = two[i][2:4]
            v = [zero[i], one[i], two[i], three[i]]
            for k in range(6):
                acc[k] = acc[k] + fold(v[k // 2] * v[(k + 1) // 2])
    own_tile = own_rows[:, 0:LANES]
    tile_row = lax.broadcasted_iota(jnp.int32, (8, LANES), 0)
    gram = jnp.zeros((8, LANES), jnp.float32)
    for k in range(6):
        moment = jnp.sum(jnp.where(own_tile, acc[k], 0.0))
        gram = jnp.where(tile_row == k, moment, gram)
    gram_ref[...] = gram


def far_kernel(gram_ref, two_ref, far_ref, out_ref):
    obs_count, _, cols = two_ref.shape
    tiles = cols // LANES
    rest = obs_count - 16
    factors = factors_of(far_ref[0], 2)
    left = jnp.concatenate([as_float(far_ref[t]) for t in range(1 + tiles, far_ref.shape[0])], axis=0)
    total = jnp.zeros((obs_count, LANES), jnp.float32)
    for c in range(tiles):
        far = jnp.concatenate([as_float(far_ref[1 + c]) * factors[0], left[rest * c : rest * (c + 1)] * factors[1][0:rest]], axis=0)
        mine = jnp.concatenate([two_ref[e, 1:2, c * LANES : (c + 1) * LANES] for e in range(obs_count)], axis=0)
        total = total + far * mine
    part = (-2.0 * (GAIN * SMOOTH_PULL) ** 3) * jnp.sum(total)
    row = lax.broadcasted_iota(jnp.int32, (8, LANES), 0)
    out_ref[...] = gram_ref[...] + jnp.where(row == 5, part, 0.0)


def combine_kernel(*refs):
    *gram_refs, prior_ref, zero_ref, one_ref, two_ref, out_ref = refs
    gram = gram_refs[0][...]
    for ref in gram_refs[1:]:
        gram = gram + ref[...]
    m = [gram[k : k + 1, :] for k in range(6)]
    h = {(i, j): m[i + j + 1] * (1.0 / GAIN) + SHIFT * m[i + j] for i in range(3) for j in range(i, 3)}
    l10 = h[0, 1] / h[0, 0]
    l20 = h[0, 2] / h[0, 0]
    d1 = h[1, 1] - l10 * h[0, 1]
    t = h[1, 2] - l20 * h[0, 1]
    ok1 = d1 > 1e-6 * h[1, 1]
    inv1 = jnp.where(ok1, 1.0 / jnp.where(ok1, d1, 1.0), 0.0)
    l21 = t * inv1
    d2 = h[2, 2] - l20 * h[0, 2] - l21 * t
    ok2 = ok1 & (d2 > 1e-6 * h[2, 2])
    inv2 = jnp.where(ok2, 1.0 / jnp.where(ok2, d2, 1.0), 0.0)
    z1 = m[1] - l10 * m[0]
    z2 = m[2] - l20 * m[0] - l21 * z1
    y2 = z2 * inv2
    y1 = z1 * inv1 - l21 * y2
    y0 = m[0] / h[0, 0] - l10 * y1 - l20 * y2
    cols = prior_ref.shape[2]
    for c in range(0, cols, LANES):
        lanes = slice(c, c + LANES)
        out_ref[:, :, lanes] = (
            prior_ref[:, :, lanes] + y0[None] * zero_ref[:, :, lanes] + y1[None] * one_ref[:, :, lanes] + y2[None] * two_ref[:, :, lanes]
        )


def on_device(reflect, clear_conf, sun_view, sensor_id, band_gain, sensor_weight, prior):
    rows_here, obs_count, cols = prior.shape
    prior = jnp.transpose(prior, (1, 0, 2))
    count = lax.axis_size("rows")
    total_rows = rows_here * count
    block = rows_here * ENTRIES
    tiles = cols // LANES
    me = lax.axis_index("rows").astype(jnp.int32).reshape(1)
    vmem = pl.BlockSpec(memory_space=pltpu.VMEM)
    smem = pl.BlockSpec(memory_space=pltpu.SMEM)
    params = pltpu.CompilerParams(vmem_limit_bytes=24 * 2**20)
    f32 = lambda *shape: jax.ShapeDtypeStruct(shape, jnp.float32)
    packed = lambda *shape: jax.ShapeDtypeStruct(shape + (16, LANES), jnp.int16)

    scale = 0.01 / (reflect.shape[0] * count)
    index = me
    parts = []
    for chunk in range(CHUNKS):
        kept, sent = partial_sums(
            index, reflect, clear_conf, sun_view, sensor_id, band_gain, sensor_weight, prior, scale, chunk
        )
        index, _ = lax.optimization_barrier((me, sent))
        parts.append((kept, sent))
    flip = lambda x, mask: lax.ppermute(x, "rows", [(i, i ^ mask) for i in range(count)])
    swap = lambda x, bit: flip(x, 1 << bit)
    bits = list(range(1, count.bit_length() - 1))
    parts = [(kept, swap(sent, 0)) for kept, sent in parts]
    if len(bits) >= 2:
        orders = [((bits[0], 0), (bits[1], 0)), ((bits[1], 1), (bits[0], 0))]
        for step in range(2):
            for chunk in range(CHUNKS):
                bit, place = orders[chunk % 2][step]
                kept, sent = add_split(me // 2**bit % 2, place, *parts[chunk])
                parts[chunk] = (kept, swap(sent, bit))
        bits = bits[2:]
    parts = [x for part in parts for x in part]
    for bit in bits:
        kept, sent = add_split(me // 2**bit % 2, 0, *parts)
        parts = [kept, swap(sent, bit)]

    own, msg, first = pl.pallas_call(
        functools.partial(residual_kernel, total_rows=total_rows),
        in_specs=[smem] + [vmem] * (1 + len(parts)),
        out_specs=[vmem, vmem, vmem],
        out_shape=[f32(block, cols), packed(1, 1 + block // 16 * tiles), packed(1 + tiles + -(-(obs_count - 16) * tiles // 16))],
        scratch_shapes=[pltpu.VMEM((tiles, block, LANES), jnp.float32)],
        compiler_params=params,
        name="residual",
    )(me, prior, *parts)

    msg = msg[0]
    mate = swap(msg, 0)
    border = [(i, i + 1) for i in range(1, count - 1, 2)]
    across = lax.ppermute(msg, "rows", border + [(target, source) for source, target in border])
    far = lax.ppermute(first, "rows", [(i + 2, i) for i in range(count - 2)])
    zero, one, two, gram = pl.pallas_call(
        functools.partial(krylov_kernel, total_rows=total_rows, rows_here=rows_here),
        in_specs=[smem, vmem, vmem, vmem],
        out_specs=[vmem] * 4,
        out_shape=[f32(obs_count, rows_here, cols)] * 3 + [f32(8, LANES)],
        scratch_shapes=[pltpu.VMEM((tiles, ENTRIES * 8, LANES), jnp.float32)],
        compiler_params=params,
        name="krylov",
    )(me, own, mate, across)

    grams = [
        pl.pallas_call(
            far_kernel, in_specs=[vmem] * 3, out_specs=vmem, out_shape=f32(8, LANES), compiler_params=params, name="far"
        )(gram, two, far)
    ]
    for bit in range(0, count.bit_length() - 1, 2):
        masks = [mask << bit for mask in (1, 2, 3) if mask << bit < count]
        gram = sum(grams[1:], grams[0])
        grams = [gram] + [flip(gram, mask) for mask in masks]
    out = pl.pallas_call(
        combine_kernel,
        in_specs=[vmem] * (len(grams) + 4),
        out_specs=vmem,
        out_shape=f32(obs_count, rows_here, cols),
        compiler_params=params,
        name="combine",
    )(*grams, prior, zero, one, two)
    return jnp.transpose(out, (1, 0, 2))


def solution(mesh):
    return jax.shard_map(
        on_device,
        mesh=mesh,
        in_specs=(
            P("rows", None, None, "tiles"),
            P("rows", None, "tiles"),
            P("rows", None, None, "tiles"),
            P(),
            P(),
            P(),
            P("rows", None, "tiles"),
        ),
        out_specs=P("rows", None, "tiles"),
        check_vma=False,
    )
```

profile of v0, /device:TPU:0, one launch (start us, length us, event | category | flops | bytes accessed | tf_op | source)
XLA Modules:
  0.0 58.7 jit_solution(7361443028992189489)
XLA Ops:
  0.0 6.4 %partial_sums.2 = (f32[8,48,512]{2,1,0:T(8,128)}, s16[8,13,16,128]{3,2,1,0:T(8,128)(2,1)}) custom-call(s32[1]{0:T(128)} %bitcast.me_ref, s32[128]{0:T(128)} %ids_ref.3, f32[4,6]{1,0:T(4,128)} %gain_ref.3, f32[4]{0:T(128)} %weight_ref.3, bf16[8,6,32,1024]{3,2,1,0:T(8,128)(2,1)} %reflect_ref.3, s32[8,32,1024]{2,1,0:T(8,128)} %conf_ref.3, ...), custom_call_target="tpu_custom_call" | custom-call | tf_op jit(solution)/shard_map/partial_sums/pallas_call | solution.py:205
  6.9 5.3 %partial_sums.3 = (f32[8,48,512]{2,1,0:T(8,128)S(1)}, s16[8,13,16,128]{3,2,1,0:T(8,128)(2,1)S(1)}) custom-call(s32[1]{0:T(128)} %bitcast.me_ref, s32[128]{0:T(128)S(1)} %copy-done.3, f32[4,6]{1,0:T(4,128)S(1)} %copy-done.2, f32[4]{0:T(128)S(1)} %copy-done.4, bf16[8,6,32,1024]{3,2,1,0:T(8,128)(2,1)} %reflect_ref.3, s32[8,32,1024]{2,1,0:T(8,128)} %conf_ref.3, ...), custom_call_target="tpu_custom_call" | custom-call | tf_op jit(solution)/shard_map/partial_sums/pallas_call | solution.py:205
  12.8 3.0 %collective-permute-start.1 = (s16[4,13,16,128]{3,2,1,0:T(8,128)(2,1)S(1)}, s16[4,13,16,128]{3,2,1,0:T(8,128)(2,1)S(1)}, u32[]{:S(2)}, u32[]{:S(2)}) collective-permute-start(s16[4,13,16,128]{3,2,1,0:T(8,128)(2,1)S(1)} %get-tuple-element.30), channel_id=1, source_target_pairs={{0,2},{1,3},{2,0},{3,1},{4,6},{5,7},{6,4},{7,5},{8,10},{9,11},{10,... | collective-permute-start | bytes 638984 | tf_op jit(solution)/shard_map/ppermute | solution.py:491
  16.2 1.7 %collective-permute-start.4 = (s16[4,13,16,128]{3,2,1,0:T(8,128)(2,1)S(1)}, s16[4,13,16,128]{3,2,1,0:T(8,128)(2,1)S(1)}, u32[]{:S(2)}, u32[]{:S(2)}) collective-permute-start(s16[4,13,16,128]{3,2,1,0:T(8,128)(2,1)S(1)} %get-tuple-element.37), channel_id=1, source_target_pairs={{0,4},{1,5},{2,6},{3,7},{4,0},{5,1},{6,2},{7,3},{8,12},{9,13},{10,... | collective-permute-start | bytes 638984 | tf_op jit(solution)/shard_map/ppermute | solution.py:491
  17.8 3.4 %collective-permute-done.1.refs_1_ = s16[4,13,16,128]{3,2,1,0:T(8,128)(2,1)S(1)} collective-permute-done((s16[4,13,16,128]{3,2,1,0:T(8,128)(2,1)S(1)}, s16[4,13,16,128]{3,2,1,0:T(8,128)(2,1)S(1)}, u32[]{:S(2)}, u32[]{:S(2)}) %collective-permute-start.1) | collective-permute-done | bytes 213024 | tf_op jit(solution)/shard_map/ppermute | solution.py:491
  21.6 1.9 %collective-permute-start.2 = (s16[2,13,16,128]{3,2,1,0:T(8,128)(2,1)S(1)}, s16[2,13,16,128]{3,2,1,0:T(8,128)(2,1)S(1)}, u32[]{:S(2)}, u32[]{:S(2)}) collective-permute-start(s16[2,13,16,128]{3,2,1,0:T(8,128)(2,1)S(1)} %get-tuple-element.32), channel_id=1, source_target_pairs={{0,4},{1,5},{2,6},{3,7},{4,0},{5,1},{6,2},{7,3},{8,12},{9,13},{10,... | collective-permute-start | bytes 319496 | tf_op jit(solution)/shard_map/ppermute | solution.py:491
  23.9 1.6 %collective-permute-start.5 = (s16[2,13,16,128]{3,2,1,0:T(8,128)(2,1)S(1)}, s16[2,13,16,128]{3,2,1,0:T(8,128)(2,1)S(1)}, u32[]{:S(2)}, u32[]{:S(2)}) collective-permute-start(s16[2,13,16,128]{3,2,1,0:T(8,128)(2,1)S(1)} %get-tuple-element.39), channel_id=1, source_target_pairs={{0,2},{1,3},{2,0},{3,1},{4,6},{5,7},{6,4},{7,5},{8,10},{9,11},{10,... | collective-permute-start | bytes 319496 | tf_op jit(solution)/shard_map/ppermute | solution.py:491
  25.5 0.9 %collective-permute-done.2.refs_1_ = s16[2,13,16,128]{3,2,1,0:T(8,128)(2,1)S(1)} collective-permute-done((s16[2,13,16,128]{3,2,1,0:T(8,128)(2,1)S(1)}, s16[2,13,16,128]{3,2,1,0:T(8,128)(2,1)S(1)}, u32[]{:S(2)}, u32[]{:S(2)}) %collective-permute-start.2) | collective-permute-done | bytes 106528 | tf_op jit(solution)/shard_map/ppermute | solution.py:491
  26.4 2.2 %collective-permute-done.5.refs_3_ = s16[2,13,16,128]{3,2,1,0:T(8,128)(2,1)S(1)} collective-permute-done((s16[2,13,16,128]{3,2,1,0:T(8,128)(2,1)S(1)}, s16[2,13,16,128]{3,2,1,0:T(8,128)(2,1)S(1)}, u32[]{:S(2)}, u32[]{:S(2)}) %collective-permute-start.5) | collective-permute-done | bytes 106528 | tf_op jit(solution)/shard_map/ppermute | solution.py:491
  29.0 2.7 %collective-permute-start.6 = (s16[1,25,16,128]{3,2,1,0:T(8,128)(2,1)S(1)}, s16[1,25,16,128]{3,2,1,0:T(8,128)(2,1)S(1)}, u32[]{:S(2)}, u32[]{:S(2)}) collective-permute-start(s16[1,25,16,128]{3,2,1,0:T(8,128)(2,1)S(1)} %get-tuple-element.41), channel_id=1, source_target_pairs={{0,8},{1,9},{2,10},{3,11},{4,12},{5,13},{6,14},{7,15},{8,0},{9,1},... | collective-permute-start | bytes 307208 | tf_op jit(solution)/shard_map/ppermute | solution.py:491
  31.7 4.1 %collective-permute-done.6.refs_1_ = s16[1,25,16,128]{3,2,1,0:T(8,128)(2,1)S(1)} collective-permute-done((s16[1,25,16,128]{3,2,1,0:T(8,128)(2,1)S(1)}, s16[1,25,16,128]{3,2,1,0:T(8,128)(2,1)S(1)}, u32[]{:S(2)}, u32[]{:S(2)}) %collective-permute-start.6) | collective-permute-done | bytes 102432 | tf_op jit(solution)/shard_map/ppermute | solution.py:491
  35.7 0.7 %residual.1 = (f32[48,1024]{1,0:T(8,128)S(1)}, s16[1,25,16,128]{3,2,1,0:T(8,128)(2,1)S(1)}, s16[10,16,128]{2,1,0:T(8,128)(2,1)S(1)}) custom-call(s32[1]{0:T(128)} %bitcast.me_ref, f32[18,2,1024]{2,1,0:T(2,128)S(1)} %bitcast.6, f32[1,48,1024]{2,1,0:T(8,128)S(1)} %get-tuple-element.40.refs_0_, s16[1,25,16,128]{3,2,1,0:T(8,128)(2,1)S(1)} %collective-permute-done.6.refs_1_), custom_call_target="tpu_custom_call" | custom-call | tf_op jit(solution)/shard_map/residual/pallas_call | solution.py:508
  36.5 0.7 %collective-permute-start.8 = (s16[25,16,128]{2,1,0:T(8,128)(2,1)S(1)}, s16[25,16,128]{2,1,0:T(8,128)(2,1)S(1)}, u32[]{:S(2)}, u32[]{:S(2)}) collective-permute-start(s16[25,16,128]{2,1,0:T(8,128)(2,1)S(1)} %bitcast.8), channel_id=1, source_target_pairs={{1,2},{3,4},{5,6},{7,8},{9,10},{11,12},{13,14},{2,1},{4,3},{6,5},{... | collective-permute-start | bytes 307208 | tf_op jit(solution)/shard_map/ppermute | solution.py:521
  37.1 2.9 %collective-permute-start.7 = (s16[25,16,128]{2,1,0:T(8,128)(2,1)S(1)}, s16[25,16,128]{2,1,0:T(8,128)(2,1)S(1)}, u32[]{:S(2)}, u32[]{:S(2)}) collective-permute-start(s16[25,16,128]{2,1,0:T(8,128)(2,1)S(1)} %bitcast.9), channel_id=1, source_target_pairs={{0,1},{1,0},{2,3},{3,2},{4,5},{5,4},{6,7},{7,6},{8,9},{9,8},{10,11... | collective-permute-start | bytes 307208 | tf_op jit(solution)/shard_map/ppermute | solution.py:491
  40.1 1.3 %collective-permute-start.9 = (s16[10,16,128]{2,1,0:T(8,128)(2,1)S(1)}, s16[10,16,128]{2,1,0:T(8,128)(2,1)S(1)}, u32[]{:S(2)}, u32[]{:S(2)}) collective-permute-start(s16[10,16,128]{2,1,0:T(8,128)(2,1)S(1)} %get-tuple-element.46), channel_id=1, source_target_pairs={{2,0},{3,1},{4,2},{5,3},{6,4},{7,5},{8,6},{9,7},{10,8},{11,9},{12,... | collective-permute-start | bytes 122888 | tf_op jit(solution)/shard_map/ppermute | solution.py:522
  41.4 1.8 %krylov.1 = (f32[18,2,1024]{2,1,0:T(2,128)S(1)}, f32[18,2,1024]{2,1,0:T(2,128)S(1)}, f32[18,2,1024]{2,1,0:T(2,128)S(1)}, f32[8,128]{1,0:T(8,128)S(1)}) custom-call(s32[1]{0:T(128)} %bitcast.me_ref, f32[48,1024]{1,0:T(8,128)S(1)} %get-tuple-element.42.own_ref, s16[25,16,128]{2,1,0:T(8,128)(2,1)S(1)} %collective-permute-done.7.mate_ref, ...), custom_call_target="tpu_custom_call" | custom-call | tf_op jit(solution)/shard_map/krylov/pallas_call | solution.py:523
  43.2 2.7 %collective-permute-done.9.far_ref = s16[10,16,128]{2,1,0:T(8,128)(2,1)S(1)} collective-permute-done((s16[10,16,128]{2,1,0:T(8,128)(2,1)S(1)}, s16[10,16,128]{2,1,0:T(8,128)(2,1)S(1)}, u32[]{:S(2)}, u32[]{:S(2)}) %collective-permute-start.9) | collective-permute-done | bytes 40992 | tf_op jit(solution)/shard_map/ppermute | solution.py:522
  46.3 1.4 %collective-permute-start.11 = (f32[8,128]{1,0:T(8,128)S(1)}, f32[8,128]{1,0:T(8,128)S(1)}, u32[]{:S(2)}, u32[]{:S(2)}) collective-permute-start(f32[8,128]{1,0:T(8,128)S(1)} %far.1), channel_id=1, source_target_pairs={{0,2},{1,3},{2,0},{3,1},{4,6},{5,7},{6,4},{7,5},{8,10},{9,11},{10,... | collective-permute-start | bytes 12296 | tf_op jit(solution)/shard_map/ppermute | solution.py:491
  48.2 1.2 %collective-permute-done.12 = f32[8,128]{1,0:T(8,128)S(1)} collective-permute-done((f32[8,128]{1,0:T(8,128)S(1)}, f32[8,128]{1,0:T(8,128)S(1)}, u32[]{:S(2)}, u32[]{:S(2)}) %collective-permute-start.12) | collective-permute-done | bytes 4128 | tf_op jit(solution)/shard_map/ppermute | solution.py:491
  50.0 3.3 %collective-permute-start.15 = (f32[8,128]{1,0:T(8,128)S(1)}, f32[8,128]{1,0:T(8,128)S(1)}, u32[]{:S(2)}, u32[]{:S(2)}) collective-permute-start(f32[8,128]{1,0:T(8,128)S(1)} %add_add_fusion.refs_0_), channel_id=1, source_target_pairs={{0,12},{1,13},{2,14},{3,15},{4,8},{5,9},{6,10},{7,11},{8,4},{9,5},... | collective-permute-start | bytes 12296 | tf_op jit(solution)/shard_map/ppermute | solution.py:491
  53.3 1.1 %collective-permute-start.13 = (f32[8,128]{1,0:T(8,128)S(1)}, f32[8,128]{1,0:T(8,128)S(1)}, u32[]{:S(2)}, u32[]{:S(2)}) collective-permute-start(f32[8,128]{1,0:T(8,128)S(1)} %add_add_fusion.refs_0_), channel_id=1, source_target_pairs={{0,4},{1,5},{2,6},{3,7},{4,0},{5,1},{6,2},{7,3},{8,12},{9,13},{10,... | collective-permute-start | bytes 12296 | tf_op jit(solution)/shard_map/ppermute | solution.py:491
  54.5 1.0 %collective-permute-done.15.refs_3_ = f32[8,128]{1,0:T(8,128)S(1)} collective-permute-done((f32[8,128]{1,0:T(8,128)S(1)}, f32[8,128]{1,0:T(8,128)S(1)}, u32[]{:S(2)}, u32[]{:S(2)}) %collective-permute-start.15) | collective-permute-done | bytes 4128 | tf_op jit(solution)/shard_map/ppermute | solution.py:491
  55.5 2.4 %collective-permute-done.14.refs_2_ = f32[8,128]{1,0:T(8,128)S(1)} collective-permute-done((f32[8,128]{1,0:T(8,128)S(1)}, f32[8,128]{1,0:T(8,128)S(1)}, u32[]{:S(2)}, u32[]{:S(2)}) %collective-permute-start.14) | collective-permute-done | bytes 4128 | tf_op jit(solution)/shard_map/ppermute | solution.py:491
  57.8 0.9 %combine.1 = f32[18,2,1024]{2,1,0:T(2,128)} custom-call(f32[8,128]{1,0:T(8,128)S(1)} %add_add_fusion.refs_0_, f32[8,128]{1,0:T(8,128)S(1)} %collective-permute-done.13.refs_1_, f32[8,128]{1,0:T(8,128)S(1)} %collective-permute-done.14.refs_2_, f32[8,128]{1,0:T(8,128)S(1)} %collective-permute-done.15.refs_3_, f32[18,2,1024]{2,1,0:T(2,128)S(1)} %bitcast.7, ...), custom_call_target="tpu_custom_call" | custom-call | tf_op jit(solution)/shard_map/combine/pallas_call | solution.py:542
  (30 shorter events, 4.1 us)
Async XLA Ops:
  0.0 6.9 %copy-start = (f32[2,18,1024]{2,0,1:T(2,128)S(1)}, f32[2,18,1024]{2,0,1:T(2,128)}, u32[]{:S(2)}) copy-start(f32[2,18,1024]{2,0,1:T(2,128)} %param.13) | copy-start | bytes 442372
  0.0 6.9 %copy-start.2 = (f32[4,6]{1,0:T(4,128)S(1)}, f32[4,6]{1,0:T(4,128)}, u32[]{:S(2)}) copy-start(f32[4,6]{1,0:T(4,128)} %gain_ref.3) | copy-start | bytes 292
  0.0 6.9 %copy-start.3 = (s32[128]{0:T(128)S(1)}, s32[128]{0:T(128)}, u32[]{:S(2)}) copy-start(s32[128]{0:T(128)} %ids_ref.3) | copy-start | bytes 1540
  0.0 6.9 %copy-start.4 = (f32[4]{0:T(128)S(1)}, f32[4]{0:T(128)}, u32[]{:S(2)}) copy-start(f32[4]{0:T(128)} %weight_ref.3) | copy-start | bytes 52
  6.4 6.0 %copy-start.1 = (f32[8,48,512]{2,1,0:T(8,128)S(1)}, f32[8,48,512]{2,1,0:T(8,128)}, u32[]{:S(2)}) copy-start(f32[8,48,512]{2,1,0:T(8,128)} %get-tuple-element.27.refs_0_) | copy-start | bytes 2359300
  6.4 6.0 %collective-permute-start = (s16[8,13,16,128]{3,2,1,0:T(8,128)(2,1)}, s16[8,13,16,128]{3,2,1,0:T(8,128)(2,1)S(1)}, u32[]{:S(2)}, u32[]{:S(2)}) collective-permute-start(s16[8,13,16,128]{3,2,1,0:T(8,128)(2,1)} %get-tuple-element.28), channel_id=1, source_target_pairs={{0,1},{1,0},{2,3},{3,2},{4,5},{5,4},{6,7},{7,6},{8,9},{9,8},{10,11... | collective-permute-start | bytes 1277960 | tf_op jit(solution)/shard_map/ppermute | solution.py:491
  12.2 3.6 %collective-permute-start.3 = (s16[8,13,16,128]{3,2,1,0:T(8,128)(2,1)S(1)}, s16[8,13,16,128]{3,2,1,0:T(8,128)(2,1)S(1)}, u32[]{:S(2)}, u32[]{:S(2)}) collective-permute-start(s16[8,13,16,128]{3,2,1,0:T(8,128)(2,1)S(1)} %get-tuple-element.35), channel_id=1, source_target_pairs={{0,1},{1,0},{2,3},{3,2},{4,5},{5,4},{6,7},{7,6},{8,9},{9,8},{10,11... | collective-permute-start | bytes 1277960 | tf_op jit(solution)/shard_map/ppermute | solution.py:491
  12.8 8.5 %collective-permute-start.1 = (s16[4,13,16,128]{3,2,1,0:T(8,128)(2,1)S(1)}, s16[4,13,16,128]{3,2,1,0:T(8,128)(2,1)S(1)}, u32[]{:S(2)}, u32[]{:S(2)}) collective-permute-start(s16[4,13,16,128]{3,2,1,0:T(8,128)(2,1)S(1)} %get-tuple-element.30), channel_id=1, source_target_pairs={{0,2},{1,3},{2,0},{3,1},{4,6},{5,7},{6,4},{7,5},{8,10},{9,11},{10,... | collective-permute-start | bytes 638984 | tf_op jit(solution)/shard_map/ppermute | solution.py:491
  16.2 7.3 %collective-permute-start.4 = (s16[4,13,16,128]{3,2,1,0:T(8,128)(2,1)S(1)}, s16[4,13,16,128]{3,2,1,0:T(8,128)(2,1)S(1)}, u32[]{:S(2)}, u32[]{:S(2)}) collective-permute-start(s16[4,13,16,128]{3,2,1,0:T(8,128)(2,1)S(1)} %get-tuple-element.37), channel_id=1, source_target_pairs={{0,4},{1,5},{2,6},{3,7},{4,0},{5,1},{6,2},{7,3},{8,12},{9,13},{10,... | collective-permute-start | bytes 638984 | tf_op jit(solution)/shard_map/ppermute | solution.py:491
  21.6 4.8 %collective-permute-start.2 = (s16[2,13,16,128]{3,2,1,0:T(8,128)(2,1)S(1)}, s16[2,13,16,128]{3,2,1,0:T(8,128)(2,1)S(1)}, u32[]{:S(2)}, u32[]{:S(2)}) collective-permute-start(s16[2,13,16,128]{3,2,1,0:T(8,128)(2,1)S(1)} %get-tuple-element.32), channel_id=1, source_target_pairs={{0,4},{1,5},{2,6},{3,7},{4,0},{5,1},{6,2},{7,3},{8,12},{9,13},{10,... | collective-permute-start | bytes 319496 | tf_op jit(solution)/shard_map/ppermute | solution.py:491
  23.9 4.8 %collective-permute-start.5 = (s16[2,13,16,128]{3,2,1,0:T(8,128)(2,1)S(1)}, s16[2,13,16,128]{3,2,1,0:T(8,128)(2,1)S(1)}, u32[]{:S(2)}, u32[]{:S(2)}) collective-permute-start(s16[2,13,16,128]{3,2,1,0:T(8,128)(2,1)S(1)} %get-tuple-element.39), channel_id=1, source_target_pairs={{0,2},{1,3},{2,0},{3,1},{4,6},{5,7},{6,4},{7,5},{8,10},{9,11},{10,... | collective-permute-start | bytes 319496 | tf_op jit(solution)/shard_map/ppermute | solution.py:491
  29.0 6.7 %collective-permute-start.6 = (s16[1,25,16,128]{3,2,1,0:T(8,128)(2,1)S(1)}, s16[1,25,16,128]{3,2,1,0:T(8,128)(2,1)S(1)}, u32[]{:S(2)}, u32[]{:S(2)}) collective-permute-start(s16[1,25,16,128]{3,2,1,0:T(8,128)(2,1)S(1)} %get-tuple-element.41), channel_id=1, source_target_pairs={{0,8},{1,9},{2,10},{3,11},{4,12},{5,13},{6,14},{7,15},{8,0},{9,1},... | collective-permute-start | bytes 307208 | tf_op jit(solution)/shard_map/ppermute | solution.py:491
  36.5 4.9 %collective-permute-start.8 = (s16[25,16,128]{2,1,0:T(8,128)(2,1)S(1)}, s16[25,16,128]{2,1,0:T(8,128)(2,1)S(1)}, u32[]{:S(2)}, u32[]{:S(2)}) collective-permute-start(s16[25,16,128]{2,1,0:T(8,128)(2,1)S(1)} %bitcast.8), channel_id=1, source_target_pairs={{1,2},{3,4},{5,6},{7,8},{9,10},{11,12},{13,14},{2,1},{4,3},{6,5},{... | collective-permute-start | bytes 307208 | tf_op jit(solution)/shard_map/ppermute | solution.py:521
  37.1 4.2 %collective-permute-start.7 = (s16[25,16,128]{2,1,0:T(8,128)(2,1)S(1)}, s16[25,16,128]{2,1,0:T(8,128)(2,1)S(1)}, u32[]{:S(2)}, u32[]{:S(2)}) collective-permute-start(s16[25,16,128]{2,1,0:T(8,128)(2,1)S(1)} %bitcast.9), channel_id=1, source_target_pairs={{0,1},{1,0},{2,3},{3,2},{4,5},{5,4},{6,7},{7,6},{8,9},{9,8},{10,11... | collective-permute-start | bytes 307208 | tf_op jit(solution)/shard_map/ppermute | solution.py:491
  40.1 5.9 %collective-permute-start.9 = (s16[10,16,128]{2,1,0:T(8,128)(2,1)S(1)}, s16[10,16,128]{2,1,0:T(8,128)(2,1)S(1)}, u32[]{:S(2)}, u32[]{:S(2)}) collective-permute-start(s16[10,16,128]{2,1,0:T(8,128)(2,1)S(1)} %get-tuple-element.46), channel_id=1, source_target_pairs={{2,0},{3,1},{4,2},{5,3},{6,4},{7,5},{8,6},{9,7},{10,8},{11,9},{12,... | collective-permute-start | bytes 122888 | tf_op jit(solution)/shard_map/ppermute | solution.py:522
  46.3 3.1 %collective-permute-start.12 = (f32[8,128]{1,0:T(8,128)S(1)}, f32[8,128]{1,0:T(8,128)S(1)}, u32[]{:S(2)}, u32[]{:S(2)}) collective-permute-start(f32[8,128]{1,0:T(8,128)S(1)} %far.1), channel_id=1, source_target_pairs={{0,3},{1,2},{2,1},{3,0},{4,7},{5,6},{6,5},{7,4},{8,11},{9,10},{10,... | collective-permute-start | bytes 12296 | tf_op jit(solution)/shard_map/ppermute | solution.py:491
  46.3 3.7 %collective-permute-start.11 = (f32[8,128]{1,0:T(8,128)S(1)}, f32[8,128]{1,0:T(8,128)S(1)}, u32[]{:S(2)}, u32[]{:S(2)}) collective-permute-start(f32[8,128]{1,0:T(8,128)S(1)} %far.1), channel_id=1, source_target_pairs={{0,2},{1,3},{2,0},{3,1},{4,6},{5,7},{6,4},{7,5},{8,10},{9,11},{10,... | collective-permute-start | bytes 12296 | tf_op jit(solution)/shard_map/ppermute | solution.py:491
  47.8 2.2 %collective-permute-start.10 = (f32[8,128]{1,0:T(8,128)S(1)}, f32[8,128]{1,0:T(8,128)S(1)}, u32[]{:S(2)}, u32[]{:S(2)}) collective-permute-start(f32[8,128]{1,0:T(8,128)S(1)} %far.1), channel_id=1, source_target_pairs={{0,1},{1,0},{2,3},{3,2},{4,5},{5,4},{6,7},{7,6},{8,9},{9,8},{10,11... | collective-permute-start | bytes 12296 | tf_op jit(solution)/shard_map/ppermute | solution.py:491
  50.0 5.5 %collective-permute-start.15 = (f32[8,128]{1,0:T(8,128)S(1)}, f32[8,128]{1,0:T(8,128)S(1)}, u32[]{:S(2)}, u32[]{:S(2)}) collective-permute-start(f32[8,128]{1,0:T(8,128)S(1)} %add_add_fusion.refs_0_), channel_id=1, source_target_pairs={{0,12},{1,13},{2,14},{3,15},{4,8},{5,9},{6,10},{7,11},{8,4},{9,5},... | collective-permute-start | bytes 12296 | tf_op jit(solution)/shard_map/ppermute | solution.py:491
  53.3 4.5 %collective-permute-start.14 = (f32[8,128]{1,0:T(8,128)S(1)}, f32[8,128]{1,0:T(8,128)S(1)}, u32[]{:S(2)}, u32[]{:S(2)}) collective-permute-start(f32[8,128]{1,0:T(8,128)S(1)} %add_add_fusion.refs_0_), channel_id=1, source_target_pairs={{0,8},{1,9},{2,10},{3,11},{4,12},{5,13},{6,14},{7,15},{8,0},{9,1},... | collective-permute-start | bytes 12296 | tf_op jit(solution)/shard_map/ppermute | solution.py:491
  53.3 4.5 %collective-permute-start.13 = (f32[8,128]{1,0:T(8,128)S(1)}, f32[8,128]{1,0:T(8,128)S(1)}, u32[]{:S(2)}, u32[]{:S(2)}) collective-permute-start(f32[8,128]{1,0:T(8,128)S(1)} %add_add_fusion.refs_0_), channel_id=1, source_target_pairs={{0,4},{1,5},{2,6},{3,7},{4,0},{5,1},{6,2},{7,3},{8,12},{9,13},{10,... | collective-permute-start | bytes 12296 | tf_op jit(solution)/shard_map/ppermute | solution.py:491
where the time goes:
time: 59 us; the launch traced here: 58.7 us
  starting transfers between devices  22.7 us (38%)
  waiting for transfers between devices  18.6 us (32%)
  Pallas kernels  17.2 us (29%)
    ppermute x14, starting transfers between devices, on_device(): lax.ppermute(x, 'rows', [(i, i ^ mask) for i in range(count)])  20.8 us
    ppermute x14, waiting for transfers between devices, on_device(): lax.ppermute(x, 'rows', [(i, i ^ mask) for i in range(count)])  15.9 us
    pallas_call x2, Pallas kernels, partial_sums(): pl.pallas_call(functools.partial(sums_kernel, scale=scale, rows_here=rows...  11.6 us
    ppermute x1, waiting for transfers between devices, on_device(): far = lax.ppermute(first, 'rows', [(i + 2, i) for i in range(count - 2)])  2.74 us
    pallas_call x5, Pallas kernels, add_split(): pl.pallas_call(functools.partial(add_split_kernel, place=place), in_specs...  1.9 us
    pallas_call x1, Pallas kernels, on_device(): pl.pallas_call(functools.partial(krylov_kernel, total_rows=total_rows, ro...  1.82 us
    ppermute x1, starting transfers between devices, on_device(): far = lax.ppermute(first, 'rows', [(i + 2, i) for i in range(count - 2)])  1.28 us
  transfers between devices with their start and end apart: 16, of which 9 were waited for; matrix products, arithmetic and copies ran while one was open for 0% of the time, Pallas kernels for 15%

commit v1 on v0

--- a/solution.py
+++ b/solution.py
@@ -122,35 +122,71 @@
 
 
 def sums_kernel(
-    me_ref, ids_ref, gain_ref, weight_ref, reflect_ref, conf_ref, sun_ref, prior_ref, keep_ref, msg_ref, sums_ref, kernels_ref, *, scale, rows_here
+    me_ref,
+    ids_ref,
+    gain_ref,
+    weight_ref,
+    reflect_hbm,
+    conf_hbm,
+    sun_hbm,
+    prior_ref,
+    keep_ref,
+    msg_ref,
+    sums_ref,
+    kernels_ref,
+    reflect_ref,
+    conf_ref,
+    sun_ref,
+    sems,
+    *,
+    scale,
+    rows_here,
+    first_col,
 ):
-    dates, bands, tile_rows, cols = reflect_ref.shape
+    steps, dates, bands, tile_rows, _ = reflect_ref.shape
+    lane_tiles = sums_ref.shape[0]
     me = me_ref[0]
     block = rows_here * ENTRIES
     obs_count = 3 * bands
-    first_tile = pl.program_id(1) * (cols // LANES)
-
-    def lane_tile(index, carry):
-        lanes = pl.ds(pl.multiple_of(index * LANES, LANES), LANES)
+
+    def copies(step):
+        rows = pl.ds(pl.multiple_of(step // lane_tiles * tile_rows, tile_rows), tile_rows)
+        cols = pl.ds(pl.multiple_of(first_col + step % lane_tiles * LANES, LANES), LANES)
+        return (
+            pltpu.make_async_copy(sun_hbm.at[:, :, rows, cols], sun_ref.at[step], sems.at[step, 0]),
+            pltpu.make_async_copy(conf_hbm.at[:, rows, cols], conf_ref.at[step], sems.at[step, 1]),
+            pltpu.make_async_copy(reflect_hbm.at[:, :, rows, cols], reflect_ref.at[step], sems.at[step, 2]),
+        )
+
+    def start(step, carry):
+        for copy in copies(step):
+            copy.start()
+        return carry
+
+    lax.fori_loop(0, steps, start, 0)
+
+    def lane_tile(index, row_tile):
+        step = row_tile * lane_tiles + index
+        for copy in copies(step):
+            copy.wait()
         sensors = [ids_ref[me * dates + d] for d in range(dates)]
 
         def store(top, entry, total):
-            sums_ref[first_tile + index, pl.ds(top * ENTRIES + entry, 8, stride=ENTRIES), :] = total
+            sums_ref[index, pl.ds(top * ENTRIES + entry, 8, stride=ENTRIES), :] = total
 
         def plus(total, term):
             return term if total is None else total + term
 
         for top in range(0, tile_rows, 8):
+            here = slice(top, top + 8)
             normal = [None] * 6
             for d in range(dates):
-                volume, geometric = ross_li(
-                    sun_ref[d, 0, top : top + 8, lanes], sun_ref[d, 1, top : top + 8, lanes], sun_ref[d, 2, top : top + 8, lanes]
-                )
-                weight = conf_ref[d, top : top + 8, lanes].astype(jnp.float32) * (weight_ref[sensors[d]] * scale)
+                volume, geometric = ross_li(*[sun_ref[step, d, angle, here, :] for angle in range(3)])
+                weight = conf_ref[step, d, here, :].astype(jnp.float32) * (weight_ref[sensors[d]] * scale)
                 weighted_vol = weight * volume
                 weighted_geo = weight * geometric
                 for i, value in enumerate((weight, weighted_vol, weighted_geo)):
-                    kernels_ref[d, i, top : top + 8, :] = value
+                    kernels_ref[d, i, here, :] = value
                 terms = (weight, weighted_vol, weighted_geo, weighted_vol * volume, weighted_vol * geometric, weighted_geo * geometric)
                 normal = [plus(total, term) for total, term in zip(normal, terms)]
             for k in range(6):
@@ -158,19 +194,17 @@
         for b in range(bands):
             observed = [None] * 3
             for d in range(dates):
-                signal = reflect_ref[d, b, :, lanes].astype(jnp.float32) * gain_ref[sensors[d], b]
+                signal = reflect_ref[step, d, b].astype(jnp.float32) * gain_ref[sensors[d], b]
                 observed = [plus(total, kernels_ref[d, i] * signal) for i, total in enumerate(observed)]
             for i in range(3):
                 for top in range(0, tile_rows, 8):
                     store(top, 3 * b + i, observed[i][top : top + 8])
-        return carry
-
-    lax.fori_loop(0, cols // LANES, lane_tile, 0)
-
-    @pl.when(pl.program_id(1) == pl.num_programs(1) - 1)
-    def _():
-        tiles = range(sums_ref.shape[0])
-        first_row = pl.program_id(0) * tile_rows
+        return row_tile
+
+    def row_tile_sums(row_tile, carry):
+        lax.fori_loop(0, lane_tiles, lane_tile, row_tile)
+        tiles = range(lane_tiles)
+        first_row = row_tile * tile_rows
         for row, source in ((me * rows_here - 1 - first_row, 0), ((me + 1) * rows_here - first_row, rows_here - 1)):
 
             @pl.when((row >= 0) & (row < tile_rows))
@@ -182,12 +216,16 @@
                     sums_ref[c, at, :] = sums_ref[c, at, :] + SMOOTH_PULL * part
 
         bit = me % 2
-        for j in range(keep_ref.shape[0]):
+        per_tile = tile_rows // rows_here // 2
+        for j in range(per_tile):
             own = pl.ds(pl.multiple_of((2 * j + bit) * block, 8), block)
             other = pl.ds(pl.multiple_of((2 * j + 1 - bit) * block, 8), block)
             for c in tiles:
-                keep_ref[j, :, c * LANES : (c + 1) * LANES] = sums_ref[c, own, :]
-            pack([sums_ref[c, other, :] for c in tiles], msg_ref, j)
+                keep_ref[row_tile * per_tile + j, :, c * LANES : (c + 1) * LANES] = sums_ref[c, own, :]
+            pack([sums_ref[c, other, :] for c in tiles], msg_ref, row_tile * per_tile + j)
+        return carry
+
+    lax.fori_loop(0, steps // lane_tiles, row_tile_sums, 0)
 
 
 def partial_sums(me, reflect, clear_conf, sun_view, sensor_id, band_gain, sensor_weight, prior, scale, chunk):
@@ -196,36 +234,28 @@
     rows_here = prior.shape[1]
     count = rows // rows_here
     tile_rows = 16
-    width = min(256, cols)
-    first = chunk * (cols // width)
     block = rows_here * ENTRIES
-    per_tile = tile_rows // rows_here // 2
-    places = 1 + block // 16 * (cols // LANES)
+    lane_tiles = cols // LANES
+    steps = rows // tile_rows * lane_tiles
     smem = pl.BlockSpec(memory_space=pltpu.SMEM)
+    vmem = pl.BlockSpec(memory_space=pltpu.VMEM)
+    hbm = pl.BlockSpec(memory_space=pl.ANY)
     return pl.pallas_call(
-        functools.partial(sums_kernel, scale=scale, rows_here=rows_here),
-        grid=(rows // tile_rows, cols // width),
-        in_specs=[
-            smem,
-            smem,
-            smem,
-            smem,
-            pl.BlockSpec((dates, bands, tile_rows, width), lambda i, j: (0, 0, i, first + j)),
-            pl.BlockSpec((dates, tile_rows, width), lambda i, j: (0, i, first + j)),
-            pl.BlockSpec((dates, 3, tile_rows, width), lambda i, j: (0, 0, i, first + j)),
-            pl.BlockSpec((3 * bands, rows_here, cols), lambda i, j: (0, 0, chunk)),
-        ],
-        out_specs=[
-            pl.BlockSpec((per_tile, block, cols), lambda i, j: (i, 0, 0)),
-            pl.BlockSpec((per_tile, places, 16, LANES), lambda i, j: (i, 0, 0, 0)),
-        ],
+        functools.partial(sums_kernel, scale=scale, rows_here=rows_here, first_col=chunk * cols),
+        grid=(1,),
+        in_specs=[smem] * 4 + [hbm] * 3 + [pl.BlockSpec((3 * bands, rows_here, cols), lambda i: (0, 0, chunk))],
+        out_specs=[vmem, vmem],
         out_shape=[
             jax.ShapeDtypeStruct((count // 2, block, cols), jnp.float32),
-            jax.ShapeDtypeStruct((count // 2, places, 16, LANES), jnp.int16),
+            jax.ShapeDtypeStruct((count // 2, 1 + block // 16 * lane_tiles, 16, LANES), jnp.int16),
         ],
         scratch_shapes=[
-            pltpu.VMEM((cols // LANES, tile_rows * ENTRIES, LANES), jnp.float32),
+            pltpu.VMEM((lane_tiles, tile_rows * ENTRIES, LANES), jnp.float32),
             pltpu.VMEM((dates, 3, tile_rows, LANES), jnp.float32),
+            pltpu.VMEM((steps, dates, bands, tile_rows, LANES), reflect.dtype),
+            pltpu.VMEM((steps, dates, tile_rows, LANES), jnp.int32),
+            pltpu.VMEM((steps, dates, 3, tile_rows, LANES), jnp.int32),
+            pltpu.SemaphoreType.DMA((steps, 3)),
         ],
         compiler_params=pltpu.CompilerParams(vmem_limit_bytes=(62 if chunk == 0 else 52) * 2**20),
         name="partial_sums",

time: 59 us -> 58.9 us (level)
  no operation moved by 1% of the time
where the time goes in v1:
time: 58.9 us; the launch traced here: 58.8 us
  starting transfers between devices  22.7 us (39%)
  waiting for transfers between devices  18.6 us (32%)
  Pallas kernels  17.2 us (29%)
    ppermute x14, starting transfers between devices, on_device(): lax.ppermute(x, 'rows', [(i, i ^ mask) for i in range(count)])  20.8 us
    ppermute x14, waiting for transfers between devices, on_device(): lax.ppermute(x, 'rows', [(i, i ^ mask) for i in range(count)])  15.9 us
    pallas_call x2, Pallas kernels, partial_sums(): pl.pallas_call(functools.partial(sums_kernel, scale=scale, rows_here=rows...  11.7 us
    ppermute x1, waiting for transfers between devices, on_device(): far = lax.ppermute(first, 'rows', [(i + 2, i) for i in range(count - 2)])  2.74 us
    pallas_call x5, Pallas kernels, add_split(): pl.pallas_call(functools.partial(add_split_kernel, place=place), in_specs...  1.91 us
    pallas_call x1, Pallas kernels, on_device(): pl.pallas_call(functools.partial(krylov_kernel, total_rows=total_rows, ro...  1.82 us
    ppermute x1, starting transfers between devices, on_device(): far = lax.ppermute(first, 'rows', [(i + 2, i) for i in range(count - 2)])  1.28 us
  transfers between devices with their start and end apart: 16, of which 9 were waited for; matrix products, arithmetic and copies ran while one was open for 0% of the time, Pallas kernels for 15%

profile of v1, /device:TPU:0, one launch (start us, length us, event | category | flops | bytes accessed | tf_op | source)
XLA Modules:
  0.0 58.8 jit_solution(7251429676690439376)
XLA Ops:
  0.0 6.4 %partial_sums.2 = (f32[8,48,512]{2,1,0:T(8,128)}, s16[8,13,16,128]{3,2,1,0:T(8,128)(2,1)}) custom-call(s32[1]{0:T(128)} %bitcast.me_ref, s32[128]{0:T(128)} %ids_ref.3, f32[4,6]{1,0:T(4,128)} %gain_ref.3, f32[4]{0:T(128)} %weight_ref.3, bf16[8,6,32,1024]{3,2,1,0:T(8,128)(2,1)} %reflect_hbm.3, s32[8,32,1024]{2,1,0:T(8,128)} %conf_hbm.3, ...), custom_call_target="tpu_custom_call" | custom-call | tf_op jit(solution)/shard_map/partial_sums/pallas_call | solution.py:243
  7.0 5.2 %partial_sums.3 = (f32[8,48,512]{2,1,0:T(8,128)S(1)}, s16[8,13,16,128]{3,2,1,0:T(8,128)(2,1)S(1)}) custom-call(s32[1]{0:T(128)} %bitcast.me_ref, s32[128]{0:T(128)S(1)} %copy-done.3, f32[4,6]{1,0:T(4,128)S(1)} %copy-done.2, f32[4]{0:T(128)S(1)} %copy-done.4, bf16[8,6,32,1024]{3,2,1,0:T(8,128)(2,1)} %reflect_hbm.3, s32[8,32,1024]{2,1,0:T(8,128)} %conf_hbm.3, ...), custom_call_target="tpu_custom_call" | custom-call | tf_op jit(solution)/shard_map/partial_sums/pallas_call | solution.py:243
  12.8 3.0 %collective-permute-start.1 = (s16[4,13,16,128]{3,2,1,0:T(8,128)(2,1)S(1)}, s16[4,13,16,128]{3,2,1,0:T(8,128)(2,1)S(1)}, u32[]{:S(2)}, u32[]{:S(2)}) collective-permute-start(s16[4,13,16,128]{3,2,1,0:T(8,128)(2,1)S(1)} %get-tuple-element.30), channel_id=1, source_target_pairs={{0,2},{1,3},{2,0},{3,1},{4,6},{5,7},{6,4},{7,5},{8,10},{9,11},{10,... | collective-permute-start | bytes 638984 | tf_op jit(solution)/shard_map/ppermute | solution.py:521
  16.3 1.6 %collective-permute-start.4 = (s16[4,13,16,128]{3,2,1,0:T(8,128)(2,1)S(1)}, s16[4,13,16,128]{3,2,1,0:T(8,128)(2,1)S(1)}, u32[]{:S(2)}, u32[]{:S(2)}) collective-permute-start(s16[4,13,16,128]{3,2,1,0:T(8,128)(2,1)S(1)} %get-tuple-element.37), channel_id=1, source_target_pairs={{0,4},{1,5},{2,6},{3,7},{4,0},{5,1},{6,2},{7,3},{8,12},{9,13},{10,... | collective-permute-start | bytes 638984 | tf_op jit(solution)/shard_map/ppermute | solution.py:521
  17.9 3.4 %collective-permute-done.1.refs_1_ = s16[4,13,16,128]{3,2,1,0:T(8,128)(2,1)S(1)} collective-permute-done((s16[4,13,16,128]{3,2,1,0:T(8,128)(2,1)S(1)}, s16[4,13,16,128]{3,2,1,0:T(8,128)(2,1)S(1)}, u32[]{:S(2)}, u32[]{:S(2)}) %collective-permute-start.1) | collective-permute-done | bytes 213024 | tf_op jit(solution)/shard_map/ppermute | solution.py:521
  21.7 1.9 %collective-permute-start.2 = (s16[2,13,16,128]{3,2,1,0:T(8,128)(2,1)S(1)}, s16[2,13,16,128]{3,2,1,0:T(8,128)(2,1)S(1)}, u32[]{:S(2)}, u32[]{:S(2)}) collective-permute-start(s16[2,13,16,128]{3,2,1,0:T(8,128)(2,1)S(1)} %get-tuple-element.32), channel_id=1, source_target_pairs={{0,4},{1,5},{2,6},{3,7},{4,0},{5,1},{6,2},{7,3},{8,12},{9,13},{10,... | collective-permute-start | bytes 319496 | tf_op jit(solution)/shard_map/ppermute | solution.py:521
  23.9 1.6 %collective-permute-start.5 = (s16[2,13,16,128]{3,2,1,0:T(8,128)(2,1)S(1)}, s16[2,13,16,128]{3,2,1,0:T(8,128)(2,1)S(1)}, u32[]{:S(2)}, u32[]{:S(2)}) collective-permute-start(s16[2,13,16,128]{3,2,1,0:T(8,128)(2,1)S(1)} %get-tuple-element.39), channel_id=1, source_target_pairs={{0,2},{1,3},{2,0},{3,1},{4,6},{5,7},{6,4},{7,5},{8,10},{9,11},{10,... | collective-permute-start | bytes 319496 | tf_op jit(solution)/shard_map/ppermute | solution.py:521
  25.5 0.9 %collective-permute-done.2.refs_1_ = s16[2,13,16,128]{3,2,1,0:T(8,128)(2,1)S(1)} collective-permute-done((s16[2,13,16,128]{3,2,1,0:T(8,128)(2,1)S(1)}, s16[2,13,16,128]{3,2,1,0:T(8,128)(2,1)S(1)}, u32[]{:S(2)}, u32[]{:S(2)}) %collective-permute-start.2) | collective-permute-done | bytes 106528 | tf_op jit(solution)/shard_map/ppermute | solution.py:521
  26.5 2.2 %collective-permute-done.5.refs_3_ = s16[2,13,16,128]{3,2,1,0:T(8,128)(2,1)S(1)} collective-permute-done((s16[2,13,16,128]{3,2,1,0:T(8,128)(2,1)S(1)}, s16[2,13,16,128]{3,2,1,0:T(8,128)(2,1)S(1)}, u32[]{:S(2)}, u32[]{:S(2)}) %collective-permute-start.5) | collective-permute-done | bytes 106528 | tf_op jit(solution)/shard_map/ppermute | solution.py:521
  29.1 2.7 %collective-permute-start.6 = (s16[1,25,16,128]{3,2,1,0:T(8,128)(2,1)S(1)}, s16[1,25,16,128]{3,2,1,0:T(8,128)(2,1)S(1)}, u32[]{:S(2)}, u32[]{:S(2)}) collective-permute-start(s16[1,25,16,128]{3,2,1,0:T(8,128)(2,1)S(1)} %get-tuple-element.41), channel_id=1, source_target_pairs={{0,8},{1,9},{2,10},{3,11},{4,12},{5,13},{6,14},{7,15},{8,0},{9,1},... | collective-permute-start | bytes 307208 | tf_op jit(solution)/shard_map/ppermute | solution.py:521
  31.7 4.1 %collective-permute-done.6.refs_1_ = s16[1,25,16,128]{3,2,1,0:T(8,128)(2,1)S(1)} collective-permute-done((s16[1,25,16,128]{3,2,1,0:T(8,128)(2,1)S(1)}, s16[1,25,16,128]{3,2,1,0:T(8,128)(2,1)S(1)}, u32[]{:S(2)}, u32[]{:S(2)}) %collective-permute-start.6) | collective-permute-done | bytes 102432 | tf_op jit(solution)/shard_map/ppermute | solution.py:521
  35.8 0.7 %residual.1 = (f32[48,1024]{1,0:T(8,128)S(1)}, s16[1,25,16,128]{3,2,1,0:T(8,128)(2,1)S(1)}, s16[10,16,128]{2,1,0:T(8,128)(2,1)S(1)}) custom-call(s32[1]{0:T(128)} %bitcast.me_ref, f32[18,2,1024]{2,1,0:T(2,128)S(1)} %bitcast.6, f32[1,48,1024]{2,1,0:T(8,128)S(1)} %get-tuple-element.40.refs_0_, s16[1,25,16,128]{3,2,1,0:T(8,128)(2,1)S(1)} %collective-permute-done.6.refs_1_), custom_call_target="tpu_custom_call" | custom-call | tf_op jit(solution)/shard_map/residual/pallas_call | solution.py:538
  36.5 0.7 %collective-permute-start.8 = (s16[25,16,128]{2,1,0:T(8,128)(2,1)S(1)}, s16[25,16,128]{2,1,0:T(8,128)(2,1)S(1)}, u32[]{:S(2)}, u32[]{:S(2)}) collective-permute-start(s16[25,16,128]{2,1,0:T(8,128)(2,1)S(1)} %bitcast.8), channel_id=1, source_target_pairs={{1,2},{3,4},{5,6},{7,8},{9,10},{11,12},{13,14},{2,1},{4,3},{6,5},{... | collective-permute-start | bytes 307208 | tf_op jit(solution)/shard_map/ppermute | solution.py:551
  37.2 2.9 %collective-permute-start.7 = (s16[25,16,128]{2,1,0:T(8,128)(2,1)S(1)}, s16[25,16,128]{2,1,0:T(8,128)(2,1)S(1)}, u32[]{:S(2)}, u32[]{:S(2)}) collective-permute-start(s16[25,16,128]{2,1,0:T(8,128)(2,1)S(1)} %bitcast.9), channel_id=1, source_target_pairs={{0,1},{1,0},{2,3},{3,2},{4,5},{5,4},{6,7},{7,6},{8,9},{9,8},{10,11... | collective-permute-start | bytes 307208 | tf_op jit(solution)/shard_map/ppermute | solution.py:521
  40.2 1.3 %collective-permute-start.9 = (s16[10,16,128]{2,1,0:T(8,128)(2,1)S(1)}, s16[10,16,128]{2,1,0:T(8,128)(2,1)S(1)}, u32[]{:S(2)}, u32[]{:S(2)}) collective-permute-start(s16[10,16,128]{2,1,0:T(8,128)(2,1)S(1)} %get-tuple-element.46), channel_id=1, source_target_pairs={{2,0},{3,1},{4,2},{5,3},{6,4},{7,5},{8,6},{9,7},{10,8},{11,9},{12,... | collective-permute-start | bytes 122888 | tf_op jit(solution)/shard_map/ppermute | solution.py:552
  41.5 1.8 %krylov.1 = (f32[18,2,1024]{2,1,0:T(2,128)S(1)}, f32[18,2,1024]{2,1,0:T(2,128)S(1)}, f32[18,2,1024]{2,1,0:T(2,128)S(1)}, f32[8,128]{1,0:T(8,128)S(1)}) custom-call(s32[1]{0:T(128)} %bitcast.me_ref, f32[48,1024]{1,0:T(8,128)S(1)} %get-tuple-element.42.own_ref, s16[25,16,128]{2,1,0:T(8,128)(2,1)S(1)} %collective-permute-done.7.mate_ref, ...), custom_call_target="tpu_custom_call" | custom-call | tf_op jit(solution)/shard_map/krylov/pallas_call | solution.py:553
  43.3 2.7 %collective-permute-done.9.far_ref = s16[10,16,128]{2,1,0:T(8,128)(2,1)S(1)} collective-permute-done((s16[10,16,128]{2,1,0:T(8,128)(2,1)S(1)}, s16[10,16,128]{2,1,0:T(8,128)(2,1)S(1)}, u32[]{:S(2)}, u32[]{:S(2)}) %collective-permute-start.9) | collective-permute-done | bytes 40992 | tf_op jit(solution)/shard_map/ppermute | solution.py:552
  46.4 1.4 %collective-permute-start.11 = (f32[8,128]{1,0:T(8,128)S(1)}, f32[8,128]{1,0:T(8,128)S(1)}, u32[]{:S(2)}, u32[]{:S(2)}) collective-permute-start(f32[8,128]{1,0:T(8,128)S(1)} %far.1), channel_id=1, source_target_pairs={{0,2},{1,3},{2,0},{3,1},{4,6},{5,7},{6,4},{7,5},{8,10},{9,11},{10,... | collective-permute-start | bytes 12296 | tf_op jit(solution)/shard_map/ppermute | solution.py:521
  48.3 1.2 %collective-permute-done.12 = f32[8,128]{1,0:T(8,128)S(1)} collective-permute-done((f32[8,128]{1,0:T(8,128)S(1)}, f32[8,128]{1,0:T(8,128)S(1)}, u32[]{:S(2)}, u32[]{:S(2)}) %collective-permute-start.12) | collective-permute-done | bytes 4128 | tf_op jit(solution)/shard_map/ppermute | solution.py:521
  50.1 3.3 %collective-permute-start.15 = (f32[8,128]{1,0:T(8,128)S(1)}, f32[8,128]{1,0:T(8,128)S(1)}, u32[]{:S(2)}, u32[]{:S(2)}) collective-permute-start(f32[8,128]{1,0:T(8,128)S(1)} %add_add_fusion.refs_0_), channel_id=1, source_target_pairs={{0,12},{1,13},{2,14},{3,15},{4,8},{5,9},{6,10},{7,11},{8,4},{9,5},... | collective-permute-start | bytes 12296 | tf_op jit(solution)/shard_map/ppermute | solution.py:521
  53.4 1.1 %collective-permute-start.13 = (f32[8,128]{1,0:T(8,128)S(1)}, f32[8,128]{1,0:T(8,128)S(1)}, u32[]{:S(2)}, u32[]{:S(2)}) collective-permute-start(f32[8,128]{1,0:T(8,128)S(1)} %add_add_fusion.refs_0_), channel_id=1, source_target_pairs={{0,4},{1,5},{2,6},{3,7},{4,0},{5,1},{6,2},{7,3},{8,12},{9,13},{10,... | collective-permute-start | bytes 12296 | tf_op jit(solution)/shard_map/ppermute | solution.py:521
  54.5 1.0 %collective-permute-done.15.refs_3_ = f32[8,128]{1,0:T(8,128)S(1)} collective-permute-done((f32[8,128]{1,0:T(8,128)S(1)}, f32[8,128]{1,0:T(8,128)S(1)}, u32[]{:S(2)}, u32[]{:S(2)}) %collective-permute-start.15) | collective-permute-done | bytes 4128 | tf_op jit(solution)/shard_map/ppermute | solution.py:521
  55.6 2.4 %collective-permute-done.14.refs_2_ = f32[8,128]{1,0:T(8,128)S(1)} collective-permute-done((f32[8,128]{1,0:T(8,128)S(1)}, f32[8,128]{1,0:T(8,128)S(1)}, u32[]{:S(2)}, u32[]{:S(2)}) %collective-permute-start.14) | collective-permute-done | bytes 4128 | tf_op jit(solution)/shard_map/ppermute | solution.py:521
  57.9 0.9 %combine.1 = f32[18,2,1024]{2,1,0:T(2,128)} custom-call(f32[8,128]{1,0:T(8,128)S(1)} %add_add_fusion.refs_0_, f32[8,128]{1,0:T(8,128)S(1)} %collective-permute-done.13.refs_1_, f32[8,128]{1,0:T(8,128)S(1)} %collective-permute-done.14.refs_2_, f32[8,128]{1,0:T(8,128)S(1)} %collective-permute-done.15.refs_3_, f32[18,2,1024]{2,1,0:T(2,128)S(1)} %bitcast.7, ...), custom_call_target="tpu_custom_call" | custom-call | tf_op jit(solution)/shard_map/combine/pallas_call | solution.py:572
  (30 shorter events, 4.1 us)
Async XLA Ops:
  0.0 7.0 %copy-start = (f32[2,18,1024]{2,0,1:T(2,128)S(1)}, f32[2,18,1024]{2,0,1:T(2,128)}, u32[]{:S(2)}) copy-start(f32[2,18,1024]{2,0,1:T(2,128)} %param.13) | copy-start | bytes 442372
  0.0 7.0 %copy-start.2 = (f32[4,6]{1,0:T(4,128)S(1)}, f32[4,6]{1,0:T(4,128)}, u32[]{:S(2)}) copy-start(f32[4,6]{1,0:T(4,128)} %gain_ref.3) | copy-start | bytes 292
  0.0 7.0 %copy-start.3 = (s32[128]{0:T(128)S(1)}, s32[128]{0:T(128)}, u32[]{:S(2)}) copy-start(s32[128]{0:T(128)} %ids_ref.3) | copy-start | bytes 1540
  0.0 7.0 %copy-start.4 = (f32[4]{0:T(128)S(1)}, f32[4]{0:T(128)}, u32[]{:S(2)}) copy-start(f32[4]{0:T(128)} %weight_ref.3) | copy-start | bytes 52
  6.4 5.9 %copy-start.1 = (f32[8,48,512]{2,1,0:T(8,128)S(1)}, f32[8,48,512]{2,1,0:T(8,128)}, u32[]{:S(2)}) copy-start(f32[8,48,512]{2,1,0:T(8,128)} %get-tuple-element.27.refs_0_) | copy-start | bytes 2359300
  6.5 5.9 %collective-permute-start = (s16[8,13,16,128]{3,2,1,0:T(8,128)(2,1)}, s16[8,13,16,128]{3,2,1,0:T(8,128)(2,1)S(1)}, u32[]{:S(2)}, u32[]{:S(2)}) collective-permute-start(s16[8,13,16,128]{3,2,1,0:T(8,128)(2,1)} %get-tuple-element.28), channel_id=1, source_target_pairs={{0,1},{1,0},{2,3},{3,2},{4,5},{5,4},{6,7},{7,6},{8,9},{9,8},{10,11... | collective-permute-start | bytes 1277960 | tf_op jit(solution)/shard_map/ppermute | solution.py:521
  12.2 3.6 %collective-permute-start.3 = (s16[8,13,16,128]{3,2,1,0:T(8,128)(2,1)S(1)}, s16[8,13,16,128]{3,2,1,0:T(8,128)(2,1)S(1)}, u32[]{:S(2)}, u32[]{:S(2)}) collective-permute-start(s16[8,13,16,128]{3,2,1,0:T(8,128)(2,1)S(1)} %get-tuple-element.35), channel_id=1, source_target_pairs={{0,1},{1,0},{2,3},{3,2},{4,5},{5,4},{6,7},{7,6},{8,9},{9,8},{10,11... | collective-permute-start | bytes 1277960 | tf_op jit(solution)/shard_map/ppermute | solution.py:521
  12.8 8.5 %collective-permute-start.1 = (s16[4,13,16,128]{3,2,1,0:T(8,128)(2,1)S(1)}, s16[4,13,16,128]{3,2,1,0:T(8,128)(2,1)S(1)}, u32[]{:S(2)}, u32[]{:S(2)}) collective-permute-start(s16[4,13,16,128]{3,2,1,0:T(8,128)(2,1)S(1)} %get-tuple-element.30), channel_id=1, source_target_pairs={{0,2},{1,3},{2,0},{3,1},{4,6},{5,7},{6,4},{7,5},{8,10},{9,11},{10,... | collective-permute-start | bytes 638984 | tf_op jit(solution)/shard_map/ppermute | solution.py:521
  16.3 7.3 %collective-permute-start.4 = (s16[4,13,16,128]{3,2,1,0:T(8,128)(2,1)S(1)}, s16[4,13,16,128]{3,2,1,0:T(8,128)(2,1)S(1)}, u32[]{:S(2)}, u32[]{:S(2)}) collective-permute-start(s16[4,13,16,128]{3,2,1,0:T(8,128)(2,1)S(1)} %get-tuple-element.37), channel_id=1, source_target_pairs={{0,4},{1,5},{2,6},{3,7},{4,0},{5,1},{6,2},{7,3},{8,12},{9,13},{10,... | collective-permute-start | bytes 638984 | tf_op jit(solution)/shard_map/ppermute | solution.py:521
  21.7 4.8 %collective-permute-start.2 = (s16[2,13,16,128]{3,2,1,0:T(8,128)(2,1)S(1)}, s16[2,13,16,128]{3,2,1,0:T(8,128)(2,1)S(1)}, u32[]{:S(2)}, u32[]{:S(2)}) collective-permute-start(s16[2,13,16,128]{3,2,1,0:T(8,128)(2,1)S(1)} %get-tuple-element.32), channel_id=1, source_target_pairs={{0,4},{1,5},{2,6},{3,7},{4,0},{5,1},{6,2},{7,3},{8,12},{9,13},{10,... | collective-permute-start | bytes 319496 | tf_op jit(solution)/shard_map/ppermute | solution.py:521
  23.9 4.8 %collective-permute-start.5 = (s16[2,13,16,128]{3,2,1,0:T(8,128)(2,1)S(1)}, s16[2,13,16,128]{3,2,1,0:T(8,128)(2,1)S(1)}, u32[]{:S(2)}, u32[]{:S(2)}) collective-permute-start(s16[2,13,16,128]{3,2,1,0:T(8,128)(2,1)S(1)} %get-tuple-element.39), channel_id=1, source_target_pairs={{0,2},{1,3},{2,0},{3,1},{4,6},{5,7},{6,4},{7,5},{8,10},{9,11},{10,... | collective-permute-start | bytes 319496 | tf_op jit(solution)/shard_map/ppermute | solution.py:521
  29.1 6.7 %collective-permute-start.6 = (s16[1,25,16,128]{3,2,1,0:T(8,128)(2,1)S(1)}, s16[1,25,16,128]{3,2,1,0:T(8,128)(2,1)S(1)}, u32[]{:S(2)}, u32[]{:S(2)}) collective-permute-start(s16[1,25,16,128]{3,2,1,0:T(8,128)(2,1)S(1)} %get-tuple-element.41), channel_id=1, source_target_pairs={{0,8},{1,9},{2,10},{3,11},{4,12},{5,13},{6,14},{7,15},{8,0},{9,1},... | collective-permute-start | bytes 307208 | tf_op jit(solution)/shard_map/ppermute | solution.py:521
  36.5 4.9 %collective-permute-start.8 = (s16[25,16,128]{2,1,0:T(8,128)(2,1)S(1)}, s16[25,16,128]{2,1,0:T(8,128)(2,1)S(1)}, u32[]{:S(2)}, u32[]{:S(2)}) collective-permute-start(s16[25,16,128]{2,1,0:T(8,128)(2,1)S(1)} %bitcast.8), channel_id=1, source_target_pairs={{1,2},{3,4},{5,6},{7,8},{9,10},{11,12},{13,14},{2,1},{4,3},{6,5},{... | collective-permute-start | bytes 307208 | tf_op jit(solution)/shard_map/ppermute | solution.py:551
  37.2 4.2 %collective-permute-start.7 = (s16[25,16,128]{2,1,0:T(8,128)(2,1)S(1)}, s16[25,16,128]{2,1,0:T(8,128)(2,1)S(1)}, u32[]{:S(2)}, u32[]{:S(2)}) collective-permute-start(s16[25,16,128]{2,1,0:T(8,128)(2,1)S(1)} %bitcast.9), channel_id=1, source_target_pairs={{0,1},{1,0},{2,3},{3,2},{4,5},{5,4},{6,7},{7,6},{8,9},{9,8},{10,11... | collective-permute-start | bytes 307208 | tf_op jit(solution)/shard_map/ppermute | solution.py:521
  40.2 5.9 %collective-permute-start.9 = (s16[10,16,128]{2,1,0:T(8,128)(2,1)S(1)}, s16[10,16,128]{2,1,0:T(8,128)(2,1)S(1)}, u32[]{:S(2)}, u32[]{:S(2)}) collective-permute-start(s16[10,16,128]{2,1,0:T(8,128)(2,1)S(1)} %get-tuple-element.46), channel_id=1, source_target_pairs={{2,0},{3,1},{4,2},{5,3},{6,4},{7,5},{8,6},{9,7},{10,8},{11,9},{12,... | collective-permute-start | bytes 122888 | tf_op jit(solution)/shard_map/ppermute | solution.py:552
  46.3 3.1 %collective-permute-start.12 = (f32[8,128]{1,0:T(8,128)S(1)}, f32[8,128]{1,0:T(8,128)S(1)}, u32[]{:S(2)}, u32[]{:S(2)}) collective-permute-start(f32[8,128]{1,0:T(8,128)S(1)} %far.1), channel_id=1, source_target_pairs={{0,3},{1,2},{2,1},{3,0},{4,7},{5,6},{6,5},{7,4},{8,11},{9,10},{10,... | collective-permute-start | bytes 12296 | tf_op jit(solution)/shard_map/ppermute | solution.py:521
  46.4 3.7 %collective-permute-start.11 = (f32[8,128]{1,0:T(8,128)S(1)}, f32[8,128]{1,0:T(8,128)S(1)}, u32[]{:S(2)}, u32[]{:S(2)}) collective-permute-start(f32[8,128]{1,0:T(8,128)S(1)} %far.1), channel_id=1, source_target_pairs={{0,2},{1,3},{2,0},{3,1},{4,6},{5,7},{6,4},{7,5},{8,10},{9,11},{10,... | collective-permute-start | bytes 12296 | tf_op jit(solution)/shard_map/ppermute | solution.py:521
  47.8 2.3 %collective-permute-start.10 = (f32[8,128]{1,0:T(8,128)S(1)}, f32[8,128]{1,0:T(8,128)S(1)}, u32[]{:S(2)}, u32[]{:S(2)}) collective-permute-start(f32[8,128]{1,0:T(8,128)S(1)} %far.1), channel_id=1, source_target_pairs={{0,1},{1,0},{2,3},{3,2},{4,5},{5,4},{6,7},{7,6},{8,9},{9,8},{10,11... | collective-permute-start | bytes 12296 | tf_op jit(solution)/shard_map/ppermute | solution.py:521
  50.1 5.5 %collective-permute-start.15 = (f32[8,128]{1,0:T(8,128)S(1)}, f32[8,128]{1,0:T(8,128)S(1)}, u32[]{:S(2)}, u32[]{:S(2)}) collective-permute-start(f32[8,128]{1,0:T(8,128)S(1)} %add_add_fusion.refs_0_), channel_id=1, source_target_pairs={{0,12},{1,13},{2,14},{3,15},{4,8},{5,9},{6,10},{7,11},{8,4},{9,5},... | collective-permute-start | bytes 12296 | tf_op jit(solution)/shard_map/ppermute | solution.py:521
  53.4 4.5 %collective-permute-start.14 = (f32[8,128]{1,0:T(8,128)S(1)}, f32[8,128]{1,0:T(8,128)S(1)}, u32[]{:S(2)}, u32[]{:S(2)}) collective-permute-start(f32[8,128]{1,0:T(8,128)S(1)} %add_add_fusion.refs_0_), channel_id=1, source_target_pairs={{0,8},{1,9},{2,10},{3,11},{4,12},{5,13},{6,14},{7,15},{8,0},{9,1},... | collective-permute-start | bytes 12296 | tf_op jit(solution)/shard_map/ppermute | solution.py:521
  53.4 4.5 %collective-permute-start.13 = (f32[8,128]{1,0:T(8,128)S(1)}, f32[8,128]{1,0:T(8,128)S(1)}, u32[]{:S(2)}, u32[]{:S(2)}) collective-permute-start(f32[8,128]{1,0:T(8,128)S(1)} %add_add_fusion.refs_0_), channel_id=1, source_target_pairs={{0,4},{1,5},{2,6},{3,7},{4,0},{5,1},{6,2},{7,3},{8,12},{9,13},{10,... | collective-permute-start | bytes 12296 | tf_op jit(solution)/shard_map/ppermute | solution.py:521

commit v2 on v1

--- a/solution.py
+++ b/solution.py
@@ -17,6 +17,7 @@
 LANES = 128
 QUANT = 32000.0
 GROUP = LANES // 4
+FIRST_ORDER = [4 * (2 * m + h) + j for m in range(3) for j in range(4) for h in range(2)]
 CHUNKS = 2
 
 
@@ -121,6 +122,17 @@
     ]
 
 
+def part_rows(tiles):
+    sublane = lax.broadcasted_iota(jnp.int32, (8, LANES), 0)
+    odd, upper = sublane // 2 % 2 == 1, sublane >= 4
+    pairs = []
+    for first, second in (tiles[0:2], tiles[2:4]):
+        pairs.append((jnp.where(odd, pltpu.roll(second, 2, axis=0), first), jnp.where(odd, second, pltpu.roll(first, 6, axis=0))))
+    low = [jnp.where(upper, pltpu.roll(pairs[1][core], 4, axis=0), pairs[0][core]) for core in range(2)]
+    high = [jnp.where(upper, pairs[1][core], pltpu.roll(pairs[0][core], 4, axis=0)) for core in range(2)]
+    return low + high
+
+
 def sums_kernel(
     me_ref,
     ids_ref,
@@ -171,13 +183,12 @@
             copy.wait()
         sensors = [ids_ref[me * dates + d] for d in range(dates)]
 
-        def store(top, entry, total):
-            sums_ref[index, pl.ds(top * ENTRIES + entry, 8, stride=ENTRIES), :] = total
-
         def plus(total, term):
             return term if total is None else total + term
 
-        for top in range(0, tile_rows, 8):
+        tops = range(0, tile_rows, 8)
+        normals = []
+        for top in tops:
             here = slice(top, top + 8)
             normal = [None] * 6
             for d in range(dates):
@@ -189,16 +200,23 @@
                     kernels_ref[d, i, here, :] = value
                 terms = (weight, weighted_vol, weighted_geo, weighted_vol * volume, weighted_vol * geometric, weighted_geo * geometric)
                 normal = [plus(total, term) for total, term in zip(normal, terms)]
-            for k in range(6):
-                store(top, obs_count + k, normal[k])
-        for b in range(bands):
-            observed = [None] * 3
-            for d in range(dates):
-                signal = reflect_ref[step, d, b].astype(jnp.float32) * gain_ref[sensors[d], b]
-                observed = [plus(total, kernels_ref[d, i] * signal) for i, total in enumerate(observed)]
-            for i in range(3):
-                for top in range(0, tile_rows, 8):
-                    store(top, 3 * b + i, observed[i][top : top + 8])
+            normals.append(normal)
+        waiting = [[] for _ in tops]
+        done = 0
+        for b in range(bands + 1):
+            if b < bands:
+                observed = [None] * 3
+                for d in range(dates):
+                    signal = reflect_ref[step, d, b].astype(jnp.float32) * gain_ref[sensors[d], b]
+                    observed = [plus(total, kernels_ref[d, i] * signal) for i, total in enumerate(observed)]
+            for at, top in enumerate(tops):
+                waiting[at] += [total[top : top + 8] for total in observed] if b < bands else normals[at]
+            while len(waiting[0]) >= 4:
+                for at, top in enumerate(tops):
+                    for unit, rows in enumerate(part_rows(waiting[at][:4])):
+                        sums_ref[index, pl.ds((top // 2 + unit) * block + done * 2, 8), :] = rows
+                    waiting[at] = waiting[at][4:]
+                done += 4
         return row_tile
 
     def row_tile_sums(row_tile, carry):
@@ -209,11 +227,15 @@
 
             @pl.when((row >= 0) & (row < tile_rows))
             def _():
+                at = pl.ds(pl.multiple_of(row // rows_here * block, 8), obs_count * rows_here)
+                target = rows_here - 1 - source
+                zero = jnp.zeros((1, LANES), jnp.float32)
                 for c in tiles:
                     lanes = slice(c * LANES, (c + 1) * LANES)
-                    at = pl.ds(pl.multiple_of(row * ENTRIES, 8), obs_count)
-                    part = jnp.concatenate([prior_ref[e, source : source + 1, lanes] for e in range(obs_count)], axis=0)
-                    sums_ref[c, at, :] = sums_ref[c, at, :] + SMOOTH_PULL * part
+                    part = []
+                    for e in range(obs_count):
+                        part += [prior_ref[e, source : source + 1, lanes] if r == target else zero for r in range(rows_here)]
+                    sums_ref[c, at, :] = sums_ref[c, at, :] + SMOOTH_PULL * jnp.concatenate(part, axis=0)
 
         bit = me % 2
         per_tile = tile_rows // rows_here // 2
@@ -300,15 +322,13 @@
     )(bit, *parts)
 
 
-def take(ref, start, size, stride):
-    at = pl.ds(start, size, stride=stride)
-    return jnp.concatenate([ref[c, at, :] for c in range(ref.shape[0])], axis=1)
-
-
-def put(ref, start, size, stride, value):
-    at = pl.ds(start, size, stride=stride)
+def take(ref, entry, rows):
+    return jnp.concatenate([ref[c, entry * rows : (entry + 1) * rows, :] for c in range(ref.shape[0])], axis=1)
+
+
+def put(ref, entry, rows, value):
     for c in range(ref.shape[0]):
-        ref[c, at, :] = value[:, c * LANES : (c + 1) * LANES]
+        ref[c, entry * rows : (entry + 1) * rows, :] = value[:, c * LANES : (c + 1) * LANES]
 
 
 def beside_columns(x):
@@ -353,7 +373,7 @@
     shape = (rows_here, cols)
     row = me_ref[0] * rows_here + lax.broadcasted_iota(jnp.int32, shape, 0)
     degree = degree_of(row, shape, total_rows)
-    normal = [take(sums_ref, obs_count + k, rows_here, ENTRIES) for k in range(6)]
+    normal = [take(sums_ref, obs_count + k, rows_here) for k in range(6)]
     for b in range(obs_count // 3):
         fields = [prior_ref[3 * b + i] for i in range(3)]
         coupled = couple(normal, fields)
@@ -364,20 +384,25 @@
                 zero = jnp.zeros((1, cols), jnp.float32)
                 beside = beside + jnp.concatenate([zero, field[:-1]], axis=0) + jnp.concatenate([field[1:], zero], axis=0)
             entry = 3 * b + i
-            observed = take(sums_ref, entry, rows_here, ENTRIES)
-            put(sums_ref, entry, rows_here, ENTRIES, observed - coupled[i] - SMOOTH_PULL * (degree * field - beside))
+            observed = take(sums_ref, entry, rows_here)
+            put(sums_ref, entry, rows_here, observed - coupled[i] - SMOOTH_PULL * (degree * field - beside))
     for c in range(tiles):
         out_ref[:, c * LANES : (c + 1) * LANES] = sums_ref[c]
     scales, numbers = pack([sums_ref[c] for c in range(tiles)], msg_ref, 0)
     first_ref[0] = scales
+    lefts = []
     for c in range(tiles):
-        first_ref[1 + c] = numbers[c][0:16].astype(jnp.int16)
-    left = jnp.concatenate([number[16:obs_count] for number in numbers], axis=0)
-    spare = (first_ref.shape[0] - 1 - tiles) * 16 - left.shape[0]
-    if spare:
-        left = jnp.concatenate([left, jnp.zeros((spare, LANES), jnp.int32)], axis=0)
-    for t in range(left.shape[0] // 16):
-        first_ref[1 + tiles + t] = left[16 * t : 16 * t + 16].astype(jnp.int16)
+        rows = first_rows(numbers[c])
+        first_ref[1 + c] = rows[0:16].astype(jnp.int16)
+        lefts.append(rows[16:24])
+    for t in range(tiles // 2):
+        first_ref[1 + tiles + t] = jnp.concatenate(lefts[2 * t : 2 * t + 2], axis=0).astype(jnp.int16)
+
+
+def first_rows(block):
+    odd = lax.broadcasted_iota(jnp.int32, (8, LANES), 0) % 2 == 1
+    rows = [block[8 * k : 8 * k + 8] for k in range(6)]
+    return jnp.concatenate([jnp.where(odd, pltpu.roll(rows[k + 1], 1, axis=0), rows[k]) for k in (0, 2, 4)], axis=0)
 
 
 def krylov_kernel(me_ref, own_ref, mate_ref, across_ref, zero_ref, one_ref, two_ref, gram_ref, window_ref, *, total_rows, rows_here):
@@ -386,21 +411,19 @@
     tiles = cols // LANES
     row_tiles = own_ref.shape[0] // 16
 
-    def lay(place, part, r):
-        at = pl.ds(place, ENTRIES, stride=8)
-        for c in range(tiles):
-            window_ref[c, at, :] = part[c][r * ENTRIES : (r + 1) * ENTRIES]
-
     own = [own_ref[:, c * LANES : (c + 1) * LANES] for c in range(tiles)]
     mate = unpack(lambda place: mate_ref[place], row_tiles, tiles)
     across = unpack(lambda place: across_ref[place], row_tiles, tiles)
-    odd = me_ref[0] % 2
-    for r in range(2):
-        lay(2 + r, own, r)
-        lay(4 * (1 - odd) + r, mate, r)
-        lay(4 * odd + r, across, r)
-    for empty in (6, 7):
-        put(window_ref, empty, ENTRIES, 8, jnp.zeros((ENTRIES, cols), jnp.float32))
+    odd = me_ref[0] % 2 == 1
+    sublane = lax.broadcasted_iota(jnp.int32, (8, LANES), 0)
+    for c in range(tiles):
+        low = jnp.where(odd, mate[c], across[c])
+        high = jnp.where(odd, across[c], mate[c])
+        for entry in range(ENTRIES):
+            here, at = slice(entry // 4 * 8, entry // 4 * 8 + 8), entry % 4 * 2
+            rows = [pltpu.roll(part[here], (2 * k - at) % 8, axis=0) for k, part in enumerate((low, own[c], high))]
+            tile = jnp.where(sublane < 2, rows[0], jnp.where(sublane < 4, rows[1], jnp.where(sublane < 6, rows[2], 0.0)))
+            window_ref[c, entry * 8 : entry * 8 + 8, :] = tile
     window = lambda entry: jnp.concatenate([window_ref[c, entry * 8 : entry * 8 + 8, :] for c in range(cols // LANES)], axis=1)
     shape = (8, cols)
     place = lax.broadcasted_iota(jnp.int32, shape, 0)
@@ -452,14 +475,15 @@
 def far_kernel(gram_ref, two_ref, far_ref, out_ref):
     obs_count, _, cols = two_ref.shape
     tiles = cols // LANES
-    rest = obs_count - 16
-    factors = factors_of(far_ref[0], 2)
-    left = jnp.concatenate([as_float(far_ref[t]) for t in range(1 + tiles, far_ref.shape[0])], axis=0)
-    total = jnp.zeros((obs_count, LANES), jnp.float32)
+    factors = first_rows(jnp.concatenate(factors_of(far_ref[0], 3), axis=0))
+    total = jnp.zeros((ENTRIES, LANES), jnp.float32)
+    zero = jnp.zeros((1, LANES), jnp.float32)
     for c in range(tiles):
-        far = jnp.concatenate([as_float(far_ref[1 + c]) * factors[0], left[rest * c : rest * (c + 1)] * factors[1][0:rest]], axis=0)
-        mine = jnp.concatenate([two_ref[e, 1:2, c * LANES : (c + 1) * LANES] for e in range(obs_count)], axis=0)
-        total = total + far * mine
+        left = as_float(far_ref[1 + tiles + c // 2])[c % 2 * 8 : c % 2 * 8 + 8]
+        far = jnp.concatenate([as_float(far_ref[1 + c]), left], axis=0) * factors
+        lanes = slice(c * LANES, (c + 1) * LANES)
+        mine = [two_ref[e, 1:2, lanes] if e < obs_count else zero for e in FIRST_ORDER]
+        total = total + far * jnp.concatenate(mine, axis=0)
     part = (-2.0 * (GAIN * SMOOTH_PULL) ** 3) * jnp.sum(total)
     row = lax.broadcasted_iota(jnp.int32, (8, LANES), 0)
     out_ref[...] = gram_ref[...] + jnp.where(row == 5, part, 0.0)
@@ -539,7 +563,7 @@
         functools.partial(residual_kernel, total_rows=total_rows),
         in_specs=[smem] + [vmem] * (1 + len(parts)),
         out_specs=[vmem, vmem, vmem],
-        out_shape=[f32(block, cols), packed(1, 1 + block // 16 * tiles), packed(1 + tiles + -(-(obs_count - 16) * tiles // 16))],
+        out_shape=[f32(block, cols), packed(1, 1 + block // 16 * tiles), packed(1 + tiles + tiles // 2)],
         scratch_shapes=[pltpu.VMEM((tiles, block, LANES), jnp.float32)],
         compiler_params=params,
         name="residual",

time: 58.9 us -> 59.6 us (1.012)
  no operation moved by 1% of the time
where the time goes in v2:
time: 59.6 us; the launch traced here: 59.5 us
  starting transfers between devices  22.8 us (38%)
  waiting for transfers between devices  18.8 us (32%)
  Pallas kernels  17.7 us (30%)
    ppermute x14, starting transfers between devices, on_device(): lax.ppermute(x, 'rows', [(i, i ^ mask) for i in range(count)])  20.8 us
    ppermute x14, waiting for transfers between devices, on_device(): lax.ppermute(x, 'rows', [(i, i ^ mask) for i in range(count)])  15.9 us
    pallas_call x2, Pallas kernels, partial_sums(): pl.pallas_call(functools.partial(sums_kernel, scale=scale, rows_here=rows...  12.2 us
    ppermute x1, waiting for transfers between devices, on_device(): far = lax.ppermute(first, 'rows', [(i + 2, i) for i in range(count - 2)])  2.93 us
    pallas_call x5, Pallas kernels, add_split(): pl.pallas_call(functools.partial(add_split_kernel, place=place), in_specs...  1.91 us
    pallas_call x1, Pallas kernels, on_device(): pl.pallas_call(functools.partial(krylov_kernel, total_rows=total_rows, ro...  1.77 us
    ppermute x1, starting transfers between devices, on_device(): far = lax.ppermute(first, 'rows', [(i + 2, i) for i in range(count - 2)])  1.28 us
  transfers between devices with their start and end apart: 16, of which 9 were waited for; matrix products, arithmetic and copies ran while one was open for 0% of the time, Pallas kernels for 15%

profile of v2, /device:TPU:0, one launch (start us, length us, event | category | flops | bytes accessed | tf_op | source)
XLA Modules:
  0.0 59.5 jit_solution(14653572458044508434)
XLA Ops:
  0.0 6.7 %partial_sums.2 = (f32[8,48,512]{2,1,0:T(8,128)}, s16[8,13,16,128]{3,2,1,0:T(8,128)(2,1)}) custom-call(s32[1]{0:T(128)} %bitcast.me_ref, s32[128]{0:T(128)} %ids_ref.3, f32[4,6]{1,0:T(4,128)} %gain_ref.3, f32[4]{0:T(128)} %weight_ref.3, bf16[8,6,32,1024]{3,2,1,0:T(8,128)(2,1)} %reflect_hbm.3, s32[8,32,1024]{2,1,0:T(8,128)} %conf_hbm.3, ...), custom_call_target="tpu_custom_call" | custom-call | tf_op jit(solution)/shard_map/partial_sums/pallas_call | solution.py:265
  7.3 5.5 %partial_sums.3 = (f32[8,48,512]{2,1,0:T(8,128)S(1)}, s16[8,13,16,128]{3,2,1,0:T(8,128)(2,1)S(1)}) custom-call(s32[1]{0:T(128)} %bitcast.me_ref, s32[128]{0:T(128)S(1)} %copy-done.3, f32[4,6]{1,0:T(4,128)S(1)} %copy-done.2, f32[4]{0:T(128)S(1)} %copy-done.4, bf16[8,6,32,1024]{3,2,1,0:T(8,128)(2,1)} %reflect_hbm.3, s32[8,32,1024]{2,1,0:T(8,128)} %conf_hbm.3, ...), custom_call_target="tpu_custom_call" | custom-call | tf_op jit(solution)/shard_map/partial_sums/pallas_call | solution.py:265
  13.4 3.0 %collective-permute-start.1 = (s16[4,13,16,128]{3,2,1,0:T(8,128)(2,1)S(1)}, s16[4,13,16,128]{3,2,1,0:T(8,128)(2,1)S(1)}, u32[]{:S(2)}, u32[]{:S(2)}) collective-permute-start(s16[4,13,16,128]{3,2,1,0:T(8,128)(2,1)S(1)} %get-tuple-element.30), channel_id=1, source_target_pairs={{0,2},{1,3},{2,0},{3,1},{4,6},{5,7},{6,4},{7,5},{8,10},{9,11},{10,... | collective-permute-start | bytes 638984 | tf_op jit(solution)/shard_map/ppermute | solution.py:545
  16.8 1.6 %collective-permute-start.4 = (s16[4,13,16,128]{3,2,1,0:T(8,128)(2,1)S(1)}, s16[4,13,16,128]{3,2,1,0:T(8,128)(2,1)S(1)}, u32[]{:S(2)}, u32[]{:S(2)}) collective-permute-start(s16[4,13,16,128]{3,2,1,0:T(8,128)(2,1)S(1)} %get-tuple-element.37), channel_id=1, source_target_pairs={{0,4},{1,5},{2,6},{3,7},{4,0},{5,1},{6,2},{7,3},{8,12},{9,13},{10,... | collective-permute-start | bytes 638984 | tf_op jit(solution)/shard_map/ppermute | solution.py:545
  18.5 3.4 %collective-permute-done.1.refs_1_ = s16[4,13,16,128]{3,2,1,0:T(8,128)(2,1)S(1)} collective-permute-done((s16[4,13,16,128]{3,2,1,0:T(8,128)(2,1)S(1)}, s16[4,13,16,128]{3,2,1,0:T(8,128)(2,1)S(1)}, u32[]{:S(2)}, u32[]{:S(2)}) %collective-permute-start.1) | collective-permute-done | bytes 213024 | tf_op jit(solution)/shard_map/ppermute | solution.py:545
  22.3 1.9 %collective-permute-start.2 = (s16[2,13,16,128]{3,2,1,0:T(8,128)(2,1)S(1)}, s16[2,13,16,128]{3,2,1,0:T(8,128)(2,1)S(1)}, u32[]{:S(2)}, u32[]{:S(2)}) collective-permute-start(s16[2,13,16,128]{3,2,1,0:T(8,128)(2,1)S(1)} %get-tuple-element.32), channel_id=1, source_target_pairs={{0,4},{1,5},{2,6},{3,7},{4,0},{5,1},{6,2},{7,3},{8,12},{9,13},{10,... | collective-permute-start | bytes 319496 | tf_op jit(solution)/shard_map/ppermute | solution.py:545
  24.5 1.6 %collective-permute-start.5 = (s16[2,13,16,128]{3,2,1,0:T(8,128)(2,1)S(1)}, s16[2,13,16,128]{3,2,1,0:T(8,128)(2,1)S(1)}, u32[]{:S(2)}, u32[]{:S(2)}) collective-permute-start(s16[2,13,16,128]{3,2,1,0:T(8,128)(2,1)S(1)} %get-tuple-element.39), channel_id=1, source_target_pairs={{0,2},{1,3},{2,0},{3,1},{4,6},{5,7},{6,4},{7,5},{8,10},{9,11},{10,... | collective-permute-start | bytes 319496 | tf_op jit(solution)/shard_map/ppermute | solution.py:545
  26.1 0.9 %collective-permute-done.2.refs_1_ = s16[2,13,16,128]{3,2,1,0:T(8,128)(2,1)S(1)} collective-permute-done((s16[2,13,16,128]{3,2,1,0:T(8,128)(2,1)S(1)}, s16[2,13,16,128]{3,2,1,0:T(8,128)(2,1)S(1)}, u32[]{:S(2)}, u32[]{:S(2)}) %collective-permute-start.2) | collective-permute-done | bytes 106528 | tf_op jit(solution)/shard_map/ppermute | solution.py:545
  27.1 2.2 %collective-permute-done.5.refs_3_ = s16[2,13,16,128]{3,2,1,0:T(8,128)(2,1)S(1)} collective-permute-done((s16[2,13,16,128]{3,2,1,0:T(8,128)(2,1)S(1)}, s16[2,13,16,128]{3,2,1,0:T(8,128)(2,1)S(1)}, u32[]{:S(2)}, u32[]{:S(2)}) %collective-permute-start.5) | collective-permute-done | bytes 106528 | tf_op jit(solution)/shard_map/ppermute | solution.py:545
  29.7 2.7 %collective-permute-start.6 = (s16[1,25,16,128]{3,2,1,0:T(8,128)(2,1)S(1)}, s16[1,25,16,128]{3,2,1,0:T(8,128)(2,1)S(1)}, u32[]{:S(2)}, u32[]{:S(2)}) collective-permute-start(s16[1,25,16,128]{3,2,1,0:T(8,128)(2,1)S(1)} %get-tuple-element.41), channel_id=1, source_target_pairs={{0,8},{1,9},{2,10},{3,11},{4,12},{5,13},{6,14},{7,15},{8,0},{9,1},... | collective-permute-start | bytes 307208 | tf_op jit(solution)/shard_map/ppermute | solution.py:545
  32.3 4.1 %collective-permute-done.6.refs_1_ = s16[1,25,16,128]{3,2,1,0:T(8,128)(2,1)S(1)} collective-permute-done((s16[1,25,16,128]{3,2,1,0:T(8,128)(2,1)S(1)}, s16[1,25,16,128]{3,2,1,0:T(8,128)(2,1)S(1)}, u32[]{:S(2)}, u32[]{:S(2)}) %collective-permute-start.6) | collective-permute-done | bytes 102432 | tf_op jit(solution)/shard_map/ppermute | solution.py:545
  36.4 0.7 %residual.1 = (f32[48,1024]{1,0:T(8,128)S(1)}, s16[1,25,16,128]{3,2,1,0:T(8,128)(2,1)S(1)}, s16[13,16,128]{2,1,0:T(8,128)(2,1)S(1)}) custom-call(s32[1]{0:T(128)} %bitcast.me_ref, f32[18,2,1024]{2,1,0:T(2,128)S(1)} %bitcast.6, f32[1,48,1024]{2,1,0:T(8,128)S(1)} %get-tuple-element.40.refs_0_, s16[1,25,16,128]{3,2,1,0:T(8,128)(2,1)S(1)} %collective-permute-done.6.refs_1_), custom_call_target="tpu_custom_call" | custom-call | tf_op jit(solution)/shard_map/residual/pallas_call | solution.py:562
  37.1 0.7 %collective-permute-start.8 = (s16[25,16,128]{2,1,0:T(8,128)(2,1)S(1)}, s16[25,16,128]{2,1,0:T(8,128)(2,1)S(1)}, u32[]{:S(2)}, u32[]{:S(2)}) collective-permute-start(s16[25,16,128]{2,1,0:T(8,128)(2,1)S(1)} %bitcast.8), channel_id=1, source_target_pairs={{1,2},{3,4},{5,6},{7,8},{9,10},{11,12},{13,14},{2,1},{4,3},{6,5},{... | collective-permute-start | bytes 307208 | tf_op jit(solution)/shard_map/ppermute | solution.py:575
  37.8 2.9 %collective-permute-start.7 = (s16[25,16,128]{2,1,0:T(8,128)(2,1)S(1)}, s16[25,16,128]{2,1,0:T(8,128)(2,1)S(1)}, u32[]{:S(2)}, u32[]{:S(2)}) collective-permute-start(s16[25,16,128]{2,1,0:T(8,128)(2,1)S(1)} %bitcast.9), channel_id=1, source_target_pairs={{0,1},{1,0},{2,3},{3,2},{4,5},{5,4},{6,7},{7,6},{8,9},{9,8},{10,11... | collective-permute-start | bytes 307208 | tf_op jit(solution)/shard_map/ppermute | solution.py:545
  40.7 1.3 %collective-permute-start.9 = (s16[13,16,128]{2,1,0:T(8,128)(2,1)S(1)}, s16[13,16,128]{2,1,0:T(8,128)(2,1)S(1)}, u32[]{:S(2)}, u32[]{:S(2)}) collective-permute-start(s16[13,16,128]{2,1,0:T(8,128)(2,1)S(1)} %get-tuple-element.46), channel_id=1, source_target_pairs={{2,0},{3,1},{4,2},{5,3},{6,4},{7,5},{8,6},{9,7},{10,8},{11,9},{12,... | collective-permute-start | bytes 159752 | tf_op jit(solution)/shard_map/ppermute | solution.py:576
  42.1 1.8 %krylov.1 = (f32[18,2,1024]{2,1,0:T(2,128)S(1)}, f32[18,2,1024]{2,1,0:T(2,128)S(1)}, f32[18,2,1024]{2,1,0:T(2,128)S(1)}, f32[8,128]{1,0:T(8,128)S(1)}) custom-call(s32[1]{0:T(128)} %bitcast.me_ref, f32[48,1024]{1,0:T(8,128)S(1)} %get-tuple-element.42.own_ref, s16[25,16,128]{2,1,0:T(8,128)(2,1)S(1)} %collective-permute-done.7.mate_ref, ...), custom_call_target="tpu_custom_call" | custom-call | tf_op jit(solution)/shard_map/krylov/pallas_call | solution.py:577
  43.8 2.9 %collective-permute-done.9.far_ref = s16[13,16,128]{2,1,0:T(8,128)(2,1)S(1)} collective-permute-done((s16[13,16,128]{2,1,0:T(8,128)(2,1)S(1)}, s16[13,16,128]{2,1,0:T(8,128)(2,1)S(1)}, u32[]{:S(2)}, u32[]{:S(2)}) %collective-permute-start.9) | collective-permute-done | bytes 53280 | tf_op jit(solution)/shard_map/ppermute | solution.py:576
  47.1 1.4 %collective-permute-start.11 = (f32[8,128]{1,0:T(8,128)S(1)}, f32[8,128]{1,0:T(8,128)S(1)}, u32[]{:S(2)}, u32[]{:S(2)}) collective-permute-start(f32[8,128]{1,0:T(8,128)S(1)} %far.1), channel_id=1, source_target_pairs={{0,2},{1,3},{2,0},{3,1},{4,6},{5,7},{6,4},{7,5},{8,10},{9,11},{10,... | collective-permute-start | bytes 12296 | tf_op jit(solution)/shard_map/ppermute | solution.py:545
  49.0 1.2 %collective-permute-done.12 = f32[8,128]{1,0:T(8,128)S(1)} collective-permute-done((f32[8,128]{1,0:T(8,128)S(1)}, f32[8,128]{1,0:T(8,128)S(1)}, u32[]{:S(2)}, u32[]{:S(2)}) %collective-permute-start.12) | collective-permute-done | bytes 4128 | tf_op jit(solution)/shard_map/ppermute | solution.py:545
  50.8 3.3 %collective-permute-start.15 = (f32[8,128]{1,0:T(8,128)S(1)}, f32[8,128]{1,0:T(8,128)S(1)}, u32[]{:S(2)}, u32[]{:S(2)}) collective-permute-start(f32[8,128]{1,0:T(8,128)S(1)} %add_add_fusion.refs_0_), channel_id=1, source_target_pairs={{0,12},{1,13},{2,14},{3,15},{4,8},{5,9},{6,10},{7,11},{8,4},{9,5},... | collective-permute-start | bytes 12296 | tf_op jit(solution)/shard_map/ppermute | solution.py:545
  54.1 1.1 %collective-permute-start.13 = (f32[8,128]{1,0:T(8,128)S(1)}, f32[8,128]{1,0:T(8,128)S(1)}, u32[]{:S(2)}, u32[]{:S(2)}) collective-permute-start(f32[8,128]{1,0:T(8,128)S(1)} %add_add_fusion.refs_0_), channel_id=1, source_target_pairs={{0,4},{1,5},{2,6},{3,7},{4,0},{5,1},{6,2},{7,3},{8,12},{9,13},{10,... | collective-permute-start | bytes 12296 | tf_op jit(solution)/shard_map/ppermute | solution.py:545
  55.3 1.0 %collective-permute-done.15.refs_3_ = f32[8,128]{1,0:T(8,128)S(1)} collective-permute-done((f32[8,128]{1,0:T(8,128)S(1)}, f32[8,128]{1,0:T(8,128)S(1)}, u32[]{:S(2)}, u32[]{:S(2)}) %collective-permute-start.15) | collective-permute-done | bytes 4128 | tf_op jit(solution)/shard_map/ppermute | solution.py:545
  56.3 2.3 %collective-permute-done.14.refs_2_ = f32[8,128]{1,0:T(8,128)S(1)} collective-permute-done((f32[8,128]{1,0:T(8,128)S(1)}, f32[8,128]{1,0:T(8,128)S(1)}, u32[]{:S(2)}, u32[]{:S(2)}) %collective-permute-start.14) | collective-permute-done | bytes 4128 | tf_op jit(solution)/shard_map/ppermute | solution.py:545
  58.6 0.9 %combine.1 = f32[18,2,1024]{2,1,0:T(2,128)} custom-call(f32[8,128]{1,0:T(8,128)S(1)} %add_add_fusion.refs_0_, f32[8,128]{1,0:T(8,128)S(1)} %collective-permute-done.13.refs_1_, f32[8,128]{1,0:T(8,128)S(1)} %collective-permute-done.14.refs_2_, f32[8,128]{1,0:T(8,128)S(1)} %collective-permute-done.15.refs_3_, f32[18,2,1024]{2,1,0:T(2,128)S(1)} %bitcast.7, ...), custom_call_target="tpu_custom_call" | custom-call | tf_op jit(solution)/shard_map/combine/pallas_call | solution.py:596
  (30 shorter events, 4.1 us)
Async XLA Ops:
  0.0 7.3 %copy-start = (f32[2,18,1024]{2,0,1:T(2,128)S(1)}, f32[2,18,1024]{2,0,1:T(2,128)}, u32[]{:S(2)}) copy-start(f32[2,18,1024]{2,0,1:T(2,128)} %param.13) | copy-start | bytes 442372
  0.0 7.3 %copy-start.2 = (f32[4,6]{1,0:T(4,128)S(1)}, f32[4,6]{1,0:T(4,128)}, u32[]{:S(2)}) copy-start(f32[4,6]{1,0:T(4,128)} %gain_ref.3) | copy-start | bytes 292
  0.0 7.3 %copy-start.3 = (s32[128]{0:T(128)S(1)}, s32[128]{0:T(128)}, u32[]{:S(2)}) copy-start(s32[128]{0:T(128)} %ids_ref.3) | copy-start | bytes 1540
  0.0 7.3 %copy-start.4 = (f32[4]{0:T(128)S(1)}, f32[4]{0:T(128)}, u32[]{:S(2)}) copy-start(f32[4]{0:T(128)} %weight_ref.3) | copy-start | bytes 52
  6.7 6.3 %copy-start.1 = (f32[8,48,512]{2,1,0:T(8,128)S(1)}, f32[8,48,512]{2,1,0:T(8,128)}, u32[]{:S(2)}) copy-start(f32[8,48,512]{2,1,0:T(8,128)} %get-tuple-element.27.refs_0_) | copy-start | bytes 2359300
  6.7 6.2 %collective-permute-start = (s16[8,13,16,128]{3,2,1,0:T(8,128)(2,1)}, s16[8,13,16,128]{3,2,1,0:T(8,128)(2,1)S(1)}, u32[]{:S(2)}, u32[]{:S(2)}) collective-permute-start(s16[8,13,16,128]{3,2,1,0:T(8,128)(2,1)} %get-tuple-element.28), channel_id=1, source_target_pairs={{0,1},{1,0},{2,3},{3,2},{4,5},{5,4},{6,7},{7,6},{8,9},{9,8},{10,11... | collective-permute-start | bytes 1277960 | tf_op jit(solution)/shard_map/ppermute | solution.py:545
  12.8 3.6 %collective-permute-start.3 = (s16[8,13,16,128]{3,2,1,0:T(8,128)(2,1)S(1)}, s16[8,13,16,128]{3,2,1,0:T(8,128)(2,1)S(1)}, u32[]{:S(2)}, u32[]{:S(2)}) collective-permute-start(s16[8,13,16,128]{3,2,1,0:T(8,128)(2,1)S(1)} %get-tuple-element.35), channel_id=1, source_target_pairs={{0,1},{1,0},{2,3},{3,2},{4,5},{5,4},{6,7},{7,6},{8,9},{9,8},{10,11... | collective-permute-start | bytes 1277960 | tf_op jit(solution)/shard_map/ppermute | solution.py:545
  13.4 8.5 %collective-permute-start.1 = (s16[4,13,16,128]{3,2,1,0:T(8,128)(2,1)S(1)}, s16[4,13,16,128]{3,2,1,0:T(8,128)(2,1)S(1)}, u32[]{:S(2)}, u32[]{:S(2)}) collective-permute-start(s16[4,13,16,128]{3,2,1,0:T(8,128)(2,1)S(1)} %get-tuple-element.30), channel_id=1, source_target_pairs={{0,2},{1,3},{2,0},{3,1},{4,6},{5,7},{6,4},{7,5},{8,10},{9,11},{10,... | collective-permute-start | bytes 638984 | tf_op jit(solution)/shard_map/ppermute | solution.py:545
  16.8 7.3 %collective-permute-start.4 = (s16[4,13,16,128]{3,2,1,0:T(8,128)(2,1)S(1)}, s16[4,13,16,128]{3,2,1,0:T(8,128)(2,1)S(1)}, u32[]{:S(2)}, u32[]{:S(2)}) collective-permute-start(s16[4,13,16,128]{3,2,1,0:T(8,128)(2,1)S(1)} %get-tuple-element.37), channel_id=1, source_target_pairs={{0,4},{1,5},{2,6},{3,7},{4,0},{5,1},{6,2},{7,3},{8,12},{9,13},{10,... | collective-permute-start | bytes 638984 | tf_op jit(solution)/shard_map/ppermute | solution.py:545
  22.3 4.8 %collective-permute-start.2 = (s16[2,13,16,128]{3,2,1,0:T(8,128)(2,1)S(1)}, s16[2,13,16,128]{3,2,1,0:T(8,128)(2,1)S(1)}, u32[]{:S(2)}, u32[]{:S(2)}) collective-permute-start(s16[2,13,16,128]{3,2,1,0:T(8,128)(2,1)S(1)} %get-tuple-element.32), channel_id=1, source_target_pairs={{0,4},{1,5},{2,6},{3,7},{4,0},{5,1},{6,2},{7,3},{8,12},{9,13},{10,... | collective-permute-start | bytes 319496 | tf_op jit(solution)/shard_map/ppermute | solution.py:545
  24.5 4.8 %collective-permute-start.5 = (s16[2,13,16,128]{3,2,1,0:T(8,128)(2,1)S(1)}, s16[2,13,16,128]{3,2,1,0:T(8,128)(2,1)S(1)}, u32[]{:S(2)}, u32[]{:S(2)}) collective-permute-start(s16[2,13,16,128]{3,2,1,0:T(8,128)(2,1)S(1)} %get-tuple-element.39), channel_id=1, source_target_pairs={{0,2},{1,3},{2,0},{3,1},{4,6},{5,7},{6,4},{7,5},{8,10},{9,11},{10,... | collective-permute-start | bytes 319496 | tf_op jit(solution)/shard_map/ppermute | solution.py:545
  29.7 6.7 %collective-permute-start.6 = (s16[1,25,16,128]{3,2,1,0:T(8,128)(2,1)S(1)}, s16[1,25,16,128]{3,2,1,0:T(8,128)(2,1)S(1)}, u32[]{:S(2)}, u32[]{:S(2)}) collective-permute-start(s16[1,25,16,128]{3,2,1,0:T(8,128)(2,1)S(1)} %get-tuple-element.41), channel_id=1, source_target_pairs={{0,8},{1,9},{2,10},{3,11},{4,12},{5,13},{6,14},{7,15},{8,0},{9,1},... | collective-permute-start | bytes 307208 | tf_op jit(solution)/shard_map/ppermute | solution.py:545
  37.1 4.9 %collective-permute-start.8 = (s16[25,16,128]{2,1,0:T(8,128)(2,1)S(1)}, s16[25,16,128]{2,1,0:T(8,128)(2,1)S(1)}, u32[]{:S(2)}, u32[]{:S(2)}) collective-permute-start(s16[25,16,128]{2,1,0:T(8,128)(2,1)S(1)} %bitcast.8), channel_id=1, source_target_pairs={{1,2},{3,4},{5,6},{7,8},{9,10},{11,12},{13,14},{2,1},{4,3},{6,5},{... | collective-permute-start | bytes 307208 | tf_op jit(solution)/shard_map/ppermute | solution.py:575
  37.8 4.2 %collective-permute-start.7 = (s16[25,16,128]{2,1,0:T(8,128)(2,1)S(1)}, s16[25,16,128]{2,1,0:T(8,128)(2,1)S(1)}, u32[]{:S(2)}, u32[]{:S(2)}) collective-permute-start(s16[25,16,128]{2,1,0:T(8,128)(2,1)S(1)} %bitcast.9), channel_id=1, source_target_pairs={{0,1},{1,0},{2,3},{3,2},{4,5},{5,4},{6,7},{7,6},{8,9},{9,8},{10,11... | collective-permute-start | bytes 307208 | tf_op jit(solution)/shard_map/ppermute | solution.py:545
  40.7 6.0 %collective-permute-start.9 = (s16[13,16,128]{2,1,0:T(8,128)(2,1)S(1)}, s16[13,16,128]{2,1,0:T(8,128)(2,1)S(1)}, u32[]{:S(2)}, u32[]{:S(2)}) collective-permute-start(s16[13,16,128]{2,1,0:T(8,128)(2,1)S(1)} %get-tuple-element.46), channel_id=1, source_target_pairs={{2,0},{3,1},{4,2},{5,3},{6,4},{7,5},{8,6},{9,7},{10,8},{11,9},{12,... | collective-permute-start | bytes 159752 | tf_op jit(solution)/shard_map/ppermute | solution.py:576
  47.1 3.1 %collective-permute-start.12 = (f32[8,128]{1,0:T(8,128)S(1)}, f32[8,128]{1,0:T(8,128)S(1)}, u32[]{:S(2)}, u32[]{:S(2)}) collective-permute-start(f32[8,128]{1,0:T(8,128)S(1)} %far.1), channel_id=1, source_target_pairs={{0,3},{1,2},{2,1},{3,0},{4,7},{5,6},{6,5},{7,4},{8,11},{9,10},{10,... | collective-permute-start | bytes 12296 | tf_op jit(solution)/shard_map/ppermute | solution.py:545
  47.1 3.7 %collective-permute-start.11 = (f32[8,128]{1,0:T(8,128)S(1)}, f32[8,128]{1,0:T(8,128)S(1)}, u32[]{:S(2)}, u32[]{:S(2)}) collective-permute-start(f32[8,128]{1,0:T(8,128)S(1)} %far.1), channel_id=1, source_target_pairs={{0,2},{1,3},{2,0},{3,1},{4,6},{5,7},{6,4},{7,5},{8,10},{9,11},{10,... | collective-permute-start | bytes 12296 | tf_op jit(solution)/shard_map/ppermute | solution.py:545
  48.5 2.3 %collective-permute-start.10 = (f32[8,128]{1,0:T(8,128)S(1)}, f32[8,128]{1,0:T(8,128)S(1)}, u32[]{:S(2)}, u32[]{:S(2)}) collective-permute-start(f32[8,128]{1,0:T(8,128)S(1)} %far.1), channel_id=1, source_target_pairs={{0,1},{1,0},{2,3},{3,2},{4,5},{5,4},{6,7},{7,6},{8,9},{9,8},{10,11... | collective-permute-start | bytes 12296 | tf_op jit(solution)/shard_map/ppermute | solution.py:545
  50.8 5.5 %collective-permute-start.15 = (f32[8,128]{1,0:T(8,128)S(1)}, f32[8,128]{1,0:T(8,128)S(1)}, u32[]{:S(2)}, u32[]{:S(2)}) collective-permute-start(f32[8,128]{1,0:T(8,128)S(1)} %add_add_fusion.refs_0_), channel_id=1, source_target_pairs={{0,12},{1,13},{2,14},{3,15},{4,8},{5,9},{6,10},{7,11},{8,4},{9,5},... | collective-permute-start | bytes 12296 | tf_op jit(solution)/shard_map/ppermute | solution.py:545
  54.1 4.5 %collective-permute-start.14 = (f32[8,128]{1,0:T(8,128)S(1)}, f32[8,128]{1,0:T(8,128)S(1)}, u32[]{:S(2)}, u32[]{:S(2)}) collective-permute-start(f32[8,128]{1,0:T(8,128)S(1)} %add_add_fusion.refs_0_), channel_id=1, source_target_pairs={{0,8},{1,9},{2,10},{3,11},{4,12},{5,13},{6,14},{7,15},{8,0},{9,1},... | collective-permute-start | bytes 12296 | tf_op jit(solution)/shard_map/ppermute | solution.py:545
  54.1 4.5 %collective-permute-start.13 = (f32[8,128]{1,0:T(8,128)S(1)}, f32[8,128]{1,0:T(8,128)S(1)}, u32[]{:S(2)}, u32[]{:S(2)}) collective-permute-start(f32[8,128]{1,0:T(8,128)S(1)} %add_add_fusion.refs_0_), channel_id=1, source_target_pairs={{0,4},{1,5},{2,6},{3,7},{4,0},{5,1},{6,2},{7,3},{8,12},{9,13},{10,... | collective-permute-start | bytes 12296 | tf_op jit(solution)/shard_map/ppermute | solution.py:545

commit v3 on v1

--- a/solution.py
+++ b/solution.py
@@ -520,20 +520,15 @@
         parts.append((kept, sent))
     flip = lambda x, mask: lax.ppermute(x, "rows", [(i, i ^ mask) for i in range(count)])
     swap = lambda x, bit: flip(x, 1 << bit)
+    parts = [(kept, swap(sent, 0)) for kept, sent in parts]
     bits = list(range(1, count.bit_length() - 1))
-    parts = [(kept, swap(sent, 0)) for kept, sent in parts]
-    if len(bits) >= 2:
-        orders = [((bits[0], 0), (bits[1], 0)), ((bits[1], 1), (bits[0], 0))]
-        for step in range(2):
-            for chunk in range(CHUNKS):
-                bit, place = orders[chunk % 2][step]
-                kept, sent = add_split(me // 2**bit % 2, place, *parts[chunk])
-                parts[chunk] = (kept, swap(sent, bit))
-        bits = bits[2:]
+    for step in range(len(bits)):
+        for chunk in range(CHUNKS):
+            turned = chunk % 2 == 1 and len(bits) >= 2 and step < 2
+            bit, place = (bits[1 - step], 1 - step) if turned else (bits[step], 0)
+            kept, sent = add_split(me // 2**bit % 2, place, *parts[chunk])
+            parts[chunk] = (kept, swap(sent, bit))
     parts = [x for part in parts for x in part]
-    for bit in bits:
-        kept, sent = add_split(me // 2**bit % 2, 0, *parts)
-        parts = [kept, swap(sent, bit)]
 
     own, msg, first = pl.pallas_call(
         functools.partial(residual_kernel, total_rows=total_rows),

time: 58.9 us -> 57.9 us (0.983)
  waiting for transfers between devices: 18.6 us -> 14.7 us
  starting transfers between devices: 22.7 us -> 25.3 us
    ppermute x14 -> x15, waiting for transfers between devices: 15.9 us -> 11.9 us  [on_device(): lax.ppermute(x, 'rows', [(i, i ^ mask) for i in range(count)])]
    ppermute x14 -> x15, starting transfers between devices: 20.8 us -> 23.3 us  [on_device(): lax.ppermute(x, 'rows', [(i, i ^ mask) for i in range(count)])]
    pallas_call x5 -> x6, Pallas kernels: 1.91 us -> 2.21 us  [add_split(): pl.pallas_call(functools.partial(add_split_kernel, place=place), in_specs...]
  transfers between devices with their start and end apart: 16 -> 17, of which waited for: 9 -> 9; matrix products, arithmetic and copies ran while one was open for 0% -> 0% of each run, Pallas kernels for 15% -> 16%
where the time goes in v3:
time: 57.9 us; the launch traced here: 57.7 us
  starting transfers between devices  25.3 us (44%)
  Pallas kernels  17.6 us (30%)
  waiting for transfers between devices  14.7 us (25%)
    ppermute x15, starting transfers between devices, on_device(): lax.ppermute(x, 'rows', [(i, i ^ mask) for i in range(count)])  23.3 us
    ppermute x15, waiting for transfers between devices, on_device(): lax.ppermute(x, 'rows', [(i, i ^ mask) for i in range(count)])  11.9 us
    pallas_call x2, Pallas kernels, partial_sums(): pl.pallas_call(functools.partial(sums_kernel, scale=scale, rows_here=rows...  11.7 us
    ppermute x1, waiting for transfers between devices, on_device(): far = lax.ppermute(first, 'rows', [(i + 2, i) for i in range(count - 2)])  2.74 us
    pallas_call x6, Pallas kernels, add_split(): pl.pallas_call(functools.partial(add_split_kernel, place=place), in_specs...  2.21 us
    pallas_call x1, Pallas kernels, on_device(): pl.pallas_call(functools.partial(krylov_kernel, total_rows=total_rows, ro...  1.82 us
    ppermute x1, starting transfers between devices, on_device(): far = lax.ppermute(first, 'rows', [(i + 2, i) for i in range(count - 2)])  1.28 us
  transfers between devices with their start and end apart: 17, of which 9 were waited for; matrix products, arithmetic and copies ran while one was open for 0% of the time, Pallas kernels for 16%

profile of v3, /device:TPU:0, one launch (start us, length us, event | category | flops | bytes accessed | tf_op | source)
XLA Modules:
  0.0 57.7 jit_solution(1201322600000866795)
XLA Ops:
  0.0 6.4 %partial_sums.2 = (f32[8,48,512]{2,1,0:T(8,128)}, s16[8,13,16,128]{3,2,1,0:T(8,128)(2,1)}) custom-call(s32[1]{0:T(128)} %bitcast.me_ref, s32[128]{0:T(128)} %ids_ref.3, f32[4,6]{1,0:T(4,128)} %gain_ref.3, f32[4]{0:T(128)} %weight_ref.3, bf16[8,6,32,1024]{3,2,1,0:T(8,128)(2,1)} %reflect_hbm.3, s32[8,32,1024]{2,1,0:T(8,128)} %conf_hbm.3, ...), custom_call_target="tpu_custom_call" | custom-call | tf_op jit(solution)/shard_map/partial_sums/pallas_call | solution.py:243
  7.0 5.2 %partial_sums.3 = (f32[8,48,512]{2,1,0:T(8,128)S(1)}, s16[8,13,16,128]{3,2,1,0:T(8,128)(2,1)S(1)}) custom-call(s32[1]{0:T(128)} %bitcast.me_ref, s32[128]{0:T(128)S(1)} %copy-done.3, f32[4,6]{1,0:T(4,128)S(1)} %copy-done.2, f32[4]{0:T(128)S(1)} %copy-done.4, bf16[8,6,32,1024]{3,2,1,0:T(8,128)(2,1)} %reflect_hbm.3, s32[8,32,1024]{2,1,0:T(8,128)} %conf_hbm.3, ...), custom_call_target="tpu_custom_call" | custom-call | tf_op jit(solution)/shard_map/partial_sums/pallas_call | solution.py:243
  12.8 3.0 %collective-permute-start.1 = (s16[4,13,16,128]{3,2,1,0:T(8,128)(2,1)S(1)}, s16[4,13,16,128]{3,2,1,0:T(8,128)(2,1)S(1)}, u32[]{:S(2)}, u32[]{:S(2)}) collective-permute-start(s16[4,13,16,128]{3,2,1,0:T(8,128)(2,1)S(1)} %get-tuple-element.32), channel_id=1, source_target_pairs={{0,2},{1,3},{2,0},{3,1},{4,6},{5,7},{6,4},{7,5},{8,10},{9,11},{10,... | collective-permute-start | bytes 638984 | tf_op jit(solution)/shard_map/ppermute | solution.py:521
  16.3 1.6 %collective-permute-start.5 = (s16[4,13,16,128]{3,2,1,0:T(8,128)(2,1)S(1)}, s16[4,13,16,128]{3,2,1,0:T(8,128)(2,1)S(1)}, u32[]{:S(2)}, u32[]{:S(2)}) collective-permute-start(s16[4,13,16,128]{3,2,1,0:T(8,128)(2,1)S(1)} %get-tuple-element.41), channel_id=1, source_target_pairs={{0,4},{1,5},{2,6},{3,7},{4,0},{5,1},{6,2},{7,3},{8,12},{9,13},{10,... | collective-permute-start | bytes 638984 | tf_op jit(solution)/shard_map/ppermute | solution.py:521
  17.9 3.4 %collective-permute-done.1.refs_1_ = s16[4,13,16,128]{3,2,1,0:T(8,128)(2,1)S(1)} collective-permute-done((s16[4,13,16,128]{3,2,1,0:T(8,128)(2,1)S(1)}, s16[4,13,16,128]{3,2,1,0:T(8,128)(2,1)S(1)}, u32[]{:S(2)}, u32[]{:S(2)}) %collective-permute-start.1) | collective-permute-done | bytes 213024 | tf_op jit(solution)/shard_map/ppermute | solution.py:521
  21.7 1.9 %collective-permute-start.2 = (s16[2,13,16,128]{3,2,1,0:T(8,128)(2,1)S(1)}, s16[2,13,16,128]{3,2,1,0:T(8,128)(2,1)S(1)}, u32[]{:S(2)}, u32[]{:S(2)}) collective-permute-start(s16[2,13,16,128]{3,2,1,0:T(8,128)(2,1)S(1)} %get-tuple-element.34), channel_id=1, source_target_pairs={{0,4},{1,5},{2,6},{3,7},{4,0},{5,1},{6,2},{7,3},{8,12},{9,13},{10,... | collective-permute-start | bytes 319496 | tf_op jit(solution)/shard_map/ppermute | solution.py:521
  23.9 1.6 %collective-permute-start.6 = (s16[2,13,16,128]{3,2,1,0:T(8,128)(2,1)S(1)}, s16[2,13,16,128]{3,2,1,0:T(8,128)(2,1)S(1)}, u32[]{:S(2)}, u32[]{:S(2)}) collective-permute-start(s16[2,13,16,128]{3,2,1,0:T(8,128)(2,1)S(1)} %get-tuple-element.43), channel_id=1, source_target_pairs={{0,2},{1,3},{2,0},{3,1},{4,6},{5,7},{6,4},{7,5},{8,10},{9,11},{10,... | collective-permute-start | bytes 319496 | tf_op jit(solution)/shard_map/ppermute | solution.py:521
  25.5 0.9 %collective-permute-done.2.refs_1_ = s16[2,13,16,128]{3,2,1,0:T(8,128)(2,1)S(1)} collective-permute-done((s16[2,13,16,128]{3,2,1,0:T(8,128)(2,1)S(1)}, s16[2,13,16,128]{3,2,1,0:T(8,128)(2,1)S(1)}, u32[]{:S(2)}, u32[]{:S(2)}) %collective-permute-start.2) | collective-permute-done | bytes 106528 | tf_op jit(solution)/shard_map/ppermute | solution.py:521
  26.8 2.9 %collective-permute-start.3 = (s16[1,13,16,128]{3,2,1,0:T(8,128)(2,1)S(1)}, s16[1,13,16,128]{3,2,1,0:T(8,128)(2,1)S(1)}, u32[]{:S(2)}, u32[]{:S(2)}) collective-permute-start(s16[1,13,16,128]{3,2,1,0:T(8,128)(2,1)S(1)} %get-tuple-element.36), channel_id=1, source_target_pairs={{0,8},{1,9},{2,10},{3,11},{4,12},{5,13},{6,14},{7,15},{8,0},{9,1},... | collective-permute-start | bytes 159752 | tf_op jit(solution)/shard_map/ppermute | solution.py:521
  30.0 1.7 %collective-permute-start.7 = (s16[1,13,16,128]{3,2,1,0:T(8,128)(2,1)S(1)}, s16[1,13,16,128]{3,2,1,0:T(8,128)(2,1)S(1)}, u32[]{:S(2)}, u32[]{:S(2)}) collective-permute-start(s16[1,13,16,128]{3,2,1,0:T(8,128)(2,1)S(1)} %get-tuple-element.45), channel_id=1, source_target_pairs={{0,8},{1,9},{2,10},{3,11},{4,12},{5,13},{6,14},{7,15},{8,0},{9,1},... | collective-permute-start | bytes 159752 | tf_op jit(solution)/shard_map/ppermute | solution.py:521
  31.7 0.7 %collective-permute-done.3.refs_1_ = s16[1,13,16,128]{3,2,1,0:T(8,128)(2,1)S(1)} collective-permute-done((s16[1,13,16,128]{3,2,1,0:T(8,128)(2,1)S(1)}, s16[1,13,16,128]{3,2,1,0:T(8,128)(2,1)S(1)}, u32[]{:S(2)}, u32[]{:S(2)}) %collective-permute-start.3) | collective-permute-done | bytes 53280 | tf_op jit(solution)/shard_map/ppermute | solution.py:521
  32.5 2.7 %collective-permute-done.7.refs_3_ = s16[1,13,16,128]{3,2,1,0:T(8,128)(2,1)S(1)} collective-permute-done((s16[1,13,16,128]{3,2,1,0:T(8,128)(2,1)S(1)}, s16[1,13,16,128]{3,2,1,0:T(8,128)(2,1)S(1)}, u32[]{:S(2)}, u32[]{:S(2)}) %collective-permute-start.7) | collective-permute-done | bytes 53280 | tf_op jit(solution)/shard_map/ppermute | solution.py:521
  36.5 2.9 %collective-permute-start.8 = (s16[25,16,128]{2,1,0:T(8,128)(2,1)S(1)}, s16[25,16,128]{2,1,0:T(8,128)(2,1)S(1)}, u32[]{:S(2)}, u32[]{:S(2)}) collective-permute-start(s16[25,16,128]{2,1,0:T(8,128)(2,1)S(1)} %bitcast.9), channel_id=1, source_target_pairs={{0,1},{1,0},{2,3},{3,2},{4,5},{5,4},{6,7},{7,6},{8,9},{9,8},{10,11... | collective-permute-start | bytes 307208 | tf_op jit(solution)/shard_map/ppermute | solution.py:521
  39.5 1.3 %collective-permute-start.10 = (s16[10,16,128]{2,1,0:T(8,128)(2,1)S(1)}, s16[10,16,128]{2,1,0:T(8,128)(2,1)S(1)}, u32[]{:S(2)}, u32[]{:S(2)}) collective-permute-start(s16[10,16,128]{2,1,0:T(8,128)(2,1)S(1)} %get-tuple-element.50), channel_id=1, source_target_pairs={{2,0},{3,1},{4,2},{5,3},{6,4},{7,5},{8,6},{9,7},{10,8},{11,9},{12,... | collective-permute-start | bytes 122888 | tf_op jit(solution)/shard_map/ppermute | solution.py:547
  40.8 1.8 %krylov.1 = (f32[18,2,1024]{2,1,0:T(2,128)S(1)}, f32[18,2,1024]{2,1,0:T(2,128)S(1)}, f32[18,2,1024]{2,1,0:T(2,128)S(1)}, f32[8,128]{1,0:T(8,128)S(1)}) custom-call(s32[1]{0:T(128)} %bitcast.me_ref, f32[48,1024]{1,0:T(8,128)S(1)} %get-tuple-element.46.own_ref, s16[25,16,128]{2,1,0:T(8,128)(2,1)S(1)} %collective-permute-done.8.mate_ref, ...), custom_call_target="tpu_custom_call" | custom-call | tf_op jit(solution)/shard_map/krylov/pallas_call | solution.py:548
  42.6 2.7 %collective-permute-done.10.far_ref = s16[10,16,128]{2,1,0:T(8,128)(2,1)S(1)} collective-permute-done((s16[10,16,128]{2,1,0:T(8,128)(2,1)S(1)}, s16[10,16,128]{2,1,0:T(8,128)(2,1)S(1)}, u32[]{:S(2)}, u32[]{:S(2)}) %collective-permute-start.10) | collective-permute-done | bytes 40992 | tf_op jit(solution)/shard_map/ppermute | solution.py:547
  45.7 1.0 %collective-permute-start.13 = (f32[8,128]{1,0:T(8,128)S(1)}, f32[8,128]{1,0:T(8,128)S(1)}, u32[]{:S(2)}, u32[]{:S(2)}) collective-permute-start(f32[8,128]{1,0:T(8,128)S(1)} %far.1), channel_id=1, source_target_pairs={{0,3},{1,2},{2,1},{3,0},{4,7},{5,6},{6,5},{7,4},{8,11},{9,10},{10,... | collective-permute-start | bytes 12296 | tf_op jit(solution)/shard_map/ppermute | solution.py:521
  46.6 1.6 %collective-permute-start.12 = (f32[8,128]{1,0:T(8,128)S(1)}, f32[8,128]{1,0:T(8,128)S(1)}, u32[]{:S(2)}, u32[]{:S(2)}) collective-permute-start(f32[8,128]{1,0:T(8,128)S(1)} %far.1), channel_id=1, source_target_pairs={{0,2},{1,3},{2,0},{3,1},{4,6},{5,7},{6,4},{7,5},{8,10},{9,11},{10,... | collective-permute-start | bytes 12296 | tf_op jit(solution)/shard_map/ppermute | solution.py:521
  48.8 1.5 %collective-permute-done.12 = f32[8,128]{1,0:T(8,128)S(1)} collective-permute-done((f32[8,128]{1,0:T(8,128)S(1)}, f32[8,128]{1,0:T(8,128)S(1)}, u32[]{:S(2)}, u32[]{:S(2)}) %collective-permute-start.12) | collective-permute-done | bytes 4128 | tf_op jit(solution)/shard_map/ppermute | solution.py:521
  50.2 2.1 %collective-permute-start.16 = (f32[8,128]{1,0:T(8,128)S(1)}, f32[8,128]{1,0:T(8,128)S(1)}, u32[]{:S(2)}, u32[]{:S(2)}) collective-permute-start(f32[8,128]{1,0:T(8,128)S(1)} %add_add_fusion.refs_0_), channel_id=1, source_target_pairs={{0,12},{1,13},{2,14},{3,15},{4,8},{5,9},{6,10},{7,11},{8,4},{9,5},... | collective-permute-start | bytes 12296 | tf_op jit(solution)/shard_map/ppermute | solution.py:521
  52.5 2.2 %collective-permute-start.14 = (f32[8,128]{1,0:T(8,128)S(1)}, f32[8,128]{1,0:T(8,128)S(1)}, u32[]{:S(2)}, u32[]{:S(2)}) collective-permute-start(f32[8,128]{1,0:T(8,128)S(1)} %add_add_fusion.refs_0_), channel_id=1, source_target_pairs={{0,4},{1,5},{2,6},{3,7},{4,0},{5,1},{6,2},{7,3},{8,12},{9,13},{10,... | collective-permute-start | bytes 12296 | tf_op jit(solution)/shard_map/ppermute | solution.py:521
  54.7 1.0 %collective-permute-done.16.refs_3_ = f32[8,128]{1,0:T(8,128)S(1)} collective-permute-done((f32[8,128]{1,0:T(8,128)S(1)}, f32[8,128]{1,0:T(8,128)S(1)}, u32[]{:S(2)}, u32[]{:S(2)}) %collective-permute-start.16) | collective-permute-done | bytes 4128 | tf_op jit(solution)/shard_map/ppermute | solution.py:521
  55.7 1.1 %collective-permute-done.15.refs_2_ = f32[8,128]{1,0:T(8,128)S(1)} collective-permute-done((f32[8,128]{1,0:T(8,128)S(1)}, f32[8,128]{1,0:T(8,128)S(1)}, u32[]{:S(2)}, u32[]{:S(2)}) %collective-permute-start.15) | collective-permute-done | bytes 4128 | tf_op jit(solution)/shard_map/ppermute | solution.py:521
  56.9 0.9 %combine.1 = f32[18,2,1024]{2,1,0:T(2,128)} custom-call(f32[8,128]{1,0:T(8,128)S(1)} %add_add_fusion.refs_0_, f32[8,128]{1,0:T(8,128)S(1)} %collective-permute-done.14.refs_1_, f32[8,128]{1,0:T(8,128)S(1)} %collective-permute-done.15.refs_2_, f32[8,128]{1,0:T(8,128)S(1)} %collective-permute-done.16.refs_3_, f32[18,2,1024]{2,1,0:T(2,128)S(1)} %bitcast.7, ...), custom_call_target="tpu_custom_call" | custom-call | tf_op jit(solution)/shard_map/combine/pallas_call | solution.py:567
  (33 shorter events, 5.3 us)
Async XLA Ops:
  0.0 7.0 %copy-start = (f32[2,18,1024]{2,0,1:T(2,128)S(1)}, f32[2,18,1024]{2,0,1:T(2,128)}, u32[]{:S(2)}) copy-start(f32[2,18,1024]{2,0,1:T(2,128)} %param.13) | copy-start | bytes 442372
  0.0 7.0 %copy-start.2 = (f32[4,6]{1,0:T(4,128)S(1)}, f32[4,6]{1,0:T(4,128)}, u32[]{:S(2)}) copy-start(f32[4,6]{1,0:T(4,128)} %gain_ref.3) | copy-start | bytes 292
  0.0 7.0 %copy-start.3 = (s32[128]{0:T(128)S(1)}, s32[128]{0:T(128)}, u32[]{:S(2)}) copy-start(s32[128]{0:T(128)} %ids_ref.3) | copy-start | bytes 1540
  0.0 7.0 %copy-start.4 = (f32[4]{0:T(128)S(1)}, f32[4]{0:T(128)}, u32[]{:S(2)}) copy-start(f32[4]{0:T(128)} %weight_ref.3) | copy-start | bytes 52
  6.5 5.9 %copy-start.1 = (f32[8,48,512]{2,1,0:T(8,128)S(1)}, f32[8,48,512]{2,1,0:T(8,128)}, u32[]{:S(2)}) copy-start(f32[8,48,512]{2,1,0:T(8,128)} %get-tuple-element.29.refs_0_) | copy-start | bytes 2359300
  6.5 5.9 %collective-permute-start = (s16[8,13,16,128]{3,2,1,0:T(8,128)(2,1)}, s16[8,13,16,128]{3,2,1,0:T(8,128)(2,1)S(1)}, u32[]{:S(2)}, u32[]{:S(2)}) collective-permute-start(s16[8,13,16,128]{3,2,1,0:T(8,128)(2,1)} %get-tuple-element.30), channel_id=1, source_target_pairs={{0,1},{1,0},{2,3},{3,2},{4,5},{5,4},{6,7},{7,6},{8,9},{9,8},{10,11... | collective-permute-start | bytes 1277960 | tf_op jit(solution)/shard_map/ppermute | solution.py:521
  12.2 3.6 %collective-permute-start.4 = (s16[8,13,16,128]{3,2,1,0:T(8,128)(2,1)S(1)}, s16[8,13,16,128]{3,2,1,0:T(8,128)(2,1)S(1)}, u32[]{:S(2)}, u32[]{:S(2)}) collective-permute-start(s16[8,13,16,128]{3,2,1,0:T(8,128)(2,1)S(1)} %get-tuple-element.39), channel_id=1, source_target_pairs={{0,1},{1,0},{2,3},{3,2},{4,5},{5,4},{6,7},{7,6},{8,9},{9,8},{10,11... | collective-permute-start | bytes 1277960 | tf_op jit(solution)/shard_map/ppermute | solution.py:521
  12.8 8.5 %collective-permute-start.1 = (s16[4,13,16,128]{3,2,1,0:T(8,128)(2,1)S(1)}, s16[4,13,16,128]{3,2,1,0:T(8,128)(2,1)S(1)}, u32[]{:S(2)}, u32[]{:S(2)}) collective-permute-start(s16[4,13,16,128]{3,2,1,0:T(8,128)(2,1)S(1)} %get-tuple-element.32), channel_id=1, source_target_pairs={{0,2},{1,3},{2,0},{3,1},{4,6},{5,7},{6,4},{7,5},{8,10},{9,11},{10,... | collective-permute-start | bytes 638984 | tf_op jit(solution)/shard_map/ppermute | solution.py:521
  16.3 7.3 %collective-permute-start.5 = (s16[4,13,16,128]{3,2,1,0:T(8,128)(2,1)S(1)}, s16[4,13,16,128]{3,2,1,0:T(8,128)(2,1)S(1)}, u32[]{:S(2)}, u32[]{:S(2)}) collective-permute-start(s16[4,13,16,128]{3,2,1,0:T(8,128)(2,1)S(1)} %get-tuple-element.41), channel_id=1, source_target_pairs={{0,4},{1,5},{2,6},{3,7},{4,0},{5,1},{6,2},{7,3},{8,12},{9,13},{10,... | collective-permute-start | bytes 638984 | tf_op jit(solution)/shard_map/ppermute | solution.py:521
  21.7 4.8 %collective-permute-start.2 = (s16[2,13,16,128]{3,2,1,0:T(8,128)(2,1)S(1)}, s16[2,13,16,128]{3,2,1,0:T(8,128)(2,1)S(1)}, u32[]{:S(2)}, u32[]{:S(2)}) collective-permute-start(s16[2,13,16,128]{3,2,1,0:T(8,128)(2,1)S(1)} %get-tuple-element.34), channel_id=1, source_target_pairs={{0,4},{1,5},{2,6},{3,7},{4,0},{5,1},{6,2},{7,3},{8,12},{9,13},{10,... | collective-permute-start | bytes 319496 | tf_op jit(solution)/shard_map/ppermute | solution.py:521
  23.9 5.8 %collective-permute-start.6 = (s16[2,13,16,128]{3,2,1,0:T(8,128)(2,1)S(1)}, s16[2,13,16,128]{3,2,1,0:T(8,128)(2,1)S(1)}, u32[]{:S(2)}, u32[]{:S(2)}) collective-permute-start(s16[2,13,16,128]{3,2,1,0:T(8,128)(2,1)S(1)} %get-tuple-element.43), channel_id=1, source_target_pairs={{0,2},{1,3},{2,0},{3,1},{4,6},{5,7},{6,4},{7,5},{8,10},{9,11},{10,... | collective-permute-start | bytes 319496 | tf_op jit(solution)/shard_map/ppermute | solution.py:521
  26.8 5.6 %collective-permute-start.3 = (s16[1,13,16,128]{3,2,1,0:T(8,128)(2,1)S(1)}, s16[1,13,16,128]{3,2,1,0:T(8,128)(2,1)S(1)}, u32[]{:S(2)}, u32[]{:S(2)}) collective-permute-start(s16[1,13,16,128]{3,2,1,0:T(8,128)(2,1)S(1)} %get-tuple-element.36), channel_id=1, source_target_pairs={{0,8},{1,9},{2,10},{3,11},{4,12},{5,13},{6,14},{7,15},{8,0},{9,1},... | collective-permute-start | bytes 159752 | tf_op jit(solution)/shard_map/ppermute | solution.py:521
  30.0 5.1 %collective-permute-start.7 = (s16[1,13,16,128]{3,2,1,0:T(8,128)(2,1)S(1)}, s16[1,13,16,128]{3,2,1,0:T(8,128)(2,1)S(1)}, u32[]{:S(2)}, u32[]{:S(2)}) collective-permute-start(s16[1,13,16,128]{3,2,1,0:T(8,128)(2,1)S(1)} %get-tuple-element.45), channel_id=1, source_target_pairs={{0,8},{1,9},{2,10},{3,11},{4,12},{5,13},{6,14},{7,15},{8,0},{9,1},... | collective-permute-start | bytes 159752 | tf_op jit(solution)/shard_map/ppermute | solution.py:521
  35.9 4.9 %collective-permute-start.9 = (s16[25,16,128]{2,1,0:T(8,128)(2,1)S(1)}, s16[25,16,128]{2,1,0:T(8,128)(2,1)S(1)}, u32[]{:S(2)}, u32[]{:S(2)}) collective-permute-start(s16[25,16,128]{2,1,0:T(8,128)(2,1)S(1)} %bitcast.8), channel_id=1, source_target_pairs={{1,2},{3,4},{5,6},{7,8},{9,10},{11,12},{13,14},{2,1},{4,3},{6,5},{... | collective-permute-start | bytes 307208 | tf_op jit(solution)/shard_map/ppermute | solution.py:546
  36.5 4.2 %collective-permute-start.8 = (s16[25,16,128]{2,1,0:T(8,128)(2,1)S(1)}, s16[25,16,128]{2,1,0:T(8,128)(2,1)S(1)}, u32[]{:S(2)}, u32[]{:S(2)}) collective-permute-start(s16[25,16,128]{2,1,0:T(8,128)(2,1)S(1)} %bitcast.9), channel_id=1, source_target_pairs={{0,1},{1,0},{2,3},{3,2},{4,5},{5,4},{6,7},{7,6},{8,9},{9,8},{10,11... | collective-permute-start | bytes 307208 | tf_op jit(solution)/shard_map/ppermute | solution.py:521
  39.5 5.9 %collective-permute-start.10 = (s16[10,16,128]{2,1,0:T(8,128)(2,1)S(1)}, s16[10,16,128]{2,1,0:T(8,128)(2,1)S(1)}, u32[]{:S(2)}, u32[]{:S(2)}) collective-permute-start(s16[10,16,128]{2,1,0:T(8,128)(2,1)S(1)} %get-tuple-element.50), channel_id=1, source_target_pairs={{2,0},{3,1},{4,2},{5,3},{6,4},{7,5},{8,6},{9,7},{10,8},{11,9},{12,... | collective-permute-start | bytes 122888 | tf_op jit(solution)/shard_map/ppermute | solution.py:547
  45.7 3.1 %collective-permute-start.13 = (f32[8,128]{1,0:T(8,128)S(1)}, f32[8,128]{1,0:T(8,128)S(1)}, u32[]{:S(2)}, u32[]{:S(2)}) collective-permute-start(f32[8,128]{1,0:T(8,128)S(1)} %far.1), channel_id=1, source_target_pairs={{0,3},{1,2},{2,1},{3,0},{4,7},{5,6},{6,5},{7,4},{8,11},{9,10},{10,... | collective-permute-start | bytes 12296 | tf_op jit(solution)/shard_map/ppermute | solution.py:521
  46.6 3.6 %collective-permute-start.12 = (f32[8,128]{1,0:T(8,128)S(1)}, f32[8,128]{1,0:T(8,128)S(1)}, u32[]{:S(2)}, u32[]{:S(2)}) collective-permute-start(f32[8,128]{1,0:T(8,128)S(1)} %far.1), channel_id=1, source_target_pairs={{0,2},{1,3},{2,0},{3,1},{4,6},{5,7},{6,4},{7,5},{8,10},{9,11},{10,... | collective-permute-start | bytes 12296 | tf_op jit(solution)/shard_map/ppermute | solution.py:521
  48.2 2.0 %collective-permute-start.11 = (f32[8,128]{1,0:T(8,128)S(1)}, f32[8,128]{1,0:T(8,128)S(1)}, u32[]{:S(2)}, u32[]{:S(2)}) collective-permute-start(f32[8,128]{1,0:T(8,128)S(1)} %far.1), channel_id=1, source_target_pairs={{0,1},{1,0},{2,3},{3,2},{4,5},{5,4},{6,7},{7,6},{8,9},{9,8},{10,11... | collective-permute-start | bytes 12296 | tf_op jit(solution)/shard_map/ppermute | solution.py:521
  50.2 5.5 %collective-permute-start.16 = (f32[8,128]{1,0:T(8,128)S(1)}, f32[8,128]{1,0:T(8,128)S(1)}, u32[]{:S(2)}, u32[]{:S(2)}) collective-permute-start(f32[8,128]{1,0:T(8,128)S(1)} %add_add_fusion.refs_0_), channel_id=1, source_target_pairs={{0,12},{1,13},{2,14},{3,15},{4,8},{5,9},{6,10},{7,11},{8,4},{9,5},... | collective-permute-start | bytes 12296 | tf_op jit(solution)/shard_map/ppermute | solution.py:521
  52.3 4.5 %collective-permute-start.15 = (f32[8,128]{1,0:T(8,128)S(1)}, f32[8,128]{1,0:T(8,128)S(1)}, u32[]{:S(2)}, u32[]{:S(2)}) collective-permute-start(f32[8,128]{1,0:T(8,128)S(1)} %add_add_fusion.refs_0_), channel_id=1, source_target_pairs={{0,8},{1,9},{2,10},{3,11},{4,12},{5,13},{6,14},{7,15},{8,0},{9,1},... | collective-permute-start | bytes 12296 | tf_op jit(solution)/shard_map/ppermute | solution.py:521
  52.5 4.3 %collective-permute-start.14 = (f32[8,128]{1,0:T(8,128)S(1)}, f32[8,128]{1,0:T(8,128)S(1)}, u32[]{:S(2)}, u32[]{:S(2)}) collective-permute-start(f32[8,128]{1,0:T(8,128)S(1)} %add_add_fusion.refs_0_), channel_id=1, source_target_pairs={{0,4},{1,5},{2,6},{3,7},{4,0},{5,1},{6,2},{7,3},{8,12},{9,13},{10,... | collective-permute-start | bytes 12296 | tf_op jit(solution)/shard_map/ppermute | solution.py:521

commit v4 on v3

--- a/solution.py
+++ b/solution.py
@@ -560,8 +560,9 @@
             far_kernel, in_specs=[vmem] * 3, out_specs=vmem, out_shape=f32(8, LANES), compiler_params=params, name="far"
         )(gram, two, far)
     ]
-    for bit in range(0, count.bit_length() - 1, 2):
-        masks = [mask << bit for mask in (1, 2, 3) if mask << bit < count]
+    top = count.bit_length() - 1
+    rounds = [[mask << bit for mask in (1, 2, 3) if mask << bit < count] for bit in range(1, top, 2)] + [[1]]
+    for masks in rounds:
         gram = sum(grams[1:], grams[0])
         grams = [gram] + [flip(gram, mask) for mask in masks]
     out = pl.pallas_call(

time: 57.9 us -> 59.9 us (1.035)
  waiting for transfers between devices: 14.7 us -> 17.9 us
  starting transfers between devices: 25.3 us -> 24.1 us
    ppermute x15 -> x14, waiting for transfers between devices: 11.9 us -> 15.2 us  [on_device(): lax.ppermute(x, 'rows', [(i, i ^ mask) for i in range(count)])]
    ppermute x15 -> x14, starting transfers between devices: 23.3 us -> 22.1 us  [on_device(): lax.ppermute(x, 'rows', [(i, i ^ mask) for i in range(count)])]
  transfers between devices with their start and end apart: 17 -> 16, of which waited for: 9 -> 10; matrix products, arithmetic and copies ran while one was open for 0% -> 0% of each run, Pallas kernels for 16% -> 16%
where the time goes in v4:
time: 59.9 us; the launch traced here: 59.7 us
  starting transfers between devices  24.1 us (40%)
  waiting for transfers between devices  17.9 us (30%)
  Pallas kernels  17.5 us (29%)
    ppermute x14, starting transfers between devices, on_device(): lax.ppermute(x, 'rows', [(i, i ^ mask) for i in range(count)])  22.1 us
    ppermute x14, waiting for transfers between devices, on_device(): lax.ppermute(x, 'rows', [(i, i ^ mask) for i in range(count)])  15.2 us
    pallas_call x2, Pallas kernels, partial_sums(): pl.pallas_call(functools.partial(sums_kernel, scale=scale, rows_here=rows...  11.7 us
    ppermute x1, waiting for transfers between devices, on_device(): far = lax.ppermute(first, 'rows', [(i + 2, i) for i in range(count - 2)])  2.74 us
    pallas_call x6, Pallas kernels, add_split(): pl.pallas_call(functools.partial(add_split_kernel, place=place), in_specs...  2.21 us
    pallas_call x1, Pallas kernels, on_device(): pl.pallas_call(functools.partial(krylov_kernel, total_rows=total_rows, ro...  1.82 us
    ppermute x1, starting transfers between devices, on_device(): far = lax.ppermute(first, 'rows', [(i + 2, i) for i in range(count - 2)])  1.28 us
  transfers between devices with their start and end apart: 16, of which 10 were waited for; matrix products, arithmetic and copies ran while one was open for 0% of the time, Pallas kernels for 16%

profile of v4, /device:TPU:0, one launch (start us, length us, event | category | flops | bytes accessed | tf_op | source)
XLA Modules:
  0.0 59.7 jit_solution(10480063794010992014)
XLA Ops:
  0.0 6.4 %partial_sums.2 = (f32[8,48,512]{2,1,0:T(8,128)}, s16[8,13,16,128]{3,2,1,0:T(8,128)(2,1)}) custom-call(s32[1]{0:T(128)} %bitcast.me_ref, s32[128]{0:T(128)} %ids_ref.3, f32[4,6]{1,0:T(4,128)} %gain_ref.3, f32[4]{0:T(128)} %weight_ref.3, bf16[8,6,32,1024]{3,2,1,0:T(8,128)(2,1)} %reflect_hbm.3, s32[8,32,1024]{2,1,0:T(8,128)} %conf_hbm.3, ...), custom_call_target="tpu_custom_call" | custom-call | tf_op jit(solution)/shard_map/partial_sums/pallas_call | solution.py:243
  7.0 5.2 %partial_sums.3 = (f32[8,48,512]{2,1,0:T(8,128)S(1)}, s16[8,13,16,128]{3,2,1,0:T(8,128)(2,1)S(1)}) custom-call(s32[1]{0:T(128)} %bitcast.me_ref, s32[128]{0:T(128)S(1)} %copy-done.3, f32[4,6]{1,0:T(4,128)S(1)} %copy-done.2, f32[4]{0:T(128)S(1)} %copy-done.4, bf16[8,6,32,1024]{3,2,1,0:T(8,128)(2,1)} %reflect_hbm.3, s32[8,32,1024]{2,1,0:T(8,128)} %conf_hbm.3, ...), custom_call_target="tpu_custom_call" | custom-call | tf_op jit(solution)/shard_map/partial_sums/pallas_call | solution.py:243
  12.8 3.0 %collective-permute-start.1 = (s16[4,13,16,128]{3,2,1,0:T(8,128)(2,1)S(1)}, s16[4,13,16,128]{3,2,1,0:T(8,128)(2,1)S(1)}, u32[]{:S(2)}, u32[]{:S(2)}) collective-permute-start(s16[4,13,16,128]{3,2,1,0:T(8,128)(2,1)S(1)} %get-tuple-element.32), channel_id=1, source_target_pairs={{0,2},{1,3},{2,0},{3,1},{4,6},{5,7},{6,4},{7,5},{8,10},{9,11},{10,... | collective-permute-start | bytes 638984 | tf_op jit(solution)/shard_map/ppermute | solution.py:521
  16.3 1.6 %collective-permute-start.5 = (s16[4,13,16,128]{3,2,1,0:T(8,128)(2,1)S(1)}, s16[4,13,16,128]{3,2,1,0:T(8,128)(2,1)S(1)}, u32[]{:S(2)}, u32[]{:S(2)}) collective-permute-start(s16[4,13,16,128]{3,2,1,0:T(8,128)(2,1)S(1)} %get-tuple-element.41), channel_id=1, source_target_pairs={{0,4},{1,5},{2,6},{3,7},{4,0},{5,1},{6,2},{7,3},{8,12},{9,13},{10,... | collective-permute-start | bytes 638984 | tf_op jit(solution)/shard_map/ppermute | solution.py:521
  17.9 3.4 %collective-permute-done.1.refs_1_ = s16[4,13,16,128]{3,2,1,0:T(8,128)(2,1)S(1)} collective-permute-done((s16[4,13,16,128]{3,2,1,0:T(8,128)(2,1)S(1)}, s16[4,13,16,128]{3,2,1,0:T(8,128)(2,1)S(1)}, u32[]{:S(2)}, u32[]{:S(2)}) %collective-permute-start.1) | collective-permute-done | bytes 213024 | tf_op jit(solution)/shard_map/ppermute | solution.py:521
  21.7 1.9 %collective-permute-start.2 = (s16[2,13,16,128]{3,2,1,0:T(8,128)(2,1)S(1)}, s16[2,13,16,128]{3,2,1,0:T(8,128)(2,1)S(1)}, u32[]{:S(2)}, u32[]{:S(2)}) collective-permute-start(s16[2,13,16,128]{3,2,1,0:T(8,128)(2,1)S(1)} %get-tuple-element.34), channel_id=1, source_target_pairs={{0,4},{1,5},{2,6},{3,7},{4,0},{5,1},{6,2},{7,3},{8,12},{9,13},{10,... | collective-permute-start | bytes 319496 | tf_op jit(solution)/shard_map/ppermute | solution.py:521
  23.9 1.6 %collective-permute-start.6 = (s16[2,13,16,128]{3,2,1,0:T(8,128)(2,1)S(1)}, s16[2,13,16,128]{3,2,1,0:T(8,128)(2,1)S(1)}, u32[]{:S(2)}, u32[]{:S(2)}) collective-permute-start(s16[2,13,16,128]{3,2,1,0:T(8,128)(2,1)S(1)} %get-tuple-element.43), channel_id=1, source_target_pairs={{0,2},{1,3},{2,0},{3,1},{4,6},{5,7},{6,4},{7,5},{8,10},{9,11},{10,... | collective-permute-start | bytes 319496 | tf_op jit(solution)/shard_map/ppermute | solution.py:521
  25.5 0.9 %collective-permute-done.2.refs_1_ = s16[2,13,16,128]{3,2,1,0:T(8,128)(2,1)S(1)} collective-permute-done((s16[2,13,16,128]{3,2,1,0:T(8,128)(2,1)S(1)}, s16[2,13,16,128]{3,2,1,0:T(8,128)(2,1)S(1)}, u32[]{:S(2)}, u32[]{:S(2)}) %collective-permute-start.2) | collective-permute-done | bytes 106528 | tf_op jit(solution)/shard_map/ppermute | solution.py:521
  26.8 2.9 %collective-permute-start.3 = (s16[1,13,16,128]{3,2,1,0:T(8,128)(2,1)S(1)}, s16[1,13,16,128]{3,2,1,0:T(8,128)(2,1)S(1)}, u32[]{:S(2)}, u32[]{:S(2)}) collective-permute-start(s16[1,13,16,128]{3,2,1,0:T(8,128)(2,1)S(1)} %get-tuple-element.36), channel_id=1, source_target_pairs={{0,8},{1,9},{2,10},{3,11},{4,12},{5,13},{6,14},{7,15},{8,0},{9,1},... | collective-permute-start | bytes 159752 | tf_op jit(solution)/shard_map/ppermute | solution.py:521
  30.0 1.7 %collective-permute-start.7 = (s16[1,13,16,128]{3,2,1,0:T(8,128)(2,1)S(1)}, s16[1,13,16,128]{3,2,1,0:T(8,128)(2,1)S(1)}, u32[]{:S(2)}, u32[]{:S(2)}) collective-permute-start(s16[1,13,16,128]{3,2,1,0:T(8,128)(2,1)S(1)} %get-tuple-element.45), channel_id=1, source_target_pairs={{0,8},{1,9},{2,10},{3,11},{4,12},{5,13},{6,14},{7,15},{8,0},{9,1},... | collective-permute-start | bytes 159752 | tf_op jit(solution)/shard_map/ppermute | solution.py:521
  31.7 0.7 %collective-permute-done.3.refs_1_ = s16[1,13,16,128]{3,2,1,0:T(8,128)(2,1)S(1)} collective-permute-done((s16[1,13,16,128]{3,2,1,0:T(8,128)(2,1)S(1)}, s16[1,13,16,128]{3,2,1,0:T(8,128)(2,1)S(1)}, u32[]{:S(2)}, u32[]{:S(2)}) %collective-permute-start.3) | collective-permute-done | bytes 53280 | tf_op jit(solution)/shard_map/ppermute | solution.py:521
  32.4 2.7 %collective-permute-done.7.refs_3_ = s16[1,13,16,128]{3,2,1,0:T(8,128)(2,1)S(1)} collective-permute-done((s16[1,13,16,128]{3,2,1,0:T(8,128)(2,1)S(1)}, s16[1,13,16,128]{3,2,1,0:T(8,128)(2,1)S(1)}, u32[]{:S(2)}, u32[]{:S(2)}) %collective-permute-start.7) | collective-permute-done | bytes 53280 | tf_op jit(solution)/shard_map/ppermute | solution.py:521
  36.5 2.9 %collective-permute-start.8 = (s16[25,16,128]{2,1,0:T(8,128)(2,1)S(1)}, s16[25,16,128]{2,1,0:T(8,128)(2,1)S(1)}, u32[]{:S(2)}, u32[]{:S(2)}) collective-permute-start(s16[25,16,128]{2,1,0:T(8,128)(2,1)S(1)} %bitcast.9), channel_id=1, source_target_pairs={{0,1},{1,0},{2,3},{3,2},{4,5},{5,4},{6,7},{7,6},{8,9},{9,8},{10,11... | collective-permute-start | bytes 307208 | tf_op jit(solution)/shard_map/ppermute | solution.py:521
  39.5 1.3 %collective-permute-start.10 = (s16[10,16,128]{2,1,0:T(8,128)(2,1)S(1)}, s16[10,16,128]{2,1,0:T(8,128)(2,1)S(1)}, u32[]{:S(2)}, u32[]{:S(2)}) collective-permute-start(s16[10,16,128]{2,1,0:T(8,128)(2,1)S(1)} %get-tuple-element.50), channel_id=1, source_target_pairs={{2,0},{3,1},{4,2},{5,3},{6,4},{7,5},{8,6},{9,7},{10,8},{11,9},{12,... | collective-permute-start | bytes 122888 | tf_op jit(solution)/shard_map/ppermute | solution.py:547
  40.8 1.8 %krylov.1 = (f32[18,2,1024]{2,1,0:T(2,128)S(1)}, f32[18,2,1024]{2,1,0:T(2,128)S(1)}, f32[18,2,1024]{2,1,0:T(2,128)S(1)}, f32[8,128]{1,0:T(8,128)S(1)}) custom-call(s32[1]{0:T(128)} %bitcast.me_ref, f32[48,1024]{1,0:T(8,128)S(1)} %get-tuple-element.46.own_ref, s16[25,16,128]{2,1,0:T(8,128)(2,1)S(1)} %collective-permute-done.8.mate_ref, ...), custom_call_target="tpu_custom_call" | custom-call | tf_op jit(solution)/shard_map/krylov/pallas_call | solution.py:548
  42.6 2.7 %collective-permute-done.10.far_ref = s16[10,16,128]{2,1,0:T(8,128)(2,1)S(1)} collective-permute-done((s16[10,16,128]{2,1,0:T(8,128)(2,1)S(1)}, s16[10,16,128]{2,1,0:T(8,128)(2,1)S(1)}, u32[]{:S(2)}, u32[]{:S(2)}) %collective-permute-start.10) | collective-permute-done | bytes 40992 | tf_op jit(solution)/shard_map/ppermute | solution.py:547
  45.7 2.6 %collective-permute-start.13 = (f32[8,128]{1,0:T(8,128)S(1)}, f32[8,128]{1,0:T(8,128)S(1)}, u32[]{:S(2)}, u32[]{:S(2)}) collective-permute-start(f32[8,128]{1,0:T(8,128)S(1)} %far.1), channel_id=1, source_target_pairs={{0,6},{1,7},{2,4},{3,5},{4,2},{5,3},{6,0},{7,1},{8,14},{9,15},{10,... | collective-permute-start | bytes 12296 | tf_op jit(solution)/shard_map/ppermute | solution.py:521
  48.3 1.3 %collective-permute-start.12 = (f32[8,128]{1,0:T(8,128)S(1)}, f32[8,128]{1,0:T(8,128)S(1)}, u32[]{:S(2)}, u32[]{:S(2)}) collective-permute-start(f32[8,128]{1,0:T(8,128)S(1)} %far.1), channel_id=1, source_target_pairs={{0,4},{1,5},{2,6},{3,7},{4,0},{5,1},{6,2},{7,3},{8,12},{9,13},{10,... | collective-permute-start | bytes 12296 | tf_op jit(solution)/shard_map/ppermute | solution.py:521
  50.2 1.6 %collective-permute-done.12 = f32[8,128]{1,0:T(8,128)S(1)} collective-permute-done((f32[8,128]{1,0:T(8,128)S(1)}, f32[8,128]{1,0:T(8,128)S(1)}, u32[]{:S(2)}, u32[]{:S(2)}) %collective-permute-start.12) | collective-permute-done | bytes 4128 | tf_op jit(solution)/shard_map/ppermute | solution.py:521
  51.9 1.3 %collective-permute-done.11 = f32[8,128]{1,0:T(8,128)S(1)} collective-permute-done((f32[8,128]{1,0:T(8,128)S(1)}, f32[8,128]{1,0:T(8,128)S(1)}, u32[]{:S(2)}, u32[]{:S(2)}) %collective-permute-start.11) | collective-permute-done | bytes 4128 | tf_op jit(solution)/shard_map/ppermute | solution.py:521
  53.2 1.9 %collective-permute-start.14 = (f32[8,128]{1,0:T(8,128)S(1)}, f32[8,128]{1,0:T(8,128)S(1)}, u32[]{:S(2)}, u32[]{:S(2)}) collective-permute-start(f32[8,128]{1,0:T(8,128)S(1)} %add_add_fusion), channel_id=1, source_target_pairs={{0,8},{1,9},{2,10},{3,11},{4,12},{5,13},{6,14},{7,15},{8,0},{9,1},... | collective-permute-start | bytes 12296 | tf_op jit(solution)/shard_map/ppermute | solution.py:521
  55.1 2.6 %collective-permute-done.14 = f32[8,128]{1,0:T(8,128)S(1)} collective-permute-done((f32[8,128]{1,0:T(8,128)S(1)}, f32[8,128]{1,0:T(8,128)S(1)}, u32[]{:S(2)}, u32[]{:S(2)}) %collective-permute-start.14) | collective-permute-done | bytes 4128 | tf_op jit(solution)/shard_map/ppermute | solution.py:521
  57.7 1.2 %collective-permute-done.15.refs_1_ = f32[8,128]{1,0:T(8,128)S(1)} collective-permute-done((f32[8,128]{1,0:T(8,128)S(1)}, f32[8,128]{1,0:T(8,128)S(1)}, u32[]{:S(2)}, u32[]{:S(2)}) %collective-permute-start.15) | collective-permute-done | bytes 4128 | tf_op jit(solution)/shard_map/ppermute | solution.py:521
  58.9 0.8 %combine.1 = f32[18,2,1024]{2,1,0:T(2,128)} custom-call(f32[8,128]{1,0:T(8,128)S(1)} %add.41.refs_0_, f32[8,128]{1,0:T(8,128)S(1)} %collective-permute-done.15.refs_1_, f32[18,2,1024]{2,1,0:T(2,128)S(1)} %bitcast.7, f32[18,2,1024]{2,1,0:T(2,128)S(1)} %get-tuple-element.51.refs_3_, f32[18,2,1024]{2,1,0:T(2,128)S(1)} %get-tuple-element.52.refs_4_, ...), custom_call_target="tpu_custom_call" | custom-call | tf_op jit(solution)/shard_map/combine/pallas_call | solution.py:568
  (32 shorter events, 5.2 us)
Async XLA Ops:
  0.0 7.0 %copy-start = (f32[2,18,1024]{2,0,1:T(2,128)S(1)}, f32[2,18,1024]{2,0,1:T(2,128)}, u32[]{:S(2)}) copy-start(f32[2,18,1024]{2,0,1:T(2,128)} %param.13) | copy-start | bytes 442372
  0.0 7.0 %copy-start.2 = (f32[4,6]{1,0:T(4,128)S(1)}, f32[4,6]{1,0:T(4,128)}, u32[]{:S(2)}) copy-start(f32[4,6]{1,0:T(4,128)} %gain_ref.3) | copy-start | bytes 292
  0.0 7.0 %copy-start.3 = (s32[128]{0:T(128)S(1)}, s32[128]{0:T(128)}, u32[]{:S(2)}) copy-start(s32[128]{0:T(128)} %ids_ref.3) | copy-start | bytes 1540
  0.0 7.0 %copy-start.4 = (f32[4]{0:T(128)S(1)}, f32[4]{0:T(128)}, u32[]{:S(2)}) copy-start(f32[4]{0:T(128)} %weight_ref.3) | copy-start | bytes 52
  6.4 5.9 %copy-start.1 = (f32[8,48,512]{2,1,0:T(8,128)S(1)}, f32[8,48,512]{2,1,0:T(8,128)}, u32[]{:S(2)}) copy-start(f32[8,48,512]{2,1,0:T(8,128)} %get-tuple-element.29.refs_0_) | copy-start | bytes 2359300
  6.4 5.9 %collective-permute-start = (s16[8,13,16,128]{3,2,1,0:T(8,128)(2,1)}, s16[8,13,16,128]{3,2,1,0:T(8,128)(2,1)S(1)}, u32[]{:S(2)}, u32[]{:S(2)}) collective-permute-start(s16[8,13,16,128]{3,2,1,0:T(8,128)(2,1)} %get-tuple-element.30), channel_id=1, source_target_pairs={{0,1},{1,0},{2,3},{3,2},{4,5},{5,4},{6,7},{7,6},{8,9},{9,8},{10,11... | collective-permute-start | bytes 1277960 | tf_op jit(solution)/shard_map/ppermute | solution.py:521
  12.2 3.6 %collective-permute-start.4 = (s16[8,13,16,128]{3,2,1,0:T(8,128)(2,1)S(1)}, s16[8,13,16,128]{3,2,1,0:T(8,128)(2,1)S(1)}, u32[]{:S(2)}, u32[]{:S(2)}) collective-permute-start(s16[8,13,16,128]{3,2,1,0:T(8,128)(2,1)S(1)} %get-tuple-element.39), channel_id=1, source_target_pairs={{0,1},{1,0},{2,3},{3,2},{4,5},{5,4},{6,7},{7,6},{8,9},{9,8},{10,11... | collective-permute-start | bytes 1277960 | tf_op jit(solution)/shard_map/ppermute | solution.py:521
  12.8 8.5 %collective-permute-start.1 = (s16[4,13,16,128]{3,2,1,0:T(8,128)(2,1)S(1)}, s16[4,13,16,128]{3,2,1,0:T(8,128)(2,1)S(1)}, u32[]{:S(2)}, u32[]{:S(2)}) collective-permute-start(s16[4,13,16,128]{3,2,1,0:T(8,128)(2,1)S(1)} %get-tuple-element.32), channel_id=1, source_target_pairs={{0,2},{1,3},{2,0},{3,1},{4,6},{5,7},{6,4},{7,5},{8,10},{9,11},{10,... | collective-permute-start | bytes 638984 | tf_op jit(solution)/shard_map/ppermute | solution.py:521
  16.3 7.3 %collective-permute-start.5 = (s16[4,13,16,128]{3,2,1,0:T(8,128)(2,1)S(1)}, s16[4,13,16,128]{3,2,1,0:T(8,128)(2,1)S(1)}, u32[]{:S(2)}, u32[]{:S(2)}) collective-permute-start(s16[4,13,16,128]{3,2,1,0:T(8,128)(2,1)S(1)} %get-tuple-element.41), channel_id=1, source_target_pairs={{0,4},{1,5},{2,6},{3,7},{4,0},{5,1},{6,2},{7,3},{8,12},{9,13},{10,... | collective-permute-start | bytes 638984 | tf_op jit(solution)/shard_map/ppermute | solution.py:521
  21.7 4.8 %collective-permute-start.2 = (s16[2,13,16,128]{3,2,1,0:T(8,128)(2,1)S(1)}, s16[2,13,16,128]{3,2,1,0:T(8,128)(2,1)S(1)}, u32[]{:S(2)}, u32[]{:S(2)}) collective-permute-start(s16[2,13,16,128]{3,2,1,0:T(8,128)(2,1)S(1)} %get-tuple-element.34), channel_id=1, source_target_pairs={{0,4},{1,5},{2,6},{3,7},{4,0},{5,1},{6,2},{7,3},{8,12},{9,13},{10,... | collective-permute-start | bytes 319496 | tf_op jit(solution)/shard_map/ppermute | solution.py:521
  23.9 5.8 %collective-permute-start.6 = (s16[2,13,16,128]{3,2,1,0:T(8,128)(2,1)S(1)}, s16[2,13,16,128]{3,2,1,0:T(8,128)(2,1)S(1)}, u32[]{:S(2)}, u32[]{:S(2)}) collective-permute-start(s16[2,13,16,128]{3,2,1,0:T(8,128)(2,1)S(1)} %get-tuple-element.43), channel_id=1, source_target_pairs={{0,2},{1,3},{2,0},{3,1},{4,6},{5,7},{6,4},{7,5},{8,10},{9,11},{10,... | collective-permute-start | bytes 319496 | tf_op jit(solution)/shard_map/ppermute | solution.py:521
  26.8 5.6 %collective-permute-start.3 = (s16[1,13,16,128]{3,2,1,0:T(8,128)(2,1)S(1)}, s16[1,13,16,128]{3,2,1,0:T(8,128)(2,1)S(1)}, u32[]{:S(2)}, u32[]{:S(2)}) collective-permute-start(s16[1,13,16,128]{3,2,1,0:T(8,128)(2,1)S(1)} %get-tuple-element.36), channel_id=1, source_target_pairs={{0,8},{1,9},{2,10},{3,11},{4,12},{5,13},{6,14},{7,15},{8,0},{9,1},... | collective-permute-start | bytes 159752 | tf_op jit(solution)/shard_map/ppermute | solution.py:521
  30.0 5.1 %collective-permute-start.7 = (s16[1,13,16,128]{3,2,1,0:T(8,128)(2,1)S(1)}, s16[1,13,16,128]{3,2,1,0:T(8,128)(2,1)S(1)}, u32[]{:S(2)}, u32[]{:S(2)}) collective-permute-start(s16[1,13,16,128]{3,2,1,0:T(8,128)(2,1)S(1)} %get-tuple-element.45), channel_id=1, source_target_pairs={{0,8},{1,9},{2,10},{3,11},{4,12},{5,13},{6,14},{7,15},{8,0},{9,1},... | collective-permute-start | bytes 159752 | tf_op jit(solution)/shard_map/ppermute | solution.py:521
  35.9 4.9 %collective-permute-start.9 = (s16[25,16,128]{2,1,0:T(8,128)(2,1)S(1)}, s16[25,16,128]{2,1,0:T(8,128)(2,1)S(1)}, u32[]{:S(2)}, u32[]{:S(2)}) collective-permute-start(s16[25,16,128]{2,1,0:T(8,128)(2,1)S(1)} %bitcast.8), channel_id=1, source_target_pairs={{1,2},{3,4},{5,6},{7,8},{9,10},{11,12},{13,14},{2,1},{4,3},{6,5},{... | collective-permute-start | bytes 307208 | tf_op jit(solution)/shard_map/ppermute | solution.py:546
  36.5 4.2 %collective-permute-start.8 = (s16[25,16,128]{2,1,0:T(8,128)(2,1)S(1)}, s16[25,16,128]{2,1,0:T(8,128)(2,1)S(1)}, u32[]{:S(2)}, u32[]{:S(2)}) collective-permute-start(s16[25,16,128]{2,1,0:T(8,128)(2,1)S(1)} %bitcast.9), channel_id=1, source_target_pairs={{0,1},{1,0},{2,3},{3,2},{4,5},{5,4},{6,7},{7,6},{8,9},{9,8},{10,11... | collective-permute-start | bytes 307208 | tf_op jit(solution)/shard_map/ppermute | solution.py:521
  39.5 5.9 %collective-permute-start.10 = (s16[10,16,128]{2,1,0:T(8,128)(2,1)S(1)}, s16[10,16,128]{2,1,0:T(8,128)(2,1)S(1)}, u32[]{:S(2)}, u32[]{:S(2)}) collective-permute-start(s16[10,16,128]{2,1,0:T(8,128)(2,1)S(1)} %get-tuple-element.50), channel_id=1, source_target_pairs={{2,0},{3,1},{4,2},{5,3},{6,4},{7,5},{8,6},{9,7},{10,8},{11,9},{12,... | collective-permute-start | bytes 122888 | tf_op jit(solution)/shard_map/ppermute | solution.py:547
  45.7 4.6 %collective-permute-start.13 = (f32[8,128]{1,0:T(8,128)S(1)}, f32[8,128]{1,0:T(8,128)S(1)}, u32[]{:S(2)}, u32[]{:S(2)}) collective-permute-start(f32[8,128]{1,0:T(8,128)S(1)} %far.1), channel_id=1, source_target_pairs={{0,6},{1,7},{2,4},{3,5},{4,2},{5,3},{6,0},{7,1},{8,14},{9,15},{10,... | collective-permute-start | bytes 12296 | tf_op jit(solution)/shard_map/ppermute | solution.py:521
  48.3 3.6 %collective-permute-start.12 = (f32[8,128]{1,0:T(8,128)S(1)}, f32[8,128]{1,0:T(8,128)S(1)}, u32[]{:S(2)}, u32[]{:S(2)}) collective-permute-start(f32[8,128]{1,0:T(8,128)S(1)} %far.1), channel_id=1, source_target_pairs={{0,4},{1,5},{2,6},{3,7},{4,0},{5,1},{6,2},{7,3},{8,12},{9,13},{10,... | collective-permute-start | bytes 12296 | tf_op jit(solution)/shard_map/ppermute | solution.py:521
  49.6 3.6 %collective-permute-start.11 = (f32[8,128]{1,0:T(8,128)S(1)}, f32[8,128]{1,0:T(8,128)S(1)}, u32[]{:S(2)}, u32[]{:S(2)}) collective-permute-start(f32[8,128]{1,0:T(8,128)S(1)} %far.1), channel_id=1, source_target_pairs={{0,2},{1,3},{2,0},{3,1},{4,6},{5,7},{6,4},{7,5},{8,10},{9,11},{10,... | collective-permute-start | bytes 12296 | tf_op jit(solution)/shard_map/ppermute | solution.py:521
  53.2 4.5 %collective-permute-start.14 = (f32[8,128]{1,0:T(8,128)S(1)}, f32[8,128]{1,0:T(8,128)S(1)}, u32[]{:S(2)}, u32[]{:S(2)}) collective-permute-start(f32[8,128]{1,0:T(8,128)S(1)} %add_add_fusion), channel_id=1, source_target_pairs={{0,8},{1,9},{2,10},{3,11},{4,12},{5,13},{6,14},{7,15},{8,0},{9,1},... | collective-permute-start | bytes 12296 | tf_op jit(solution)/shard_map/ppermute | solution.py:521
  57.7 1.2 %collective-permute-start.15 = (f32[8,128]{1,0:T(8,128)S(1)}, f32[8,128]{1,0:T(8,128)S(1)}, u32[]{:S(2)}, u32[]{:S(2)}) collective-permute-start(f32[8,128]{1,0:T(8,128)S(1)} %add.41.refs_0_), channel_id=1, source_target_pairs={{0,1},{1,0},{2,3},{3,2},{4,5},{5,4},{6,7},{7,6},{8,9},{9,8},{10,11... | collective-permute-start | bytes 12296 | tf_op jit(solution)/shard_map/ppermute | solution.py:521

commit v5 on v3

--- a/solution.py
+++ b/solution.py
@@ -449,15 +449,18 @@
     gram_ref[...] = gram
 
 
-def far_kernel(gram_ref, two_ref, far_ref, out_ref):
+def far_kernel(me_ref, gram_ref, two_ref, mate_ref, far_ref, out_ref):
     obs_count, _, cols = two_ref.shape
     tiles = cols // LANES
     rest = obs_count - 16
+    core0 = me_ref[0] % 2 == 0
+    from_mate = unpack(lambda place: mate_ref[place], 2, tiles)
     factors = factors_of(far_ref[0], 2)
     left = jnp.concatenate([as_float(far_ref[t]) for t in range(1 + tiles, far_ref.shape[0])], axis=0)
     total = jnp.zeros((obs_count, LANES), jnp.float32)
     for c in range(tiles):
-        far = jnp.concatenate([as_float(far_ref[1 + c]) * factors[0], left[rest * c : rest * (c + 1)] * factors[1][0:rest]], axis=0)
+        rows = as_float(far_ref[1 + c]) * factors[0], left[rest * c : rest * (c + 1)] * factors[1][0:rest]
+        far = jnp.where(core0, from_mate[c][0:obs_count], jnp.concatenate(rows, axis=0))
         mine = jnp.concatenate([two_ref[e, 1:2, c * LANES : (c + 1) * LANES] for e in range(obs_count)], axis=0)
         total = total + far * mine
     part = (-2.0 * (GAIN * SMOOTH_PULL) ** 3) * jnp.sum(total)
@@ -544,7 +547,8 @@
     mate = swap(msg, 0)
     border = [(i, i + 1) for i in range(1, count - 1, 2)]
     across = lax.ppermute(msg, "rows", border + [(target, source) for source, target in border])
-    far = lax.ppermute(first, "rows", [(i + 2, i) for i in range(count - 2)])
+    far = lax.ppermute(first, "rows", [(i + 2, i) for i in range(1, count - 2, 2)])
+    beside = lax.ppermute(across[: 1 + 2 * tiles], "rows", [(i + 1, i) for i in range(0, count, 2)])
     zero, one, two, gram = pl.pallas_call(
         functools.partial(krylov_kernel, total_rows=total_rows, rows_here=rows_here),
         in_specs=[smem, vmem, vmem, vmem],
@@ -557,8 +561,8 @@
 
     grams = [
         pl.pallas_call(
-            far_kernel, in_specs=[vmem] * 3, out_specs=vmem, out_shape=f32(8, LANES), compiler_params=params, name="far"
-        )(gram, two, far)
+            far_kernel, in_specs=[smem] + [vmem] * 4, out_specs=vmem, out_shape=f32(8, LANES), compiler_params=params, name="far"
+        )(me, gram, two, beside, far)
     ]
     for bit in range(0, count.bit_length() - 1, 2):
         masks = [mask << bit for mask in (1, 2, 3) if mask << bit < count]

time: 57.9 us -> 63.2 us (1.092)
  starting transfers between devices: 25.3 us -> 31.6 us
  waiting for transfers between devices: 14.7 us -> 13.6 us
    ppermute x15, starting transfers between devices: 23.3 us -> 29 us  [on_device(): lax.ppermute(x, 'rows', [(i, i ^ mask) for i in range(count)])]
    ppermute x1 -> x2, waiting for transfers between devices: 2.74 us -> 0.8 us  [the longest x1 0.8 us: on_device(): lax.ppermute(across[:1 + 2 * tiles], 'rows', [(i + 1, i) for i in range(0...]
    ppermute x15, waiting for transfers between devices: 11.9 us -> 12.8 us  [on_device(): lax.ppermute(x, 'rows', [(i, i ^ mask) for i in range(count)])]
    ppermute x1 -> x2, starting transfers between devices: 1.28 us -> 1.96 us  [the longest x1 1.29 us: on_device(): lax.ppermute(across[:1 + 2 * tiles], 'rows', [(i + 1, i) for i in range(0...]
  transfers between devices with their start and end apart: 17 -> 18, of which waited for: 9 -> 10; matrix products, arithmetic and copies ran while one was open for 0% -> 0% of each run, Pallas kernels for 16% -> 15%
where the time goes in v5:
time: 63.2 us; the launch traced here: 63.1 us
  starting transfers between devices  31.6 us (50%)
  Pallas kernels  17.6 us (28%)
  waiting for transfers between devices  13.6 us (22%)
    ppermute x15, starting transfers between devices, on_device(): lax.ppermute(x, 'rows', [(i, i ^ mask) for i in range(count)])  29 us
    ppermute x15, waiting for transfers between devices, on_device(): lax.ppermute(x, 'rows', [(i, i ^ mask) for i in range(count)])  12.8 us
    pallas_call x2, Pallas kernels, partial_sums(): pl.pallas_call(functools.partial(sums_kernel, scale=scale, rows_here=rows...  11.7 us
    pallas_call x6, Pallas kernels, add_split(): pl.pallas_call(functools.partial(add_split_kernel, place=place), in_specs...  2.21 us
    pallas_call x1, Pallas kernels, on_device(): pl.pallas_call(functools.partial(krylov_kernel, total_rows=total_rows, ro...  1.83 us
    ppermute x1, starting transfers between devices, on_device(): lax.ppermute(across[:1 + 2 * tiles], 'rows', [(i + 1, i) for i in range(0...  1.29 us
  transfers between devices with their start and end apart: 18, of which 10 were waited for; matrix products, arithmetic and copies ran while one was open for 0% of the time, Pallas kernels for 15%

profile of v5, /device:TPU:0, one launch (start us, length us, event | category | flops | bytes accessed | tf_op | source)
XLA Modules:
  0.0 63.1 jit_solution(5650306367848678155)
XLA Ops:
  0.0 6.4 %partial_sums.2 = (f32[8,48,512]{2,1,0:T(8,128)}, s16[8,13,16,128]{3,2,1,0:T(8,128)(2,1)}) custom-call(s32[1]{0:T(128)} %bitcast.me_ref, s32[128]{0:T(128)} %ids_ref.3, f32[4,6]{1,0:T(4,128)} %gain_ref.3, f32[4]{0:T(128)} %weight_ref.3, bf16[8,6,32,1024]{3,2,1,0:T(8,128)(2,1)} %reflect_hbm.3, s32[8,32,1024]{2,1,0:T(8,128)} %conf_hbm.3, ...), custom_call_target="tpu_custom_call" | custom-call | tf_op jit(solution)/shard_map/partial_sums/pallas_call | solution.py:243
  7.0 5.2 %partial_sums.3 = (f32[8,48,512]{2,1,0:T(8,128)S(1)}, s16[8,13,16,128]{3,2,1,0:T(8,128)(2,1)S(1)}) custom-call(s32[1]{0:T(128)} %bitcast.me_ref, s32[128]{0:T(128)S(1)} %copy-done.3, f32[4,6]{1,0:T(4,128)S(1)} %copy-done.2, f32[4]{0:T(128)S(1)} %copy-done.4, bf16[8,6,32,1024]{3,2,1,0:T(8,128)(2,1)} %reflect_hbm.3, s32[8,32,1024]{2,1,0:T(8,128)} %conf_hbm.3, ...), custom_call_target="tpu_custom_call" | custom-call | tf_op jit(solution)/shard_map/partial_sums/pallas_call | solution.py:243
  12.8 3.0 %collective-permute-start.1 = (s16[4,13,16,128]{3,2,1,0:T(8,128)(2,1)S(1)}, s16[4,13,16,128]{3,2,1,0:T(8,128)(2,1)S(1)}, u32[]{:S(2)}, u32[]{:S(2)}) collective-permute-start(s16[4,13,16,128]{3,2,1,0:T(8,128)(2,1)S(1)} %get-tuple-element.32), channel_id=1, source_target_pairs={{0,2},{1,3},{2,0},{3,1},{4,6},{5,7},{6,4},{7,5},{8,10},{9,11},{10,... | collective-permute-start | bytes 638984 | tf_op jit(solution)/shard_map/ppermute | solution.py:524
  16.3 1.6 %collective-permute-start.5 = (s16[4,13,16,128]{3,2,1,0:T(8,128)(2,1)S(1)}, s16[4,13,16,128]{3,2,1,0:T(8,128)(2,1)S(1)}, u32[]{:S(2)}, u32[]{:S(2)}) collective-permute-start(s16[4,13,16,128]{3,2,1,0:T(8,128)(2,1)S(1)} %get-tuple-element.41), channel_id=1, source_target_pairs={{0,4},{1,5},{2,6},{3,7},{4,0},{5,1},{6,2},{7,3},{8,12},{9,13},{10,... | collective-permute-start | bytes 638984 | tf_op jit(solution)/shard_map/ppermute | solution.py:524
  17.9 3.4 %collective-permute-done.1.refs_1_ = s16[4,13,16,128]{3,2,1,0:T(8,128)(2,1)S(1)} collective-permute-done((s16[4,13,16,128]{3,2,1,0:T(8,128)(2,1)S(1)}, s16[4,13,16,128]{3,2,1,0:T(8,128)(2,1)S(1)}, u32[]{:S(2)}, u32[]{:S(2)}) %collective-permute-start.1) | collective-permute-done | bytes 213024 | tf_op jit(solution)/shard_map/ppermute | solution.py:524
  21.7 1.9 %collective-permute-start.2 = (s16[2,13,16,128]{3,2,1,0:T(8,128)(2,1)S(1)}, s16[2,13,16,128]{3,2,1,0:T(8,128)(2,1)S(1)}, u32[]{:S(2)}, u32[]{:S(2)}) collective-permute-start(s16[2,13,16,128]{3,2,1,0:T(8,128)(2,1)S(1)} %get-tuple-element.34), channel_id=1, source_target_pairs={{0,4},{1,5},{2,6},{3,7},{4,0},{5,1},{6,2},{7,3},{8,12},{9,13},{10,... | collective-permute-start | bytes 319496 | tf_op jit(solution)/shard_map/ppermute | solution.py:524
  24.0 1.6 %collective-permute-start.6 = (s16[2,13,16,128]{3,2,1,0:T(8,128)(2,1)S(1)}, s16[2,13,16,128]{3,2,1,0:T(8,128)(2,1)S(1)}, u32[]{:S(2)}, u32[]{:S(2)}) collective-permute-start(s16[2,13,16,128]{3,2,1,0:T(8,128)(2,1)S(1)} %get-tuple-element.43), channel_id=1, source_target_pairs={{0,2},{1,3},{2,0},{3,1},{4,6},{5,7},{6,4},{7,5},{8,10},{9,11},{10,... | collective-permute-start | bytes 319496 | tf_op jit(solution)/shard_map/ppermute | solution.py:524
  25.5 0.9 %collective-permute-done.2.refs_1_ = s16[2,13,16,128]{3,2,1,0:T(8,128)(2,1)S(1)} collective-permute-done((s16[2,13,16,128]{3,2,1,0:T(8,128)(2,1)S(1)}, s16[2,13,16,128]{3,2,1,0:T(8,128)(2,1)S(1)}, u32[]{:S(2)}, u32[]{:S(2)}) %collective-permute-start.2) | collective-permute-done | bytes 106528 | tf_op jit(solution)/shard_map/ppermute | solution.py:524
  26.8 2.9 %collective-permute-start.3 = (s16[1,13,16,128]{3,2,1,0:T(8,128)(2,1)S(1)}, s16[1,13,16,128]{3,2,1,0:T(8,128)(2,1)S(1)}, u32[]{:S(2)}, u32[]{:S(2)}) collective-permute-start(s16[1,13,16,128]{3,2,1,0:T(8,128)(2,1)S(1)} %get-tuple-element.36), channel_id=1, source_target_pairs={{0,8},{1,9},{2,10},{3,11},{4,12},{5,13},{6,14},{7,15},{8,0},{9,1},... | collective-permute-start | bytes 159752 | tf_op jit(solution)/shard_map/ppermute | solution.py:524
  30.0 1.7 %collective-permute-start.7 = (s16[1,13,16,128]{3,2,1,0:T(8,128)(2,1)S(1)}, s16[1,13,16,128]{3,2,1,0:T(8,128)(2,1)S(1)}, u32[]{:S(2)}, u32[]{:S(2)}) collective-permute-start(s16[1,13,16,128]{3,2,1,0:T(8,128)(2,1)S(1)} %get-tuple-element.45), channel_id=1, source_target_pairs={{0,8},{1,9},{2,10},{3,11},{4,12},{5,13},{6,14},{7,15},{8,0},{9,1},... | collective-permute-start | bytes 159752 | tf_op jit(solution)/shard_map/ppermute | solution.py:524
  31.7 0.7 %collective-permute-done.3.refs_1_ = s16[1,13,16,128]{3,2,1,0:T(8,128)(2,1)S(1)} collective-permute-done((s16[1,13,16,128]{3,2,1,0:T(8,128)(2,1)S(1)}, s16[1,13,16,128]{3,2,1,0:T(8,128)(2,1)S(1)}, u32[]{:S(2)}, u32[]{:S(2)}) %collective-permute-start.3) | collective-permute-done | bytes 53280 | tf_op jit(solution)/shard_map/ppermute | solution.py:524
  32.5 2.7 %collective-permute-done.7.refs_3_ = s16[1,13,16,128]{3,2,1,0:T(8,128)(2,1)S(1)} collective-permute-done((s16[1,13,16,128]{3,2,1,0:T(8,128)(2,1)S(1)}, s16[1,13,16,128]{3,2,1,0:T(8,128)(2,1)S(1)}, u32[]{:S(2)}, u32[]{:S(2)}) %collective-permute-start.7) | collective-permute-done | bytes 53280 | tf_op jit(solution)/shard_map/ppermute | solution.py:524
  36.6 2.9 %collective-permute-start.8 = (s16[25,16,128]{2,1,0:T(8,128)(2,1)S(1)}, s16[25,16,128]{2,1,0:T(8,128)(2,1)S(1)}, u32[]{:S(2)}, u32[]{:S(2)}) collective-permute-start(s16[25,16,128]{2,1,0:T(8,128)(2,1)S(1)} %bitcast.9), channel_id=1, source_target_pairs={{0,1},{1,0},{2,3},{3,2},{4,5},{5,4},{6,7},{7,6},{8,9},{9,8},{10,11... | collective-permute-start | bytes 307208 | tf_op jit(solution)/shard_map/ppermute | solution.py:524
  39.5 1.3 %collective-permute-start.10 = (s16[17,16,128]{2,1,0:T(8,128)(2,1)S(1)}, s16[17,16,128]{2,1,0:T(8,128)(2,1)S(1)}, u32[]{:S(2)}, u32[]{:S(2)}) collective-permute-start(s16[17,16,128]{2,1,0:T(8,128)(2,1)S(1)} %slice.4), channel_id=1, source_target_pairs={{1,0},{3,2},{5,4},{7,6},{9,8},{11,10},{13,12},{15,14},{17,16},{19,... | collective-permute-start | bytes 208904 | tf_op jit(solution)/shard_map/ppermute | solution.py:551
  41.5 1.8 %krylov.1 = (f32[18,2,1024]{2,1,0:T(2,128)S(1)}, f32[18,2,1024]{2,1,0:T(2,128)S(1)}, f32[18,2,1024]{2,1,0:T(2,128)S(1)}, f32[8,128]{1,0:T(8,128)S(1)}) custom-call(s32[1]{0:T(128)} %bitcast.me_ref, f32[48,1024]{1,0:T(8,128)S(1)} %get-tuple-element.46.own_ref, s16[25,16,128]{2,1,0:T(8,128)(2,1)S(1)} %collective-permute-done.8.mate_ref, ...), custom_call_target="tpu_custom_call" | custom-call | tf_op jit(solution)/shard_map/krylov/pallas_call | solution.py:552
  43.3 0.8 %collective-permute-done.10.mate_ref = s16[17,16,128]{2,1,0:T(8,128)(2,1)S(1)} collective-permute-done((s16[17,16,128]{2,1,0:T(8,128)(2,1)S(1)}, s16[17,16,128]{2,1,0:T(8,128)(2,1)S(1)}, u32[]{:S(2)}, u32[]{:S(2)}) %collective-permute-start.10) | collective-permute-done | bytes 69664 | tf_op jit(solution)/shard_map/ppermute | solution.py:551
  44.4 8.1 %collective-permute-start.14 = (f32[8,128]{1,0:T(8,128)S(1)}, f32[8,128]{1,0:T(8,128)S(1)}, u32[]{:S(2)}, u32[]{:S(2)}) collective-permute-start(f32[8,128]{1,0:T(8,128)S(1)} %far.1), channel_id=1, source_target_pairs={{0,3},{1,2},{2,1},{3,0},{4,7},{5,6},{6,5},{7,4},{8,11},{9,10},{10,... | collective-permute-start | bytes 12296 | tf_op jit(solution)/shard_map/ppermute | solution.py:524
  52.7 1.1 %collective-permute-done.14 = f32[8,128]{1,0:T(8,128)S(1)} collective-permute-done((f32[8,128]{1,0:T(8,128)S(1)}, f32[8,128]{1,0:T(8,128)S(1)}, u32[]{:S(2)}, u32[]{:S(2)}) %collective-permute-start.14) | collective-permute-done | bytes 4128 | tf_op jit(solution)/shard_map/ppermute | solution.py:524
  53.9 2.3 %collective-permute-done.13 = f32[8,128]{1,0:T(8,128)S(1)} collective-permute-done((f32[8,128]{1,0:T(8,128)S(1)}, f32[8,128]{1,0:T(8,128)S(1)}, u32[]{:S(2)}, u32[]{:S(2)}) %collective-permute-start.13) | collective-permute-done | bytes 4128 | tf_op jit(solution)/shard_map/ppermute | solution.py:524
  56.1 1.2 %collective-permute-start.17 = (f32[8,128]{1,0:T(8,128)S(1)}, f32[8,128]{1,0:T(8,128)S(1)}, u32[]{:S(2)}, u32[]{:S(2)}) collective-permute-start(f32[8,128]{1,0:T(8,128)S(1)} %add_add_fusion.refs_0_), channel_id=1, source_target_pairs={{0,12},{1,13},{2,14},{3,15},{4,8},{5,9},{6,10},{7,11},{8,4},{9,5},... | collective-permute-start | bytes 12296 | tf_op jit(solution)/shard_map/ppermute | solution.py:524
  57.4 1.1 %collective-permute-start.16 = (f32[8,128]{1,0:T(8,128)S(1)}, f32[8,128]{1,0:T(8,128)S(1)}, u32[]{:S(2)}, u32[]{:S(2)}) collective-permute-start(f32[8,128]{1,0:T(8,128)S(1)} %add_add_fusion.refs_0_), channel_id=1, source_target_pairs={{0,8},{1,9},{2,10},{3,11},{4,12},{5,13},{6,14},{7,15},{8,0},{9,1},... | collective-permute-start | bytes 12296 | tf_op jit(solution)/shard_map/ppermute | solution.py:524
  58.4 2.2 %collective-permute-start.15 = (f32[8,128]{1,0:T(8,128)S(1)}, f32[8,128]{1,0:T(8,128)S(1)}, u32[]{:S(2)}, u32[]{:S(2)}) collective-permute-start(f32[8,128]{1,0:T(8,128)S(1)} %add_add_fusion.refs_0_), channel_id=1, source_target_pairs={{0,4},{1,5},{2,6},{3,7},{4,0},{5,1},{6,2},{7,3},{8,12},{9,13},{10,... | collective-permute-start | bytes 12296 | tf_op jit(solution)/shard_map/ppermute | solution.py:524
  60.6 1.0 %collective-permute-done.17.refs_3_ = f32[8,128]{1,0:T(8,128)S(1)} collective-permute-done((f32[8,128]{1,0:T(8,128)S(1)}, f32[8,128]{1,0:T(8,128)S(1)}, u32[]{:S(2)}, u32[]{:S(2)}) %collective-permute-start.17) | collective-permute-done | bytes 4128 | tf_op jit(solution)/shard_map/ppermute | solution.py:524
  62.2 0.9 %combine.1 = f32[18,2,1024]{2,1,0:T(2,128)} custom-call(f32[8,128]{1,0:T(8,128)S(1)} %add_add_fusion.refs_0_, f32[8,128]{1,0:T(8,128)S(1)} %collective-permute-done.15.refs_1_, f32[8,128]{1,0:T(8,128)S(1)} %collective-permute-done.16.refs_2_, f32[8,128]{1,0:T(8,128)S(1)} %collective-permute-done.17.refs_3_, f32[18,2,1024]{2,1,0:T(2,128)S(1)} %bitcast.7, ...), custom_call_target="tpu_custom_call" | custom-call | tf_op jit(solution)/shard_map/combine/pallas_call | solution.py:571
  (36 shorter events, 6.0 us)
Async XLA Ops:
  0.0 7.0 %copy-start = (f32[2,18,1024]{2,0,1:T(2,128)S(1)}, f32[2,18,1024]{2,0,1:T(2,128)}, u32[]{:S(2)}) copy-start(f32[2,18,1024]{2,0,1:T(2,128)} %param.13) | copy-start | bytes 442372
  0.0 7.0 %copy-start.2 = (f32[4,6]{1,0:T(4,128)S(1)}, f32[4,6]{1,0:T(4,128)}, u32[]{:S(2)}) copy-start(f32[4,6]{1,0:T(4,128)} %gain_ref.3) | copy-start | bytes 292
  0.0 7.0 %copy-start.3 = (s32[128]{0:T(128)S(1)}, s32[128]{0:T(128)}, u32[]{:S(2)}) copy-start(s32[128]{0:T(128)} %ids_ref.3) | copy-start | bytes 1540
  0.0 7.0 %copy-start.4 = (f32[4]{0:T(128)S(1)}, f32[4]{0:T(128)}, u32[]{:S(2)}) copy-start(f32[4]{0:T(128)} %weight_ref.3) | copy-start | bytes 52
  6.5 5.9 %copy-start.1 = (f32[8,48,512]{2,1,0:T(8,128)S(1)}, f32[8,48,512]{2,1,0:T(8,128)}, u32[]{:S(2)}) copy-start(f32[8,48,512]{2,1,0:T(8,128)} %get-tuple-element.29.refs_0_) | copy-start | bytes 2359300
  6.5 5.9 %collective-permute-start = (s16[8,13,16,128]{3,2,1,0:T(8,128)(2,1)}, s16[8,13,16,128]{3,2,1,0:T(8,128)(2,1)S(1)}, u32[]{:S(2)}, u32[]{:S(2)}) collective-permute-start(s16[8,13,16,128]{3,2,1,0:T(8,128)(2,1)} %get-tuple-element.30), channel_id=1, source_target_pairs={{0,1},{1,0},{2,3},{3,2},{4,5},{5,4},{6,7},{7,6},{8,9},{9,8},{10,11... | collective-permute-start | bytes 1277960 | tf_op jit(solution)/shard_map/ppermute | solution.py:524
  12.3 3.6 %collective-permute-start.4 = (s16[8,13,16,128]{3,2,1,0:T(8,128)(2,1)S(1)}, s16[8,13,16,128]{3,2,1,0:T(8,128)(2,1)S(1)}, u32[]{:S(2)}, u32[]{:S(2)}) collective-permute-start(s16[8,13,16,128]{3,2,1,0:T(8,128)(2,1)S(1)} %get-tuple-element.39), channel_id=1, source_target_pairs={{0,1},{1,0},{2,3},{3,2},{4,5},{5,4},{6,7},{7,6},{8,9},{9,8},{10,11... | collective-permute-start | bytes 1277960 | tf_op jit(solution)/shard_map/ppermute | solution.py:524
  12.8 8.5 %collective-permute-start.1 = (s16[4,13,16,128]{3,2,1,0:T(8,128)(2,1)S(1)}, s16[4,13,16,128]{3,2,1,0:T(8,128)(2,1)S(1)}, u32[]{:S(2)}, u32[]{:S(2)}) collective-permute-start(s16[4,13,16,128]{3,2,1,0:T(8,128)(2,1)S(1)} %get-tuple-element.32), channel_id=1, source_target_pairs={{0,2},{1,3},{2,0},{3,1},{4,6},{5,7},{6,4},{7,5},{8,10},{9,11},{10,... | collective-permute-start | bytes 638984 | tf_op jit(solution)/shard_map/ppermute | solution.py:524
  16.3 7.3 %collective-permute-start.5 = (s16[4,13,16,128]{3,2,1,0:T(8,128)(2,1)S(1)}, s16[4,13,16,128]{3,2,1,0:T(8,128)(2,1)S(1)}, u32[]{:S(2)}, u32[]{:S(2)}) collective-permute-start(s16[4,13,16,128]{3,2,1,0:T(8,128)(2,1)S(1)} %get-tuple-element.41), channel_id=1, source_target_pairs={{0,4},{1,5},{2,6},{3,7},{4,0},{5,1},{6,2},{7,3},{8,12},{9,13},{10,... | collective-permute-start | bytes 638984 | tf_op jit(solution)/shard_map/ppermute | solution.py:524
  21.7 4.8 %collective-permute-start.2 = (s16[2,13,16,128]{3,2,1,0:T(8,128)(2,1)S(1)}, s16[2,13,16,128]{3,2,1,0:T(8,128)(2,1)S(1)}, u32[]{:S(2)}, u32[]{:S(2)}) collective-permute-start(s16[2,13,16,128]{3,2,1,0:T(8,128)(2,1)S(1)} %get-tuple-element.34), channel_id=1, source_target_pairs={{0,4},{1,5},{2,6},{3,7},{4,0},{5,1},{6,2},{7,3},{8,12},{9,13},{10,... | collective-permute-start | bytes 319496 | tf_op jit(solution)/shard_map/ppermute | solution.py:524
  24.0 5.8 %collective-permute-start.6 = (s16[2,13,16,128]{3,2,1,0:T(8,128)(2,1)S(1)}, s16[2,13,16,128]{3,2,1,0:T(8,128)(2,1)S(1)}, u32[]{:S(2)}, u32[]{:S(2)}) collective-permute-start(s16[2,13,16,128]{3,2,1,0:T(8,128)(2,1)S(1)} %get-tuple-element.43), channel_id=1, source_target_pairs={{0,2},{1,3},{2,0},{3,1},{4,6},{5,7},{6,4},{7,5},{8,10},{9,11},{10,... | collective-permute-start | bytes 319496 | tf_op jit(solution)/shard_map/ppermute | solution.py:524
  26.8 5.6 %collective-permute-start.3 = (s16[1,13,16,128]{3,2,1,0:T(8,128)(2,1)S(1)}, s16[1,13,16,128]{3,2,1,0:T(8,128)(2,1)S(1)}, u32[]{:S(2)}, u32[]{:S(2)}) collective-permute-start(s16[1,13,16,128]{3,2,1,0:T(8,128)(2,1)S(1)} %get-tuple-element.36), channel_id=1, source_target_pairs={{0,8},{1,9},{2,10},{3,11},{4,12},{5,13},{6,14},{7,15},{8,0},{9,1},... | collective-permute-start | bytes 159752 | tf_op jit(solution)/shard_map/ppermute | solution.py:524
  30.0 5.1 %collective-permute-start.7 = (s16[1,13,16,128]{3,2,1,0:T(8,128)(2,1)S(1)}, s16[1,13,16,128]{3,2,1,0:T(8,128)(2,1)S(1)}, u32[]{:S(2)}, u32[]{:S(2)}) collective-permute-start(s16[1,13,16,128]{3,2,1,0:T(8,128)(2,1)S(1)} %get-tuple-element.45), channel_id=1, source_target_pairs={{0,8},{1,9},{2,10},{3,11},{4,12},{5,13},{6,14},{7,15},{8,0},{9,1},... | collective-permute-start | bytes 159752 | tf_op jit(solution)/shard_map/ppermute | solution.py:524
  35.9 3.6 %collective-permute-start.9 = (s16[25,16,128]{2,1,0:T(8,128)(2,1)S(1)}, s16[25,16,128]{2,1,0:T(8,128)(2,1)S(1)}, u32[]{:S(2)}, u32[]{:S(2)}) collective-permute-start(s16[25,16,128]{2,1,0:T(8,128)(2,1)S(1)} %bitcast.8), channel_id=1, source_target_pairs={{1,2},{3,4},{5,6},{7,8},{9,10},{11,12},{13,14},{2,1},{4,3},{6,5},{... | collective-permute-start | bytes 307208 | tf_op jit(solution)/shard_map/ppermute | solution.py:549
  36.6 4.9 %collective-permute-start.8 = (s16[25,16,128]{2,1,0:T(8,128)(2,1)S(1)}, s16[25,16,128]{2,1,0:T(8,128)(2,1)S(1)}, u32[]{:S(2)}, u32[]{:S(2)}) collective-permute-start(s16[25,16,128]{2,1,0:T(8,128)(2,1)S(1)} %bitcast.9), channel_id=1, source_target_pairs={{0,1},{1,0},{2,3},{3,2},{4,5},{5,4},{6,7},{7,6},{8,9},{9,8},{10,11... | collective-permute-start | bytes 307208 | tf_op jit(solution)/shard_map/ppermute | solution.py:524
  39.5 4.6 %collective-permute-start.10 = (s16[17,16,128]{2,1,0:T(8,128)(2,1)S(1)}, s16[17,16,128]{2,1,0:T(8,128)(2,1)S(1)}, u32[]{:S(2)}, u32[]{:S(2)}) collective-permute-start(s16[17,16,128]{2,1,0:T(8,128)(2,1)S(1)} %slice.4), channel_id=1, source_target_pairs={{1,0},{3,2},{5,4},{7,6},{9,8},{11,10},{13,12},{15,14},{17,16},{19,... | collective-permute-start | bytes 208904 | tf_op jit(solution)/shard_map/ppermute | solution.py:551
  40.8 2.5 %collective-permute-start.11 = (s16[10,16,128]{2,1,0:T(8,128)(2,1)S(1)}, s16[10,16,128]{2,1,0:T(8,128)(2,1)S(1)}, u32[]{:S(2)}, u32[]{:S(2)}) collective-permute-start(s16[10,16,128]{2,1,0:T(8,128)(2,1)S(1)} %get-tuple-element.50), channel_id=1, source_target_pairs={{3,1},{5,3},{7,5},{9,7},{11,9},{13,11},{15,13},{19,17},{21,19},{23... | collective-permute-start | bytes 122888 | tf_op jit(solution)/shard_map/ppermute | solution.py:550
  44.4 9.4 %collective-permute-start.14 = (f32[8,128]{1,0:T(8,128)S(1)}, f32[8,128]{1,0:T(8,128)S(1)}, u32[]{:S(2)}, u32[]{:S(2)}) collective-permute-start(f32[8,128]{1,0:T(8,128)S(1)} %far.1), channel_id=1, source_target_pairs={{0,3},{1,2},{2,1},{3,0},{4,7},{5,6},{6,5},{7,4},{8,11},{9,10},{10,... | collective-permute-start | bytes 12296 | tf_op jit(solution)/shard_map/ppermute | solution.py:524
  52.5 3.6 %collective-permute-start.13 = (f32[8,128]{1,0:T(8,128)S(1)}, f32[8,128]{1,0:T(8,128)S(1)}, u32[]{:S(2)}, u32[]{:S(2)}) collective-permute-start(f32[8,128]{1,0:T(8,128)S(1)} %far.1), channel_id=1, source_target_pairs={{0,2},{1,3},{2,0},{3,1},{4,6},{5,7},{6,4},{7,5},{8,10},{9,11},{10,... | collective-permute-start | bytes 12296 | tf_op jit(solution)/shard_map/ppermute | solution.py:524
  52.5 3.6 %collective-permute-start.12 = (f32[8,128]{1,0:T(8,128)S(1)}, f32[8,128]{1,0:T(8,128)S(1)}, u32[]{:S(2)}, u32[]{:S(2)}) collective-permute-start(f32[8,128]{1,0:T(8,128)S(1)} %far.1), channel_id=1, source_target_pairs={{0,1},{1,0},{2,3},{3,2},{4,5},{5,4},{6,7},{7,6},{8,9},{9,8},{10,11... | collective-permute-start | bytes 12296 | tf_op jit(solution)/shard_map/ppermute | solution.py:524
  56.1 5.5 %collective-permute-start.17 = (f32[8,128]{1,0:T(8,128)S(1)}, f32[8,128]{1,0:T(8,128)S(1)}, u32[]{:S(2)}, u32[]{:S(2)}) collective-permute-start(f32[8,128]{1,0:T(8,128)S(1)} %add_add_fusion.refs_0_), channel_id=1, source_target_pairs={{0,12},{1,13},{2,14},{3,15},{4,8},{5,9},{6,10},{7,11},{8,4},{9,5},... | collective-permute-start | bytes 12296 | tf_op jit(solution)/shard_map/ppermute | solution.py:524
  57.4 4.5 %collective-permute-start.16 = (f32[8,128]{1,0:T(8,128)S(1)}, f32[8,128]{1,0:T(8,128)S(1)}, u32[]{:S(2)}, u32[]{:S(2)}) collective-permute-start(f32[8,128]{1,0:T(8,128)S(1)} %add_add_fusion.refs_0_), channel_id=1, source_target_pairs={{0,8},{1,9},{2,10},{3,11},{4,12},{5,13},{6,14},{7,15},{8,0},{9,1},... | collective-permute-start | bytes 12296 | tf_op jit(solution)/shard_map/ppermute | solution.py:524
  58.4 3.7 %collective-permute-start.15 = (f32[8,128]{1,0:T(8,128)S(1)}, f32[8,128]{1,0:T(8,128)S(1)}, u32[]{:S(2)}, u32[]{:S(2)}) collective-permute-start(f32[8,128]{1,0:T(8,128)S(1)} %add_add_fusion.refs_0_), channel_id=1, source_target_pairs={{0,4},{1,5},{2,6},{3,7},{4,0},{5,1},{6,2},{7,3},{8,12},{9,13},{10,... | collective-permute-start | bytes 12296 | tf_op jit(solution)/shard_map/ppermute | solution.py:524

commit v6 on v3

--- a/solution.py
+++ b/solution.py
@@ -560,7 +560,7 @@
             far_kernel, in_specs=[vmem] * 3, out_specs=vmem, out_shape=f32(8, LANES), compiler_params=params, name="far"
         )(gram, two, far)
     ]
-    for bit in range(0, count.bit_length() - 1, 2):
+    for bit in reversed(range(0, count.bit_length() - 1, 2)):
         masks = [mask << bit for mask in (1, 2, 3) if mask << bit < count]
         gram = sum(grams[1:], grams[0])
         grams = [gram] + [flip(gram, mask) for mask in masks]

time: 57.9 us -> 57.9 us (level)
  waiting for transfers between devices: 14.7 us -> 15.4 us
  starting transfers between devices: 25.3 us -> 24.6 us
    ppermute x15, waiting for transfers between devices: 11.9 us -> 12.6 us  [on_device(): lax.ppermute(x, 'rows', [(i, i ^ mask) for i in range(count)])]
    ppermute x15, starting transfers between devices: 23.3 us -> 22.6 us  [on_device(): lax.ppermute(x, 'rows', [(i, i ^ mask) for i in range(count)])]
where the time goes in v6:
time: 57.9 us; the launch traced here: 57.7 us
  starting transfers between devices  24.6 us (42%)
  Pallas kernels  17.6 us (30%)
  waiting for transfers between devices  15.4 us (27%)
    ppermute x15, starting transfers between devices, on_device(): lax.ppermute(x, 'rows', [(i, i ^ mask) for i in range(count)])  22.6 us
    ppermute x15, waiting for transfers between devices, on_device(): lax.ppermute(x, 'rows', [(i, i ^ mask) for i in range(count)])  12.6 us
    pallas_call x2, Pallas kernels, partial_sums(): pl.pallas_call(functools.partial(sums_kernel, scale=scale, rows_here=rows...  11.7 us
    ppermute x1, waiting for transfers between devices, on_device(): far = lax.ppermute(first, 'rows', [(i + 2, i) for i in range(count - 2)])  2.74 us
    pallas_call x6, Pallas kernels, add_split(): pl.pallas_call(functools.partial(add_split_kernel, place=place), in_specs...  2.21 us
    pallas_call x1, Pallas kernels, on_device(): pl.pallas_call(functools.partial(krylov_kernel, total_rows=total_rows, ro...  1.82 us
    ppermute x1, starting transfers between devices, on_device(): far = lax.ppermute(first, 'rows', [(i + 2, i) for i in range(count - 2)])  1.28 us
  transfers between devices with their start and end apart: 17, of which 9 were waited for; matrix products, arithmetic and copies ran while one was open for 0% of the time, Pallas kernels for 16%

profile of v6, /device:TPU:0, one launch (start us, length us, event | category | flops | bytes accessed | tf_op | source)
XLA Modules:
  0.0 57.7 jit_solution(7391187649946087886)
XLA Ops:
  0.0 6.4 %partial_sums.2 = (f32[8,48,512]{2,1,0:T(8,128)}, s16[8,13,16,128]{3,2,1,0:T(8,128)(2,1)}) custom-call(s32[1]{0:T(128)} %bitcast.me_ref, s32[128]{0:T(128)} %ids_ref.3, f32[4,6]{1,0:T(4,128)} %gain_ref.3, f32[4]{0:T(128)} %weight_ref.3, bf16[8,6,32,1024]{3,2,1,0:T(8,128)(2,1)} %reflect_hbm.3, s32[8,32,1024]{2,1,0:T(8,128)} %conf_hbm.3, ...), custom_call_target="tpu_custom_call" | custom-call | tf_op jit(solution)/shard_map/partial_sums/pallas_call | solution.py:243
  7.0 5.2 %partial_sums.3 = (f32[8,48,512]{2,1,0:T(8,128)S(1)}, s16[8,13,16,128]{3,2,1,0:T(8,128)(2,1)S(1)}) custom-call(s32[1]{0:T(128)} %bitcast.me_ref, s32[128]{0:T(128)S(1)} %copy-done.3, f32[4,6]{1,0:T(4,128)S(1)} %copy-done.2, f32[4]{0:T(128)S(1)} %copy-done.4, bf16[8,6,32,1024]{3,2,1,0:T(8,128)(2,1)} %reflect_hbm.3, s32[8,32,1024]{2,1,0:T(8,128)} %conf_hbm.3, ...), custom_call_target="tpu_custom_call" | custom-call | tf_op jit(solution)/shard_map/partial_sums/pallas_call | solution.py:243
  12.8 3.0 %collective-permute-start.1 = (s16[4,13,16,128]{3,2,1,0:T(8,128)(2,1)S(1)}, s16[4,13,16,128]{3,2,1,0:T(8,128)(2,1)S(1)}, u32[]{:S(2)}, u32[]{:S(2)}) collective-permute-start(s16[4,13,16,128]{3,2,1,0:T(8,128)(2,1)S(1)} %get-tuple-element.32), channel_id=1, source_target_pairs={{0,2},{1,3},{2,0},{3,1},{4,6},{5,7},{6,4},{7,5},{8,10},{9,11},{10,... | collective-permute-start | bytes 638984 | tf_op jit(solution)/shard_map/ppermute | solution.py:521
  16.3 1.6 %collective-permute-start.5 = (s16[4,13,16,128]{3,2,1,0:T(8,128)(2,1)S(1)}, s16[4,13,16,128]{3,2,1,0:T(8,128)(2,1)S(1)}, u32[]{:S(2)}, u32[]{:S(2)}) collective-permute-start(s16[4,13,16,128]{3,2,1,0:T(8,128)(2,1)S(1)} %get-tuple-element.41), channel_id=1, source_target_pairs={{0,4},{1,5},{2,6},{3,7},{4,0},{5,1},{6,2},{7,3},{8,12},{9,13},{10,... | collective-permute-start | bytes 638984 | tf_op jit(solution)/shard_map/ppermute | solution.py:521
  17.9 3.4 %collective-permute-done.1.refs_1_ = s16[4,13,16,128]{3,2,1,0:T(8,128)(2,1)S(1)} collective-permute-done((s16[4,13,16,128]{3,2,1,0:T(8,128)(2,1)S(1)}, s16[4,13,16,128]{3,2,1,0:T(8,128)(2,1)S(1)}, u32[]{:S(2)}, u32[]{:S(2)}) %collective-permute-start.1) | collective-permute-done | bytes 213024 | tf_op jit(solution)/shard_map/ppermute | solution.py:521
  21.7 1.9 %collective-permute-start.2 = (s16[2,13,16,128]{3,2,1,0:T(8,128)(2,1)S(1)}, s16[2,13,16,128]{3,2,1,0:T(8,128)(2,1)S(1)}, u32[]{:S(2)}, u32[]{:S(2)}) collective-permute-start(s16[2,13,16,128]{3,2,1,0:T(8,128)(2,1)S(1)} %get-tuple-element.34), channel_id=1, source_target_pairs={{0,4},{1,5},{2,6},{3,7},{4,0},{5,1},{6,2},{7,3},{8,12},{9,13},{10,... | collective-permute-start | bytes 319496 | tf_op jit(solution)/shard_map/ppermute | solution.py:521
  23.9 1.6 %collective-permute-start.6 = (s16[2,13,16,128]{3,2,1,0:T(8,128)(2,1)S(1)}, s16[2,13,16,128]{3,2,1,0:T(8,128)(2,1)S(1)}, u32[]{:S(2)}, u32[]{:S(2)}) collective-permute-start(s16[2,13,16,128]{3,2,1,0:T(8,128)(2,1)S(1)} %get-tuple-element.43), channel_id=1, source_target_pairs={{0,2},{1,3},{2,0},{3,1},{4,6},{5,7},{6,4},{7,5},{8,10},{9,11},{10,... | collective-permute-start | bytes 319496 | tf_op jit(solution)/shard_map/ppermute | solution.py:521
  25.5 0.9 %collective-permute-done.2.refs_1_ = s16[2,13,16,128]{3,2,1,0:T(8,128)(2,1)S(1)} collective-permute-done((s16[2,13,16,128]{3,2,1,0:T(8,128)(2,1)S(1)}, s16[2,13,16,128]{3,2,1,0:T(8,128)(2,1)S(1)}, u32[]{:S(2)}, u32[]{:S(2)}) %collective-permute-start.2) | collective-permute-done | bytes 106528 | tf_op jit(solution)/shard_map/ppermute | solution.py:521
  26.8 2.9 %collective-permute-start.3 = (s16[1,13,16,128]{3,2,1,0:T(8,128)(2,1)S(1)}, s16[1,13,16,128]{3,2,1,0:T(8,128)(2,1)S(1)}, u32[]{:S(2)}, u32[]{:S(2)}) collective-permute-start(s16[1,13,16,128]{3,2,1,0:T(8,128)(2,1)S(1)} %get-tuple-element.36), channel_id=1, source_target_pairs={{0,8},{1,9},{2,10},{3,11},{4,12},{5,13},{6,14},{7,15},{8,0},{9,1},... | collective-permute-start | bytes 159752 | tf_op jit(solution)/shard_map/ppermute | solution.py:521
  30.0 1.7 %collective-permute-start.7 = (s16[1,13,16,128]{3,2,1,0:T(8,128)(2,1)S(1)}, s16[1,13,16,128]{3,2,1,0:T(8,128)(2,1)S(1)}, u32[]{:S(2)}, u32[]{:S(2)}) collective-permute-start(s16[1,13,16,128]{3,2,1,0:T(8,128)(2,1)S(1)} %get-tuple-element.45), channel_id=1, source_target_pairs={{0,8},{1,9},{2,10},{3,11},{4,12},{5,13},{6,14},{7,15},{8,0},{9,1},... | collective-permute-start | bytes 159752 | tf_op jit(solution)/shard_map/ppermute | solution.py:521
  31.7 0.7 %collective-permute-done.3.refs_1_ = s16[1,13,16,128]{3,2,1,0:T(8,128)(2,1)S(1)} collective-permute-done((s16[1,13,16,128]{3,2,1,0:T(8,128)(2,1)S(1)}, s16[1,13,16,128]{3,2,1,0:T(8,128)(2,1)S(1)}, u32[]{:S(2)}, u32[]{:S(2)}) %collective-permute-start.3) | collective-permute-done | bytes 53280 | tf_op jit(solution)/shard_map/ppermute | solution.py:521
  32.5 2.7 %collective-permute-done.7.refs_3_ = s16[1,13,16,128]{3,2,1,0:T(8,128)(2,1)S(1)} collective-permute-done((s16[1,13,16,128]{3,2,1,0:T(8,128)(2,1)S(1)}, s16[1,13,16,128]{3,2,1,0:T(8,128)(2,1)S(1)}, u32[]{:S(2)}, u32[]{:S(2)}) %collective-permute-start.7) | collective-permute-done | bytes 53280 | tf_op jit(solution)/shard_map/ppermute | solution.py:521
  36.5 2.9 %collective-permute-start.8 = (s16[25,16,128]{2,1,0:T(8,128)(2,1)S(1)}, s16[25,16,128]{2,1,0:T(8,128)(2,1)S(1)}, u32[]{:S(2)}, u32[]{:S(2)}) collective-permute-start(s16[25,16,128]{2,1,0:T(8,128)(2,1)S(1)} %bitcast.9), channel_id=1, source_target_pairs={{0,1},{1,0},{2,3},{3,2},{4,5},{5,4},{6,7},{7,6},{8,9},{9,8},{10,11... | collective-permute-start | bytes 307208 | tf_op jit(solution)/shard_map/ppermute | solution.py:521
  39.5 1.3 %collective-permute-start.10 = (s16[10,16,128]{2,1,0:T(8,128)(2,1)S(1)}, s16[10,16,128]{2,1,0:T(8,128)(2,1)S(1)}, u32[]{:S(2)}, u32[]{:S(2)}) collective-permute-start(s16[10,16,128]{2,1,0:T(8,128)(2,1)S(1)} %get-tuple-element.50), channel_id=1, source_target_pairs={{2,0},{3,1},{4,2},{5,3},{6,4},{7,5},{8,6},{9,7},{10,8},{11,9},{12,... | collective-permute-start | bytes 122888 | tf_op jit(solution)/shard_map/ppermute | solution.py:547
  40.8 1.8 %krylov.1 = (f32[18,2,1024]{2,1,0:T(2,128)S(1)}, f32[18,2,1024]{2,1,0:T(2,128)S(1)}, f32[18,2,1024]{2,1,0:T(2,128)S(1)}, f32[8,128]{1,0:T(8,128)S(1)}) custom-call(s32[1]{0:T(128)} %bitcast.me_ref, f32[48,1024]{1,0:T(8,128)S(1)} %get-tuple-element.46.own_ref, s16[25,16,128]{2,1,0:T(8,128)(2,1)S(1)} %collective-permute-done.8.mate_ref, ...), custom_call_target="tpu_custom_call" | custom-call | tf_op jit(solution)/shard_map/krylov/pallas_call | solution.py:548
  42.6 2.7 %collective-permute-done.10.far_ref = s16[10,16,128]{2,1,0:T(8,128)(2,1)S(1)} collective-permute-done((s16[10,16,128]{2,1,0:T(8,128)(2,1)S(1)}, s16[10,16,128]{2,1,0:T(8,128)(2,1)S(1)}, u32[]{:S(2)}, u32[]{:S(2)}) %collective-permute-start.10) | collective-permute-done | bytes 40992 | tf_op jit(solution)/shard_map/ppermute | solution.py:547
  45.7 2.9 %collective-permute-start.13 = (f32[8,128]{1,0:T(8,128)S(1)}, f32[8,128]{1,0:T(8,128)S(1)}, u32[]{:S(2)}, u32[]{:S(2)}) collective-permute-start(f32[8,128]{1,0:T(8,128)S(1)} %far.1), channel_id=1, source_target_pairs={{0,12},{1,13},{2,14},{3,15},{4,8},{5,9},{6,10},{7,11},{8,4},{9,5},... | collective-permute-start | bytes 12296 | tf_op jit(solution)/shard_map/ppermute | solution.py:521
  48.8 1.4 %collective-permute-start.11 = (f32[8,128]{1,0:T(8,128)S(1)}, f32[8,128]{1,0:T(8,128)S(1)}, u32[]{:S(2)}, u32[]{:S(2)}) collective-permute-start(f32[8,128]{1,0:T(8,128)S(1)} %far.1), channel_id=1, source_target_pairs={{0,4},{1,5},{2,6},{3,7},{4,0},{5,1},{6,2},{7,3},{8,12},{9,13},{10,... | collective-permute-start | bytes 12296 | tf_op jit(solution)/shard_map/ppermute | solution.py:521
  50.1 1.0 %collective-permute-done.13 = f32[8,128]{1,0:T(8,128)S(1)} collective-permute-done((f32[8,128]{1,0:T(8,128)S(1)}, f32[8,128]{1,0:T(8,128)S(1)}, u32[]{:S(2)}, u32[]{:S(2)}) %collective-permute-start.13) | collective-permute-done | bytes 4128 | tf_op jit(solution)/shard_map/ppermute | solution.py:521
  51.1 1.9 %collective-permute-done.12 = f32[8,128]{1,0:T(8,128)S(1)} collective-permute-done((f32[8,128]{1,0:T(8,128)S(1)}, f32[8,128]{1,0:T(8,128)S(1)}, u32[]{:S(2)}, u32[]{:S(2)}) %collective-permute-start.12) | collective-permute-done | bytes 4128 | tf_op jit(solution)/shard_map/ppermute | solution.py:521
  53.2 1.0 %collective-permute-start.15 = (f32[8,128]{1,0:T(8,128)S(1)}, f32[8,128]{1,0:T(8,128)S(1)}, u32[]{:S(2)}, u32[]{:S(2)}) collective-permute-start(f32[8,128]{1,0:T(8,128)S(1)} %add_add_fusion.refs_0_), channel_id=1, source_target_pairs={{0,2},{1,3},{2,0},{3,1},{4,6},{5,7},{6,4},{7,5},{8,10},{9,11},{10,... | collective-permute-start | bytes 12296 | tf_op jit(solution)/shard_map/ppermute | solution.py:521
  54.2 0.8 %collective-permute-start.14 = (f32[8,128]{1,0:T(8,128)S(1)}, f32[8,128]{1,0:T(8,128)S(1)}, u32[]{:S(2)}, u32[]{:S(2)}) collective-permute-start(f32[8,128]{1,0:T(8,128)S(1)} %add_add_fusion.refs_0_), channel_id=1, source_target_pairs={{0,1},{1,0},{2,3},{3,2},{4,5},{5,4},{6,7},{7,6},{8,9},{9,8},{10,11... | collective-permute-start | bytes 12296 | tf_op jit(solution)/shard_map/ppermute | solution.py:521
  55.0 1.2 %collective-permute-done.16.refs_3_ = f32[8,128]{1,0:T(8,128)S(1)} collective-permute-done((f32[8,128]{1,0:T(8,128)S(1)}, f32[8,128]{1,0:T(8,128)S(1)}, u32[]{:S(2)}, u32[]{:S(2)}) %collective-permute-start.16) | collective-permute-done | bytes 4128 | tf_op jit(solution)/shard_map/ppermute | solution.py:521
  56.9 0.9 %combine.1 = f32[18,2,1024]{2,1,0:T(2,128)} custom-call(f32[8,128]{1,0:T(8,128)S(1)} %add_add_fusion.refs_0_, f32[8,128]{1,0:T(8,128)S(1)} %collective-permute-done.14.refs_1_, f32[8,128]{1,0:T(8,128)S(1)} %collective-permute-done.15.refs_2_, f32[8,128]{1,0:T(8,128)S(1)} %collective-permute-done.16.refs_3_, f32[18,2,1024]{2,1,0:T(2,128)S(1)} %bitcast.7, ...), custom_call_target="tpu_custom_call" | custom-call | tf_op jit(solution)/shard_map/combine/pallas_call | solution.py:567
  (33 shorter events, 5.5 us)
Async XLA Ops:
  0.0 7.0 %copy-start = (f32[2,18,1024]{2,0,1:T(2,128)S(1)}, f32[2,18,1024]{2,0,1:T(2,128)}, u32[]{:S(2)}) copy-start(f32[2,18,1024]{2,0,1:T(2,128)} %param.13) | copy-start | bytes 442372
  0.0 7.0 %copy-start.2 = (f32[4,6]{1,0:T(4,128)S(1)}, f32[4,6]{1,0:T(4,128)}, u32[]{:S(2)}) copy-start(f32[4,6]{1,0:T(4,128)} %gain_ref.3) | copy-start | bytes 292
  0.0 7.0 %copy-start.3 = (s32[128]{0:T(128)S(1)}, s32[128]{0:T(128)}, u32[]{:S(2)}) copy-start(s32[128]{0:T(128)} %ids_ref.3) | copy-start | bytes 1540
  0.0 7.0 %copy-start.4 = (f32[4]{0:T(128)S(1)}, f32[4]{0:T(128)}, u32[]{:S(2)}) copy-start(f32[4]{0:T(128)} %weight_ref.3) | copy-start | bytes 52
  6.5 5.9 %copy-start.1 = (f32[8,48,512]{2,1,0:T(8,128)S(1)}, f32[8,48,512]{2,1,0:T(8,128)}, u32[]{:S(2)}) copy-start(f32[8,48,512]{2,1,0:T(8,128)} %get-tuple-element.29.refs_0_) | copy-start | bytes 2359300
  6.5 5.9 %collective-permute-start = (s16[8,13,16,128]{3,2,1,0:T(8,128)(2,1)}, s16[8,13,16,128]{3,2,1,0:T(8,128)(2,1)S(1)}, u32[]{:S(2)}, u32[]{:S(2)}) collective-permute-start(s16[8,13,16,128]{3,2,1,0:T(8,128)(2,1)} %get-tuple-element.30), channel_id=1, source_target_pairs={{0,1},{1,0},{2,3},{3,2},{4,5},{5,4},{6,7},{7,6},{8,9},{9,8},{10,11... | collective-permute-start | bytes 1277960 | tf_op jit(solution)/shard_map/ppermute | solution.py:521
  12.2 3.6 %collective-permute-start.4 = (s16[8,13,16,128]{3,2,1,0:T(8,128)(2,1)S(1)}, s16[8,13,16,128]{3,2,1,0:T(8,128)(2,1)S(1)}, u32[]{:S(2)}, u32[]{:S(2)}) collective-permute-start(s16[8,13,16,128]{3,2,1,0:T(8,128)(2,1)S(1)} %get-tuple-element.39), channel_id=1, source_target_pairs={{0,1},{1,0},{2,3},{3,2},{4,5},{5,4},{6,7},{7,6},{8,9},{9,8},{10,11... | collective-permute-start | bytes 1277960 | tf_op jit(solution)/shard_map/ppermute | solution.py:521
  12.8 8.5 %collective-permute-start.1 = (s16[4,13,16,128]{3,2,1,0:T(8,128)(2,1)S(1)}, s16[4,13,16,128]{3,2,1,0:T(8,128)(2,1)S(1)}, u32[]{:S(2)}, u32[]{:S(2)}) collective-permute-start(s16[4,13,16,128]{3,2,1,0:T(8,128)(2,1)S(1)} %get-tuple-element.32), channel_id=1, source_target_pairs={{0,2},{1,3},{2,0},{3,1},{4,6},{5,7},{6,4},{7,5},{8,10},{9,11},{10,... | collective-permute-start | bytes 638984 | tf_op jit(solution)/shard_map/ppermute | solution.py:521
  16.3 7.3 %collective-permute-start.5 = (s16[4,13,16,128]{3,2,1,0:T(8,128)(2,1)S(1)}, s16[4,13,16,128]{3,2,1,0:T(8,128)(2,1)S(1)}, u32[]{:S(2)}, u32[]{:S(2)}) collective-permute-start(s16[4,13,16,128]{3,2,1,0:T(8,128)(2,1)S(1)} %get-tuple-element.41), channel_id=1, source_target_pairs={{0,4},{1,5},{2,6},{3,7},{4,0},{5,1},{6,2},{7,3},{8,12},{9,13},{10,... | collective-permute-start | bytes 638984 | tf_op jit(solution)/shard_map/ppermute | solution.py:521
  21.7 4.8 %collective-permute-start.2 = (s16[2,13,16,128]{3,2,1,0:T(8,128)(2,1)S(1)}, s16[2,13,16,128]{3,2,1,0:T(8,128)(2,1)S(1)}, u32[]{:S(2)}, u32[]{:S(2)}) collective-permute-start(s16[2,13,16,128]{3,2,1,0:T(8,128)(2,1)S(1)} %get-tuple-element.34), channel_id=1, source_target_pairs={{0,4},{1,5},{2,6},{3,7},{4,0},{5,1},{6,2},{7,3},{8,12},{9,13},{10,... | collective-permute-start | bytes 319496 | tf_op jit(solution)/shard_map/ppermute | solution.py:521
  23.9 5.8 %collective-permute-start.6 = (s16[2,13,16,128]{3,2,1,0:T(8,128)(2,1)S(1)}, s16[2,13,16,128]{3,2,1,0:T(8,128)(2,1)S(1)}, u32[]{:S(2)}, u32[]{:S(2)}) collective-permute-start(s16[2,13,16,128]{3,2,1,0:T(8,128)(2,1)S(1)} %get-tuple-element.43), channel_id=1, source_target_pairs={{0,2},{1,3},{2,0},{3,1},{4,6},{5,7},{6,4},{7,5},{8,10},{9,11},{10,... | collective-permute-start | bytes 319496 | tf_op jit(solution)/shard_map/ppermute | solution.py:521
  26.8 5.6 %collective-permute-start.3 = (s16[1,13,16,128]{3,2,1,0:T(8,128)(2,1)S(1)}, s16[1,13,16,128]{3,2,1,0:T(8,128)(2,1)S(1)}, u32[]{:S(2)}, u32[]{:S(2)}) collective-permute-start(s16[1,13,16,128]{3,2,1,0:T(8,128)(2,1)S(1)} %get-tuple-element.36), channel_id=1, source_target_pairs={{0,8},{1,9},{2,10},{3,11},{4,12},{5,13},{6,14},{7,15},{8,0},{9,1},... | collective-permute-start | bytes 159752 | tf_op jit(solution)/shard_map/ppermute | solution.py:521
  30.0 5.1 %collective-permute-start.7 = (s16[1,13,16,128]{3,2,1,0:T(8,128)(2,1)S(1)}, s16[1,13,16,128]{3,2,1,0:T(8,128)(2,1)S(1)}, u32[]{:S(2)}, u32[]{:S(2)}) collective-permute-start(s16[1,13,16,128]{3,2,1,0:T(8,128)(2,1)S(1)} %get-tuple-element.45), channel_id=1, source_target_pairs={{0,8},{1,9},{2,10},{3,11},{4,12},{5,13},{6,14},{7,15},{8,0},{9,1},... | collective-permute-start | bytes 159752 | tf_op jit(solution)/shard_map/ppermute | solution.py:521
  35.9 4.9 %collective-permute-start.9 = (s16[25,16,128]{2,1,0:T(8,128)(2,1)S(1)}, s16[25,16,128]{2,1,0:T(8,128)(2,1)S(1)}, u32[]{:S(2)}, u32[]{:S(2)}) collective-permute-start(s16[25,16,128]{2,1,0:T(8,128)(2,1)S(1)} %bitcast.8), channel_id=1, source_target_pairs={{1,2},{3,4},{5,6},{7,8},{9,10},{11,12},{13,14},{2,1},{4,3},{6,5},{... | collective-permute-start | bytes 307208 | tf_op jit(solution)/shard_map/ppermute | solution.py:546
  36.5 4.2 %collective-permute-start.8 = (s16[25,16,128]{2,1,0:T(8,128)(2,1)S(1)}, s16[25,16,128]{2,1,0:T(8,128)(2,1)S(1)}, u32[]{:S(2)}, u32[]{:S(2)}) collective-permute-start(s16[25,16,128]{2,1,0:T(8,128)(2,1)S(1)} %bitcast.9), channel_id=1, source_target_pairs={{0,1},{1,0},{2,3},{3,2},{4,5},{5,4},{6,7},{7,6},{8,9},{9,8},{10,11... | collective-permute-start | bytes 307208 | tf_op jit(solution)/shard_map/ppermute | solution.py:521
  39.5 5.9 %collective-permute-start.10 = (s16[10,16,128]{2,1,0:T(8,128)(2,1)S(1)}, s16[10,16,128]{2,1,0:T(8,128)(2,1)S(1)}, u32[]{:S(2)}, u32[]{:S(2)}) collective-permute-start(s16[10,16,128]{2,1,0:T(8,128)(2,1)S(1)} %get-tuple-element.50), channel_id=1, source_target_pairs={{2,0},{3,1},{4,2},{5,3},{6,4},{7,5},{8,6},{9,7},{10,8},{11,9},{12,... | collective-permute-start | bytes 122888 | tf_op jit(solution)/shard_map/ppermute | solution.py:547
  45.7 5.5 %collective-permute-start.13 = (f32[8,128]{1,0:T(8,128)S(1)}, f32[8,128]{1,0:T(8,128)S(1)}, u32[]{:S(2)}, u32[]{:S(2)}) collective-permute-start(f32[8,128]{1,0:T(8,128)S(1)} %far.1), channel_id=1, source_target_pairs={{0,12},{1,13},{2,14},{3,15},{4,8},{5,9},{6,10},{7,11},{8,4},{9,5},... | collective-permute-start | bytes 12296 | tf_op jit(solution)/shard_map/ppermute | solution.py:521
  48.6 4.5 %collective-permute-start.12 = (f32[8,128]{1,0:T(8,128)S(1)}, f32[8,128]{1,0:T(8,128)S(1)}, u32[]{:S(2)}, u32[]{:S(2)}) collective-permute-start(f32[8,128]{1,0:T(8,128)S(1)} %far.1), channel_id=1, source_target_pairs={{0,8},{1,9},{2,10},{3,11},{4,12},{5,13},{6,14},{7,15},{8,0},{9,1},... | collective-permute-start | bytes 12296 | tf_op jit(solution)/shard_map/ppermute | solution.py:521
  48.8 4.3 %collective-permute-start.11 = (f32[8,128]{1,0:T(8,128)S(1)}, f32[8,128]{1,0:T(8,128)S(1)}, u32[]{:S(2)}, u32[]{:S(2)}) collective-permute-start(f32[8,128]{1,0:T(8,128)S(1)} %far.1), channel_id=1, source_target_pairs={{0,4},{1,5},{2,6},{3,7},{4,0},{5,1},{6,2},{7,3},{8,12},{9,13},{10,... | collective-permute-start | bytes 12296 | tf_op jit(solution)/shard_map/ppermute | solution.py:521
  53.1 3.1 %collective-permute-start.16 = (f32[8,128]{1,0:T(8,128)S(1)}, f32[8,128]{1,0:T(8,128)S(1)}, u32[]{:S(2)}, u32[]{:S(2)}) collective-permute-start(f32[8,128]{1,0:T(8,128)S(1)} %add_add_fusion.refs_0_), channel_id=1, source_target_pairs={{0,3},{1,2},{2,1},{3,0},{4,7},{5,6},{6,5},{7,4},{8,11},{9,10},{10,... | collective-permute-start | bytes 12296 | tf_op jit(solution)/shard_map/ppermute | solution.py:521
  53.2 3.7 %collective-permute-start.15 = (f32[8,128]{1,0:T(8,128)S(1)}, f32[8,128]{1,0:T(8,128)S(1)}, u32[]{:S(2)}, u32[]{:S(2)}) collective-permute-start(f32[8,128]{1,0:T(8,128)S(1)} %add_add_fusion.refs_0_), channel_id=1, source_target_pairs={{0,2},{1,3},{2,0},{3,1},{4,6},{5,7},{6,4},{7,5},{8,10},{9,11},{10,... | collective-permute-start | bytes 12296 | tf_op jit(solution)/shard_map/ppermute | solution.py:521
  54.2 2.7 %collective-permute-start.14 = (f32[8,128]{1,0:T(8,128)S(1)}, f32[8,128]{1,0:T(8,128)S(1)}, u32[]{:S(2)}, u32[]{:S(2)}) collective-permute-start(f32[8,128]{1,0:T(8,128)S(1)} %add_add_fusion.refs_0_), channel_id=1, source_target_pairs={{0,1},{1,0},{2,3},{3,2},{4,5},{5,4},{6,7},{7,6},{8,9},{9,8},{10,11... | collective-permute-start | bytes 12296 | tf_op jit(solution)/shard_map/ppermute | solution.py:521

commit v7 on v3

--- a/solution.py
+++ b/solution.py
@@ -17,7 +17,7 @@
 LANES = 128
 QUANT = 32000.0
 GROUP = LANES // 4
-CHUNKS = 2
+SHARES = (5, 3)
 
 
 R_POLY = (0.9428089773, 0.04714460664, 0.007527079489, 0.001965302741, 9.052799897e-05, 0.0004621408027)
@@ -210,7 +210,7 @@
             @pl.when((row >= 0) & (row < tile_rows))
             def _():
                 for c in tiles:
-                    lanes = slice(c * LANES, (c + 1) * LANES)
+                    lanes = slice(first_col + c * LANES, first_col + (c + 1) * LANES)
                     at = pl.ds(pl.multiple_of(row * ENTRIES, 8), obs_count)
                     part = jnp.concatenate([prior_ref[e, source : source + 1, lanes] for e in range(obs_count)], axis=0)
                     sums_ref[c, at, :] = sums_ref[c, at, :] + SMOOTH_PULL * part
@@ -228,9 +228,8 @@
     lax.fori_loop(0, steps // lane_tiles, row_tile_sums, 0)
 
 
-def partial_sums(me, reflect, clear_conf, sun_view, sensor_id, band_gain, sensor_weight, prior, scale, chunk):
-    dates, bands, rows, cols = reflect.shape
-    cols = cols // CHUNKS
+def partial_sums(me, reflect, clear_conf, sun_view, sensor_id, band_gain, sensor_weight, prior, scale, first_col, cols):
+    dates, bands, rows, _ = reflect.shape
     rows_here = prior.shape[1]
     count = rows // rows_here
     tile_rows = 16
@@ -241,9 +240,8 @@
     vmem = pl.BlockSpec(memory_space=pltpu.VMEM)
     hbm = pl.BlockSpec(memory_space=pl.ANY)
     return pl.pallas_call(
-        functools.partial(sums_kernel, scale=scale, rows_here=rows_here, first_col=chunk * cols),
-        grid=(1,),
-        in_specs=[smem] * 4 + [hbm] * 3 + [pl.BlockSpec((3 * bands, rows_here, cols), lambda i: (0, 0, chunk))],
+        functools.partial(sums_kernel, scale=scale, rows_here=rows_here, first_col=first_col),
+        in_specs=[smem] * 4 + [hbm] * 3 + [vmem],
         out_specs=[vmem, vmem],
         out_shape=[
             jax.ShapeDtypeStruct((count // 2, block, cols), jnp.float32),
@@ -257,7 +255,7 @@
             pltpu.VMEM((steps, dates, 3, tile_rows, LANES), jnp.int32),
             pltpu.SemaphoreType.DMA((steps, 3)),
         ],
-        compiler_params=pltpu.CompilerParams(vmem_limit_bytes=(62 if chunk == 0 else 52) * 2**20),
+        compiler_params=pltpu.CompilerParams(vmem_limit_bytes=(62 if first_col == 0 else 52) * 2**20),
         name="partial_sums",
     )(me, sensor_id, band_gain, sensor_weight, reflect, clear_conf, sun_view, prior)
 
@@ -512,9 +510,11 @@
     scale = 0.01 / (reflect.shape[0] * count)
     index = me
     parts = []
-    for chunk in range(CHUNKS):
+    for chunk, share in enumerate(SHARES):
+        part = cols // sum(SHARES)
+        first_col = part * sum(SHARES[:chunk])
         kept, sent = partial_sums(
-            index, reflect, clear_conf, sun_view, sensor_id, band_gain, sensor_weight, prior, scale, chunk
+            index, reflect, clear_conf, sun_view, sensor_id, band_gain, sensor_weight, prior, scale, first_col, part * share
         )
         index, _ = lax.optimization_barrier((me, sent))
         parts.append((kept, sent))
@@ -523,7 +523,7 @@
     parts = [(kept, swap(sent, 0)) for kept, sent in parts]
     bits = list(range(1, count.bit_length() - 1))
     for step in range(len(bits)):
-        for chunk in range(CHUNKS):
+        for chunk in range(len(SHARES)):
             turned = chunk % 2 == 1 and len(bits) >= 2 and step < 2
             bit, place = (bits[1 - step], 1 - step) if turned else (bits[step], 0)
             kept, sent = add_split(me // 2**bit % 2, place, *parts[chunk])

time: 57.9 us -> 58.8 us (1.016)
  waiting for transfers between devices: 14.7 us -> 15.9 us
  starting transfers between devices: 25.3 us -> 24.7 us
    ppermute x15, waiting for transfers between devices: 11.9 us -> 13.2 us  [on_device(): lax.ppermute(x, 'rows', [(i, i ^ mask) for i in range(count)])]
  transfers between devices with their start and end apart: 17 -> 17, of which waited for: 9 -> 8; matrix products, arithmetic and copies ran while one was open for 0% -> 0% of each run, Pallas kernels for 16% -> 15%
where the time goes in v7:
time: 58.8 us; the launch traced here: 58.6 us
  starting transfers between devices  24.7 us (42%)
  Pallas kernels  17.8 us (30%)
  waiting for transfers between devices  15.9 us (27%)
    ppermute x15, starting transfers between devices, on_device(): lax.ppermute(x, 'rows', [(i, i ^ mask) for i in range(count)])  22.8 us
    ppermute x15, waiting for transfers between devices, on_device(): lax.ppermute(x, 'rows', [(i, i ^ mask) for i in range(count)])  13.2 us
    pallas_call x2, Pallas kernels, partial_sums(): pl.pallas_call(functools.partial(sums_kernel, scale=scale, rows_here=rows...  11.8 us
    ppermute x1, waiting for transfers between devices, on_device(): far = lax.ppermute(first, 'rows', [(i + 2, i) for i in range(count - 2)])  2.74 us
    pallas_call x6, Pallas kernels, add_split(): pl.pallas_call(functools.partial(add_split_kernel, place=place), in_specs...  2.24 us
    pallas_call x1, Pallas kernels, on_device(): pl.pallas_call(functools.partial(krylov_kernel, total_rows=total_rows, ro...  1.82 us
    ppermute x1, starting transfers between devices, on_device(): far = lax.ppermute(first, 'rows', [(i + 2, i) for i in range(count - 2)])  1.28 us
  transfers between devices with their start and end apart: 17, of which 8 were waited for; matrix products, arithmetic and copies ran while one was open for 0% of the time, Pallas kernels for 15%

profile of v7, /device:TPU:0, one launch (start us, length us, event | category | flops | bytes accessed | tf_op | source)
XLA Modules:
  0.0 58.6 jit_solution(1255458883642782928)
XLA Ops:
  0.0 7.4 %partial_sums.2 = (f32[8,48,640]{2,1,0:T(8,128)}, s16[8,16,16,128]{3,2,1,0:T(8,128)(2,1)}) custom-call(s32[1]{0:T(128)} %bitcast.me_ref, s32[128]{0:T(128)} %ids_ref.3, f32[4,6]{1,0:T(4,128)} %gain_ref.3, f32[4]{0:T(128)} %weight_ref.3, bf16[8,6,32,1024]{3,2,1,0:T(8,128)(2,1)} %reflect_hbm.3, s32[8,32,1024]{2,1,0:T(8,128)} %conf_hbm.3, ...), custom_call_target="tpu_custom_call" | custom-call | tf_op jit(solution)/shard_map/partial_sums/pallas_call | solution.py:242
  8.0 4.4 %partial_sums.3 = (f32[8,48,384]{2,1,0:T(8,128)S(1)}, s16[8,10,16,128]{3,2,1,0:T(8,128)(2,1)S(1)}) custom-call(s32[1]{0:T(128)} %bitcast.me_ref, s32[128]{0:T(128)S(1)} %copy-done.3, f32[4,6]{1,0:T(4,128)S(1)} %copy-done.2, f32[4]{0:T(128)S(1)} %copy-done.4, bf16[8,6,32,1024]{3,2,1,0:T(8,128)(2,1)} %reflect_hbm.3, s32[8,32,1024]{2,1,0:T(8,128)} %conf_hbm.3, ...), custom_call_target="tpu_custom_call" | custom-call | tf_op jit(solution)/shard_map/partial_sums/pallas_call | solution.py:242
  13.0 3.0 %collective-permute-start.1 = (s16[4,16,16,128]{3,2,1,0:T(8,128)(2,1)S(1)}, s16[4,16,16,128]{3,2,1,0:T(8,128)(2,1)S(1)}, u32[]{:S(2)}, u32[]{:S(2)}) collective-permute-start(s16[4,16,16,128]{3,2,1,0:T(8,128)(2,1)S(1)} %get-tuple-element.32), channel_id=1, source_target_pairs={{0,2},{1,3},{2,0},{3,1},{4,6},{5,7},{6,4},{7,5},{8,10},{9,11},{10,... | collective-permute-start | bytes 786440 | tf_op jit(solution)/shard_map/ppermute | solution.py:521
  16.5 1.6 %collective-permute-start.5 = (s16[4,10,16,128]{3,2,1,0:T(8,128)(2,1)S(1)}, s16[4,10,16,128]{3,2,1,0:T(8,128)(2,1)S(1)}, u32[]{:S(2)}, u32[]{:S(2)}) collective-permute-start(s16[4,10,16,128]{3,2,1,0:T(8,128)(2,1)S(1)} %get-tuple-element.41), channel_id=1, source_target_pairs={{0,4},{1,5},{2,6},{3,7},{4,0},{5,1},{6,2},{7,3},{8,12},{9,13},{10,... | collective-permute-start | bytes 491528 | tf_op jit(solution)/shard_map/ppermute | solution.py:521
  18.1 4.5 %collective-permute-done.1.refs_1_ = s16[4,16,16,128]{3,2,1,0:T(8,128)(2,1)S(1)} collective-permute-done((s16[4,16,16,128]{3,2,1,0:T(8,128)(2,1)S(1)}, s16[4,16,16,128]{3,2,1,0:T(8,128)(2,1)S(1)}, u32[]{:S(2)}, u32[]{:S(2)}) %collective-permute-start.1) | collective-permute-done | bytes 262176 | tf_op jit(solution)/shard_map/ppermute | solution.py:521
  23.0 1.9 %collective-permute-start.2 = (s16[2,16,16,128]{3,2,1,0:T(8,128)(2,1)S(1)}, s16[2,16,16,128]{3,2,1,0:T(8,128)(2,1)S(1)}, u32[]{:S(2)}, u32[]{:S(2)}) collective-permute-start(s16[2,16,16,128]{3,2,1,0:T(8,128)(2,1)S(1)} %get-tuple-element.34), channel_id=1, source_target_pairs={{0,4},{1,5},{2,6},{3,7},{4,0},{5,1},{6,2},{7,3},{8,12},{9,13},{10,... | collective-permute-start | bytes 393224 | tf_op jit(solution)/shard_map/ppermute | solution.py:521
  25.2 1.6 %collective-permute-start.6 = (s16[2,10,16,128]{3,2,1,0:T(8,128)(2,1)S(1)}, s16[2,10,16,128]{3,2,1,0:T(8,128)(2,1)S(1)}, u32[]{:S(2)}, u32[]{:S(2)}) collective-permute-start(s16[2,10,16,128]{3,2,1,0:T(8,128)(2,1)S(1)} %get-tuple-element.43), channel_id=1, source_target_pairs={{0,2},{1,3},{2,0},{3,1},{4,6},{5,7},{6,4},{7,5},{8,10},{9,11},{10,... | collective-permute-start | bytes 245768 | tf_op jit(solution)/shard_map/ppermute | solution.py:521
  26.8 1.2 %collective-permute-done.2.refs_1_ = s16[2,16,16,128]{3,2,1,0:T(8,128)(2,1)S(1)} collective-permute-done((s16[2,16,16,128]{3,2,1,0:T(8,128)(2,1)S(1)}, s16[2,16,16,128]{3,2,1,0:T(8,128)(2,1)S(1)}, u32[]{:S(2)}, u32[]{:S(2)}) %collective-permute-start.2) | collective-permute-done | bytes 131104 | tf_op jit(solution)/shard_map/ppermute | solution.py:521
  28.3 2.9 %collective-permute-start.3 = (s16[1,16,16,128]{3,2,1,0:T(8,128)(2,1)S(1)}, s16[1,16,16,128]{3,2,1,0:T(8,128)(2,1)S(1)}, u32[]{:S(2)}, u32[]{:S(2)}) collective-permute-start(s16[1,16,16,128]{3,2,1,0:T(8,128)(2,1)S(1)} %get-tuple-element.36), channel_id=1, source_target_pairs={{0,8},{1,9},{2,10},{3,11},{4,12},{5,13},{6,14},{7,15},{8,0},{9,1},... | collective-permute-start | bytes 196616 | tf_op jit(solution)/shard_map/ppermute | solution.py:521
  31.6 1.1 %collective-permute-start.7 = (s16[1,10,16,128]{3,2,1,0:T(8,128)(2,1)S(1)}, s16[1,10,16,128]{3,2,1,0:T(8,128)(2,1)S(1)}, u32[]{:S(2)}, u32[]{:S(2)}) collective-permute-start(s16[1,10,16,128]{3,2,1,0:T(8,128)(2,1)S(1)} %get-tuple-element.45), channel_id=1, source_target_pairs={{0,8},{1,9},{2,10},{3,11},{4,12},{5,13},{6,14},{7,15},{8,0},{9,1},... | collective-permute-start | bytes 122888 | tf_op jit(solution)/shard_map/ppermute | solution.py:521
  32.7 3.8 %collective-permute-done.7.refs_3_ = s16[1,10,16,128]{3,2,1,0:T(8,128)(2,1)S(1)} collective-permute-done((s16[1,10,16,128]{3,2,1,0:T(8,128)(2,1)S(1)}, s16[1,10,16,128]{3,2,1,0:T(8,128)(2,1)S(1)}, u32[]{:S(2)}, u32[]{:S(2)}) %collective-permute-start.7) | collective-permute-done | bytes 40992 | tf_op jit(solution)/shard_map/ppermute | solution.py:521
  36.5 0.7 %residual.1 = (f32[48,1024]{1,0:T(8,128)S(1)}, s16[1,25,16,128]{3,2,1,0:T(8,128)(2,1)S(1)}, s16[10,16,128]{2,1,0:T(8,128)(2,1)S(1)}) custom-call(s32[1]{0:T(128)} %bitcast.me_ref, f32[18,2,1024]{2,1,0:T(2,128)S(1)} %bitcast.6, f32[1,48,640]{2,1,0:T(8,128)S(1)} %get-tuple-element.35.refs_0_, s16[1,16,16,128]{3,2,1,0:T(8,128)(2,1)S(1)} %collective-permute-done.3.refs_1_, ...), custom_call_target="tpu_custom_call" | custom-call | tf_op jit(solution)/shard_map/residual/pallas_call | solution.py:533
  37.9 2.9 %collective-permute-start.8 = (s16[25,16,128]{2,1,0:T(8,128)(2,1)S(1)}, s16[25,16,128]{2,1,0:T(8,128)(2,1)S(1)}, u32[]{:S(2)}, u32[]{:S(2)}) collective-permute-start(s16[25,16,128]{2,1,0:T(8,128)(2,1)S(1)} %bitcast.9), channel_id=1, source_target_pairs={{0,1},{1,0},{2,3},{3,2},{4,5},{5,4},{6,7},{7,6},{8,9},{9,8},{10,11... | collective-permute-start | bytes 307208 | tf_op jit(solution)/shard_map/ppermute | solution.py:521
  40.9 1.3 %collective-permute-start.10 = (s16[10,16,128]{2,1,0:T(8,128)(2,1)S(1)}, s16[10,16,128]{2,1,0:T(8,128)(2,1)S(1)}, u32[]{:S(2)}, u32[]{:S(2)}) collective-permute-start(s16[10,16,128]{2,1,0:T(8,128)(2,1)S(1)} %get-tuple-element.50), channel_id=1, source_target_pairs={{2,0},{3,1},{4,2},{5,3},{6,4},{7,5},{8,6},{9,7},{10,8},{11,9},{12,... | collective-permute-start | bytes 122888 | tf_op jit(solution)/shard_map/ppermute | solution.py:547
  42.2 1.8 %krylov.1 = (f32[18,2,1024]{2,1,0:T(2,128)S(1)}, f32[18,2,1024]{2,1,0:T(2,128)S(1)}, f32[18,2,1024]{2,1,0:T(2,128)S(1)}, f32[8,128]{1,0:T(8,128)S(1)}) custom-call(s32[1]{0:T(128)} %bitcast.me_ref, f32[48,1024]{1,0:T(8,128)S(1)} %get-tuple-element.46.own_ref, s16[25,16,128]{2,1,0:T(8,128)(2,1)S(1)} %collective-permute-done.8.mate_ref, ...), custom_call_target="tpu_custom_call" | custom-call | tf_op jit(solution)/shard_map/krylov/pallas_call | solution.py:548
  44.0 2.7 %collective-permute-done.10.far_ref = s16[10,16,128]{2,1,0:T(8,128)(2,1)S(1)} collective-permute-done((s16[10,16,128]{2,1,0:T(8,128)(2,1)S(1)}, s16[10,16,128]{2,1,0:T(8,128)(2,1)S(1)}, u32[]{:S(2)}, u32[]{:S(2)}) %collective-permute-start.10) | collective-permute-done | bytes 40992 | tf_op jit(solution)/shard_map/ppermute | solution.py:547
  47.0 1.0 %collective-permute-start.13 = (f32[8,128]{1,0:T(8,128)S(1)}, f32[8,128]{1,0:T(8,128)S(1)}, u32[]{:S(2)}, u32[]{:S(2)}) collective-permute-start(f32[8,128]{1,0:T(8,128)S(1)} %far.1), channel_id=1, source_target_pairs={{0,3},{1,2},{2,1},{3,0},{4,7},{5,6},{6,5},{7,4},{8,11},{9,10},{10,... | collective-permute-start | bytes 12296 | tf_op jit(solution)/shard_map/ppermute | solution.py:521
  48.0 1.6 %collective-permute-start.12 = (f32[8,128]{1,0:T(8,128)S(1)}, f32[8,128]{1,0:T(8,128)S(1)}, u32[]{:S(2)}, u32[]{:S(2)}) collective-permute-start(f32[8,128]{1,0:T(8,128)S(1)} %far.1), channel_id=1, source_target_pairs={{0,2},{1,3},{2,0},{3,1},{4,6},{5,7},{6,4},{7,5},{8,10},{9,11},{10,... | collective-permute-start | bytes 12296 | tf_op jit(solution)/shard_map/ppermute | solution.py:521
  50.1 1.5 %collective-permute-done.12 = f32[8,128]{1,0:T(8,128)S(1)} collective-permute-done((f32[8,128]{1,0:T(8,128)S(1)}, f32[8,128]{1,0:T(8,128)S(1)}, u32[]{:S(2)}, u32[]{:S(2)}) %collective-permute-start.12) | collective-permute-done | bytes 4128 | tf_op jit(solution)/shard_map/ppermute | solution.py:521
  51.6 1.6 %collective-permute-start.16 = (f32[8,128]{1,0:T(8,128)S(1)}, f32[8,128]{1,0:T(8,128)S(1)}, u32[]{:S(2)}, u32[]{:S(2)}) collective-permute-start(f32[8,128]{1,0:T(8,128)S(1)} %add_add_fusion.refs_0_), channel_id=1, source_target_pairs={{0,12},{1,13},{2,14},{3,15},{4,8},{5,9},{6,10},{7,11},{8,4},{9,5},... | collective-permute-start | bytes 12296 | tf_op jit(solution)/shard_map/ppermute | solution.py:521
  53.2 0.7 %collective-permute-start.15 = (f32[8,128]{1,0:T(8,128)S(1)}, f32[8,128]{1,0:T(8,128)S(1)}, u32[]{:S(2)}, u32[]{:S(2)}) collective-permute-start(f32[8,128]{1,0:T(8,128)S(1)} %add_add_fusion.refs_0_), channel_id=1, source_target_pairs={{0,8},{1,9},{2,10},{3,11},{4,12},{5,13},{6,14},{7,15},{8,0},{9,1},... | collective-permute-start | bytes 12296 | tf_op jit(solution)/shard_map/ppermute | solution.py:521
  53.9 2.2 %collective-permute-start.14 = (f32[8,128]{1,0:T(8,128)S(1)}, f32[8,128]{1,0:T(8,128)S(1)}, u32[]{:S(2)}, u32[]{:S(2)}) collective-permute-start(f32[8,128]{1,0:T(8,128)S(1)} %add_add_fusion.refs_0_), channel_id=1, source_target_pairs={{0,4},{1,5},{2,6},{3,7},{4,0},{5,1},{6,2},{7,3},{8,12},{9,13},{10,... | collective-permute-start | bytes 12296 | tf_op jit(solution)/shard_map/ppermute | solution.py:521
  56.1 1.0 %collective-permute-done.16.refs_3_ = f32[8,128]{1,0:T(8,128)S(1)} collective-permute-done((f32[8,128]{1,0:T(8,128)S(1)}, f32[8,128]{1,0:T(8,128)S(1)}, u32[]{:S(2)}, u32[]{:S(2)}) %collective-permute-start.16) | collective-permute-done | bytes 4128 | tf_op jit(solution)/shard_map/ppermute | solution.py:521
  57.7 0.9 %combine.1 = f32[18,2,1024]{2,1,0:T(2,128)} custom-call(f32[8,128]{1,0:T(8,128)S(1)} %add_add_fusion.refs_0_, f32[8,128]{1,0:T(8,128)S(1)} %collective-permute-done.14.refs_1_, f32[8,128]{1,0:T(8,128)S(1)} %collective-permute-done.15.refs_2_, f32[8,128]{1,0:T(8,128)S(1)} %collective-permute-done.16.refs_3_, f32[18,2,1024]{2,1,0:T(2,128)S(1)} %bitcast.7, ...), custom_call_target="tpu_custom_call" | custom-call | tf_op jit(solution)/shard_map/combine/pallas_call | solution.py:567
  (33 shorter events, 5.0 us)
Async XLA Ops:
  0.0 7.9 %copy-start = (f32[2,18,1024]{2,0,1:T(2,128)S(1)}, f32[2,18,1024]{2,0,1:T(2,128)}, u32[]{:S(2)}) copy-start(f32[2,18,1024]{2,0,1:T(2,128)} %param.13) | copy-start | bytes 442372
  0.0 7.9 %copy-start.2 = (f32[4,6]{1,0:T(4,128)S(1)}, f32[4,6]{1,0:T(4,128)}, u32[]{:S(2)}) copy-start(f32[4,6]{1,0:T(4,128)} %gain_ref.3) | copy-start | bytes 292
  0.0 7.9 %copy-start.3 = (s32[128]{0:T(128)S(1)}, s32[128]{0:T(128)}, u32[]{:S(2)}) copy-start(s32[128]{0:T(128)} %ids_ref.3) | copy-start | bytes 1540
  0.0 8.0 %copy-start.4 = (f32[4]{0:T(128)S(1)}, f32[4]{0:T(128)}, u32[]{:S(2)}) copy-start(f32[4]{0:T(128)} %weight_ref.3) | copy-start | bytes 52
  7.4 5.1 %copy-start.1 = (f32[8,48,640]{2,1,0:T(8,128)S(1)}, f32[8,48,640]{2,1,0:T(8,128)}, u32[]{:S(2)}) copy-start(f32[8,48,640]{2,1,0:T(8,128)} %get-tuple-element.29.refs_0_) | copy-start | bytes 2949124
  7.4 5.1 %collective-permute-start = (s16[8,16,16,128]{3,2,1,0:T(8,128)(2,1)}, s16[8,16,16,128]{3,2,1,0:T(8,128)(2,1)S(1)}, u32[]{:S(2)}, u32[]{:S(2)}) collective-permute-start(s16[8,16,16,128]{3,2,1,0:T(8,128)(2,1)} %get-tuple-element.30), channel_id=1, source_target_pairs={{0,1},{1,0},{2,3},{3,2},{4,5},{5,4},{6,7},{7,6},{8,9},{9,8},{10,11... | collective-permute-start | bytes 1572872 | tf_op jit(solution)/shard_map/ppermute | solution.py:521
  12.4 3.6 %collective-permute-start.4 = (s16[8,10,16,128]{3,2,1,0:T(8,128)(2,1)S(1)}, s16[8,10,16,128]{3,2,1,0:T(8,128)(2,1)S(1)}, u32[]{:S(2)}, u32[]{:S(2)}) collective-permute-start(s16[8,10,16,128]{3,2,1,0:T(8,128)(2,1)S(1)} %get-tuple-element.39), channel_id=1, source_target_pairs={{0,1},{1,0},{2,3},{3,2},{4,5},{5,4},{6,7},{7,6},{8,9},{9,8},{10,11... | collective-permute-start | bytes 983048 | tf_op jit(solution)/shard_map/ppermute | solution.py:521
  13.0 9.6 %collective-permute-start.1 = (s16[4,16,16,128]{3,2,1,0:T(8,128)(2,1)S(1)}, s16[4,16,16,128]{3,2,1,0:T(8,128)(2,1)S(1)}, u32[]{:S(2)}, u32[]{:S(2)}) collective-permute-start(s16[4,16,16,128]{3,2,1,0:T(8,128)(2,1)S(1)} %get-tuple-element.32), channel_id=1, source_target_pairs={{0,2},{1,3},{2,0},{3,1},{4,6},{5,7},{6,4},{7,5},{8,10},{9,11},{10,... | collective-permute-start | bytes 786440 | tf_op jit(solution)/shard_map/ppermute | solution.py:521
  16.5 8.4 %collective-permute-start.5 = (s16[4,10,16,128]{3,2,1,0:T(8,128)(2,1)S(1)}, s16[4,10,16,128]{3,2,1,0:T(8,128)(2,1)S(1)}, u32[]{:S(2)}, u32[]{:S(2)}) collective-permute-start(s16[4,10,16,128]{3,2,1,0:T(8,128)(2,1)S(1)} %get-tuple-element.41), channel_id=1, source_target_pairs={{0,4},{1,5},{2,6},{3,7},{4,0},{5,1},{6,2},{7,3},{8,12},{9,13},{10,... | collective-permute-start | bytes 491528 | tf_op jit(solution)/shard_map/ppermute | solution.py:521
  23.0 5.0 %collective-permute-start.2 = (s16[2,16,16,128]{3,2,1,0:T(8,128)(2,1)S(1)}, s16[2,16,16,128]{3,2,1,0:T(8,128)(2,1)S(1)}, u32[]{:S(2)}, u32[]{:S(2)}) collective-permute-start(s16[2,16,16,128]{3,2,1,0:T(8,128)(2,1)S(1)} %get-tuple-element.34), channel_id=1, source_target_pairs={{0,4},{1,5},{2,6},{3,7},{4,0},{5,1},{6,2},{7,3},{8,12},{9,13},{10,... | collective-permute-start | bytes 393224 | tf_op jit(solution)/shard_map/ppermute | solution.py:521
  25.2 6.0 %collective-permute-start.6 = (s16[2,10,16,128]{3,2,1,0:T(8,128)(2,1)S(1)}, s16[2,10,16,128]{3,2,1,0:T(8,128)(2,1)S(1)}, u32[]{:S(2)}, u32[]{:S(2)}) collective-permute-start(s16[2,10,16,128]{3,2,1,0:T(8,128)(2,1)S(1)} %get-tuple-element.43), channel_id=1, source_target_pairs={{0,2},{1,3},{2,0},{3,1},{4,6},{5,7},{6,4},{7,5},{8,10},{9,11},{10,... | collective-permute-start | bytes 245768 | tf_op jit(solution)/shard_map/ppermute | solution.py:521
  28.3 8.2 %collective-permute-start.3 = (s16[1,16,16,128]{3,2,1,0:T(8,128)(2,1)S(1)}, s16[1,16,16,128]{3,2,1,0:T(8,128)(2,1)S(1)}, u32[]{:S(2)}, u32[]{:S(2)}) collective-permute-start(s16[1,16,16,128]{3,2,1,0:T(8,128)(2,1)S(1)} %get-tuple-element.36), channel_id=1, source_target_pairs={{0,8},{1,9},{2,10},{3,11},{4,12},{5,13},{6,14},{7,15},{8,0},{9,1},... | collective-permute-start | bytes 196616 | tf_op jit(solution)/shard_map/ppermute | solution.py:521
  31.6 5.0 %collective-permute-start.7 = (s16[1,10,16,128]{3,2,1,0:T(8,128)(2,1)S(1)}, s16[1,10,16,128]{3,2,1,0:T(8,128)(2,1)S(1)}, u32[]{:S(2)}, u32[]{:S(2)}) collective-permute-start(s16[1,10,16,128]{3,2,1,0:T(8,128)(2,1)S(1)} %get-tuple-element.45), channel_id=1, source_target_pairs={{0,8},{1,9},{2,10},{3,11},{4,12},{5,13},{6,14},{7,15},{8,0},{9,1},... | collective-permute-start | bytes 122888 | tf_op jit(solution)/shard_map/ppermute | solution.py:521
  37.3 4.9 %collective-permute-start.9 = (s16[25,16,128]{2,1,0:T(8,128)(2,1)S(1)}, s16[25,16,128]{2,1,0:T(8,128)(2,1)S(1)}, u32[]{:S(2)}, u32[]{:S(2)}) collective-permute-start(s16[25,16,128]{2,1,0:T(8,128)(2,1)S(1)} %bitcast.8), channel_id=1, source_target_pairs={{1,2},{3,4},{5,6},{7,8},{9,10},{11,12},{13,14},{2,1},{4,3},{6,5},{... | collective-permute-start | bytes 307208 | tf_op jit(solution)/shard_map/ppermute | solution.py:546
  37.9 4.2 %collective-permute-start.8 = (s16[25,16,128]{2,1,0:T(8,128)(2,1)S(1)}, s16[25,16,128]{2,1,0:T(8,128)(2,1)S(1)}, u32[]{:S(2)}, u32[]{:S(2)}) collective-permute-start(s16[25,16,128]{2,1,0:T(8,128)(2,1)S(1)} %bitcast.9), channel_id=1, source_target_pairs={{0,1},{1,0},{2,3},{3,2},{4,5},{5,4},{6,7},{7,6},{8,9},{9,8},{10,11... | collective-permute-start | bytes 307208 | tf_op jit(solution)/shard_map/ppermute | solution.py:521
  40.9 5.9 %collective-permute-start.10 = (s16[10,16,128]{2,1,0:T(8,128)(2,1)S(1)}, s16[10,16,128]{2,1,0:T(8,128)(2,1)S(1)}, u32[]{:S(2)}, u32[]{:S(2)}) collective-permute-start(s16[10,16,128]{2,1,0:T(8,128)(2,1)S(1)} %get-tuple-element.50), channel_id=1, source_target_pairs={{2,0},{3,1},{4,2},{5,3},{6,4},{7,5},{8,6},{9,7},{10,8},{11,9},{12,... | collective-permute-start | bytes 122888 | tf_op jit(solution)/shard_map/ppermute | solution.py:547
  47.0 3.1 %collective-permute-start.13 = (f32[8,128]{1,0:T(8,128)S(1)}, f32[8,128]{1,0:T(8,128)S(1)}, u32[]{:S(2)}, u32[]{:S(2)}) collective-permute-start(f32[8,128]{1,0:T(8,128)S(1)} %far.1), channel_id=1, source_target_pairs={{0,3},{1,2},{2,1},{3,0},{4,7},{5,6},{6,5},{7,4},{8,11},{9,10},{10,... | collective-permute-start | bytes 12296 | tf_op jit(solution)/shard_map/ppermute | solution.py:521
  48.0 3.6 %collective-permute-start.12 = (f32[8,128]{1,0:T(8,128)S(1)}, f32[8,128]{1,0:T(8,128)S(1)}, u32[]{:S(2)}, u32[]{:S(2)}) collective-permute-start(f32[8,128]{1,0:T(8,128)S(1)} %far.1), channel_id=1, source_target_pairs={{0,2},{1,3},{2,0},{3,1},{4,6},{5,7},{6,4},{7,5},{8,10},{9,11},{10,... | collective-permute-start | bytes 12296 | tf_op jit(solution)/shard_map/ppermute | solution.py:521
  49.6 2.0 %collective-permute-start.11 = (f32[8,128]{1,0:T(8,128)S(1)}, f32[8,128]{1,0:T(8,128)S(1)}, u32[]{:S(2)}, u32[]{:S(2)}) collective-permute-start(f32[8,128]{1,0:T(8,128)S(1)} %far.1), channel_id=1, source_target_pairs={{0,1},{1,0},{2,3},{3,2},{4,5},{5,4},{6,7},{7,6},{8,9},{9,8},{10,11... | collective-permute-start | bytes 12296 | tf_op jit(solution)/shard_map/ppermute | solution.py:521
  51.6 5.5 %collective-permute-start.16 = (f32[8,128]{1,0:T(8,128)S(1)}, f32[8,128]{1,0:T(8,128)S(1)}, u32[]{:S(2)}, u32[]{:S(2)}) collective-permute-start(f32[8,128]{1,0:T(8,128)S(1)} %add_add_fusion.refs_0_), channel_id=1, source_target_pairs={{0,12},{1,13},{2,14},{3,15},{4,8},{5,9},{6,10},{7,11},{8,4},{9,5},... | collective-permute-start | bytes 12296 | tf_op jit(solution)/shard_map/ppermute | solution.py:521
  53.2 4.5 %collective-permute-start.15 = (f32[8,128]{1,0:T(8,128)S(1)}, f32[8,128]{1,0:T(8,128)S(1)}, u32[]{:S(2)}, u32[]{:S(2)}) collective-permute-start(f32[8,128]{1,0:T(8,128)S(1)} %add_add_fusion.refs_0_), channel_id=1, source_target_pairs={{0,8},{1,9},{2,10},{3,11},{4,12},{5,13},{6,14},{7,15},{8,0},{9,1},... | collective-permute-start | bytes 12296 | tf_op jit(solution)/shard_map/ppermute | solution.py:521
  53.9 3.8 %collective-permute-start.14 = (f32[8,128]{1,0:T(8,128)S(1)}, f32[8,128]{1,0:T(8,128)S(1)}, u32[]{:S(2)}, u32[]{:S(2)}) collective-permute-start(f32[8,128]{1,0:T(8,128)S(1)} %add_add_fusion.refs_0_), channel_id=1, source_target_pairs={{0,4},{1,5},{2,6},{3,7},{4,0},{5,1},{6,2},{7,3},{8,12},{9,13},{10,... | collective-permute-start | bytes 12296 | tf_op jit(solution)/shard_map/ppermute | solution.py:521
